TPU v7x, 32 devices: a whole 2x2x4 slice. The times are simulated.
32 devices in a mesh: seq: 8 (over z, x), ch: 4 (over y, core).
Axes of the slice: x: 2, y: 2, z: 4, core: 2. Of those that a mesh axis runs over, the one named last changes fastest.
Arguments:
- activations: bfloat16 [16384, 4096], P('seq', 'ch'), may hold values from -16 to 16
- gate_input: bfloat16 [16384, 4096], P('seq', 'ch'), may hold values from -6 to 6
- bmat: bfloat16 [16384, 128], P('seq'), may hold values from -0.29882812 to 0.29882812
- cmat: bfloat16 [16384, 128], P('seq'), may hold values from -0.29882812 to 0.29882812
- log_fwd: float32 [64, 16384], P('ch', 'seq'), may hold values from -0.6 to 0
- log_rev: float32 [64, 16384], P('ch', 'seq'), may hold values from -0.6 to 0
- skip: float32 [64], P('ch'), may hold values from 0.5 to 2
- gain: float32 [4096], P('ch'), may hold values from 0.1 to 1.9
Outputs:
- normed: bfloat16 [16384, 4096], P('seq', 'ch')
All inputs are finite; a program needn't handle non-finite values.
Results may differ from a plain program's by a relative error of at most 0.0013.
Values sent between devices are 32-bit elements; how exact they have to be, the bound alone decides.
No kernel may reach another device: no remote copies, remote signals or barrier semaphores. Data moves between devices by JAX's collectives and lax.ppermute only.
A program may use at most 256 MiB of HBM per device.

v0:
```python
import jax
import jax.numpy as jnp
from jax import lax
from jax.sharding import PartitionSpec as P

INNER = 4096
BLOCK = 512


def carried_in(value, axis, join, neutral, backward):
    count, mine = (lax.axis_size(axis), lax.axis_index(axis))
    pieces = jax.tree.map(lambda part: lax.all_gather(part, axis), value)
    if backward:
        pieces = jax.tree.map(lambda part: part[::-1], pieces)
        mine = count - 1 - mine
    total = jax.tree.map(
        lambda part, zero: jnp.full_like(part, 0) + jnp.asarray(zero, part.dtype), value, neutral
    )

    def hop(position, total):
        longer = join(total, jax.tree.map(lambda part: part[position], pieces))
        return jax.tree.map(lambda new, old: jnp.where(position < mine, new, old), longer, total)

    return lax.fori_loop(0, count - 1, hop, total)


def local_pass(x_heads, b_rows, c_rows, log_rows):
    row_count, heads, headdim = x_heads.shape
    blocks = row_count // BLOCK
    x_blocks = x_heads.reshape(blocks, BLOCK, heads, headdim)
    b_blocks = b_rows.reshape(blocks, BLOCK, b_rows.shape[1])
    c_blocks = c_rows.reshape(blocks, BLOCK, c_rows.shape[1])
    log_blocks = log_rows.reshape(heads, blocks, BLOCK).transpose(1, 0, 2)
    lower_mask = (jnp.arange(BLOCK)[:, None] >= jnp.arange(BLOCK)[None, :])[None]

    def advance(carry, block):
        carry_state, offset = carry
        x_block, b_block, c_block, log_block = block
        cumulative = jnp.cumsum(log_block, axis=1)
        scores = jnp.einsum("in,jn->ij", c_block, b_block, preferred_element_type=jnp.float32)
        spread = cumulative[:, :, None] - cumulative[:, None, :]
        decay_matrix = jnp.where(lower_mask, jnp.exp(jnp.where(lower_mask, spread, 0.0)), 0.0)
        weights = (decay_matrix * scores[None]).astype(jnp.bfloat16)
        within = jnp.einsum("hij,jhp->ihp", weights, x_block, preferred_element_type=jnp.float32)
        to_end = jnp.exp(cumulative[:, -1:] - cumulative)
        b_scaled = (to_end[:, :, None] * b_block.astype(jnp.float32)[None]).astype(jnp.bfloat16)
        fresh_term = jnp.einsum(
            "jhp,hjn->hpn", x_block, b_scaled, preferred_element_type=jnp.float32
        )
        next_state = jnp.exp(cumulative[:, -1])[:, None, None] * carry_state + fresh_term
        return ((next_state, offset + cumulative[:, -1]), (within, carry_state, offset, cumulative))

    start = (
        jnp.zeros((heads, headdim, b_rows.shape[1]), jnp.float32),
        jnp.zeros((heads,), jnp.float32),
    )
    final, outputs = lax.scan(advance, start, (x_blocks, b_blocks, c_blocks, log_blocks))
    return (outputs, final[0], final[1])


def finish(outputs, c_rows, incoming):
    within, before, offsets, cumulatives = outputs
    blocks, length, heads, headdim = within.shape
    full_states = before + jnp.exp(offsets)[:, :, None, None] * incoming[None]
    c_blocks = c_rows.reshape(blocks, length, c_rows.shape[1]).astype(jnp.float32)
    c_scaled = jnp.exp(cumulatives)[:, :, :, None] * c_blocks[:, None]
    carried = jnp.einsum("khin,khpn->kihp", c_scaled, full_states, precision=lax.Precision.HIGHEST)
    return (within + carried).reshape(blocks * length, heads, headdim)


def link_states(earlier, later):
    return (earlier[0] * later[0], later[0][:, None, None] * earlier[1] + later[1])


def shards(activations, gate_input, bmat, cmat, log_fwd, log_rev, skip, gain):
    row_count = activations.shape[0]
    heads = log_fwd.shape[0]
    channels = activations.shape[1]
    headdim = channels // heads
    x_heads = activations.reshape(row_count, heads, headdim)
    b_flip = bmat[::-1]
    c_flip = cmat[::-1]
    fwd_parts, fwd_final, fwd_total = local_pass(x_heads, bmat, cmat, log_fwd)
    rev_parts, rev_final, rev_total = local_pass(x_heads[::-1], b_flip, c_flip, log_rev[:, ::-1])
    identity = (jnp.ones((heads,), jnp.float32), jnp.zeros(fwd_final.shape, jnp.float32))
    fwd_in = carried_in((jnp.exp(fwd_total), fwd_final), "seq", link_states, identity, False)[1]
    rev_in = carried_in((jnp.exp(rev_total), rev_final), "seq", link_states, identity, True)[1]
    forward = finish(fwd_parts, cmat, fwd_in)
    backward = finish(rev_parts, c_flip, rev_in)[::-1]
    combined = forward + backward + skip[None, :, None] * x_heads.astype(jnp.float32)
    gated = combined.reshape(row_count, channels) * jax.nn.silu(gate_input.astype(jnp.float32))
    squares = lax.psum(jnp.sum(gated * gated, axis=1), "ch")
    mean_square = squares / INNER
    return (gated * lax.rsqrt(mean_square + 1e-05)[:, None] * gain[None, :]).astype(jnp.bfloat16)


def solution(mesh):
    return jax.shard_map(
        shards,
        mesh=mesh,
        in_specs=(
            P("seq", "ch"),
            P("seq", "ch"),
            P("seq", None),
            P("seq", None),
            P("ch", "seq"),
            P("ch", "seq"),
            P("ch"),
            P("ch"),
        ),
        out_specs=P("seq", "ch"),
        check_vma=False,
    )
```

profile of v0, /device:TPU:0, one launch (start us, length us, event | category | flops | bytes accessed | tf_op | source)
XLA Modules:
  0.0 339.7 jit_solution(11352247505061130461)
XLA Ops:
  6.5 6.5 %copy.57 = bf16[2048,1024]{0,1:T(8,128)(2,1)} copy(bf16[2048,1024]{1,0:T(8,128)(2,1)} %param.16) | data formatting | bytes 8388608 | tf_op args[0]
  13.0 11.0 %rev.22 = bf16[2048,16,64]{0,2,1:T(8,128)(2,1)} reverse(bf16[2048,16,64]{0,2,1:T(8,128)(2,1)} %bitcast.172), dimensions={0} | reverse | bytes 8388608 | tf_op jit(solution)/shard_map/rev | solution.py:84
  24.0 4.8 %copy.79 = bf16[16,8,4,8,512]{4,3,1,0,2:T(8,128)(2,1)} copy(bf16[16,8,4,8,512]{4,3,2,1,0:T(8,128)(2,1)} %bitcast.176) | data formatting | bytes 8388608 | tf_op jit(solution)/shard_map/reshape | solution.py:30
  29.8 1.2 rev.21
  31.1 4.3 %broadcast.83.clone.1 = f32[4,512,16,64]{1,3,2,0:T(8,128)} broadcast(f32[]{:T(128)} %constant.104.clone.1), dimensions={} | broadcast | bytes 8388612 | tf_op jit(solution)/shard_map/broadcast.11
  35.4 1.6 broadcast.84.clone.1
  37.0 52.3 %while.75 = (s32[]{:T(128)}, f32[16,64,128]{2,1,0:T(8,128)S(1)}, f32[16]{0:T(128)S(1)}, f32[4,512,16,64]{1,3,2,0:T(8,128)}, f32[4,16,64,128]{3,2,1,0:T(8,128)}, ...) while((s32[]{:T(128)}, f32[16,64,128]{2,1,0:T(8,128)S(1)}, ...), condition=%wide.region_9.10_spmd.clone.clone, body=%wide.region_6.9_spmd.clone.clone.sunk | while | flops 763191552 | bytes 10524841 | solution.py:57
  37.1 1.2 reduce-window.34
  38.9 7.2 %bitcast_dynamic-update-slice_fusion.10 = f32[4,512,16,64]{1,3,2,0:T(8,128)} fusion(f32[4,512,16,64]{1,3,2,0:T(8,128)} %get-tuple-element.920, s32[]{:T(128)} %get-tuple-element.917, f32[512,512]{1,0:T(8,128)S(1)} %fusion.124, f32[16,512]{1,0:T(8,128)S(1)} %copy_bitcast_fusion.6, pred[512,512]{1,0:T(8,128)(4,1)S(1)} %fusion.125, ...), kind=kOutput, calls=%fused_computation.49.clone.1 | convolution fusion | flops 557842432 | bytes 4523008 | tf_op jit(solution)/shard_map/while/body/eval_jaxpr/hij,jhp->ihp/dot_general | solution.py:44
  47.3 2.7 fusion.123
  50.2 1.2 reduce-window.34
  52.0 7.1 %bitcast_dynamic-update-slice_fusion.10 = f32[4,512,16,64]{1,3,2,0:T(8,128)} fusion(f32[4,512,16,64]{1,3,2,0:T(8,128)} %get-tuple-element.920, s32[]{:T(128)} %get-tuple-element.917, f32[512,512]{1,0:T(8,128)S(1)} %fusion.124, f32[16,512]{1,0:T(8,128)S(1)} %copy_bitcast_fusion.6, pred[512,512]{1,0:T(8,128)(4,1)S(1)} %fusion.125, ...), kind=kOutput, calls=%fused_computation.49.clone.1 | convolution fusion | flops 557842432 | bytes 4523008 | tf_op jit(solution)/shard_map/while/body/eval_jaxpr/hij,jhp->ihp/dot_general | solution.py:44
  60.3 2.7 fusion.123
  63.2 1.2 reduce-window.34
  65.1 7.2 %bitcast_dynamic-update-slice_fusion.10 = f32[4,512,16,64]{1,3,2,0:T(8,128)} fusion(f32[4,512,16,64]{1,3,2,0:T(8,128)} %get-tuple-element.920, s32[]{:T(128)} %get-tuple-element.917, f32[512,512]{1,0:T(8,128)S(1)} %fusion.124, f32[16,512]{1,0:T(8,128)S(1)} %copy_bitcast_fusion.6, pred[512,512]{1,0:T(8,128)(4,1)S(1)} %fusion.125, ...), kind=kOutput, calls=%fused_computation.49.clone.1 | convolution fusion | flops 557842432 | bytes 4523008 | tf_op jit(solution)/shard_map/while/body/eval_jaxpr/hij,jhp->ihp/dot_general | solution.py:44
  73.4 2.7 fusion.123
  76.3 1.2 reduce-window.34
  78.2 7.1 %bitcast_dynamic-update-slice_fusion.10 = f32[4,512,16,64]{1,3,2,0:T(8,128)} fusion(f32[4,512,16,64]{1,3,2,0:T(8,128)} %get-tuple-element.920, s32[]{:T(128)} %get-tuple-element.917, f32[512,512]{1,0:T(8,128)S(1)} %fusion.124, f32[16,512]{1,0:T(8,128)S(1)} %copy_bitcast_fusion.6, pred[512,512]{1,0:T(8,128)(4,1)S(1)} %fusion.125, ...), kind=kOutput, calls=%fused_computation.49.clone.1 | convolution fusion | flops 557842432 | bytes 4523008 | tf_op jit(solution)/shard_map/while/body/eval_jaxpr/hij,jhp->ihp/dot_general | solution.py:44
  86.5 2.7 fusion.123
  90.2 11.7 %reshape.277 = bf16[4,512,16,64]{3,2,1,0:T(8,128)(2,1)} reshape(bf16[2048,1024]{1,0:T(8,128)(2,1)} %param.16) | data formatting | bytes 8388608 | tf_op jit(solution)/shard_map/reshape;reshape | solution.py:30
  101.9 9.8 %copy.55 = bf16[4,512,16,64]{1,3,2,0:T(8,128)(2,1)} copy(bf16[4,512,16,64]{3,2,1,0:T(8,128)(2,1)} %reshape.277) | data formatting | bytes 8388608
  111.8 4.3 %broadcast.83.clone = f32[4,512,16,64]{1,3,2,0:T(8,128)} broadcast(f32[]{:T(128)} %constant.104.clone.1), dimensions={} | broadcast | bytes 8388612 | tf_op jit(solution)/shard_map/broadcast.11
  116.0 1.6 broadcast.84.clone
  117.6 52.1 %while.74 = (s32[]{:T(128)}, f32[16,64,128]{2,1,0:T(8,128)S(1)}, f32[16]{0:T(128)S(1)}, f32[4,512,16,64]{1,3,2,0:T(8,128)}, f32[4,16,64,128]{3,2,1,0:T(8,128)}, ...) while((s32[]{:T(128)}, f32[16,64,128]{2,1,0:T(8,128)S(1)}, ...), condition=%wide.region_3.4_spmd.clone.clone, body=%wide.region_0.3_spmd.clone.clone.sunk | while | flops 763191552 | bytes 10524841 | solution.py:57
  117.7 1.2 reduce-window.32
  119.5 7.1 %bitcast_dynamic-update-slice_fusion.8 = f32[4,512,16,64]{1,3,2,0:T(8,128)} fusion(f32[4,512,16,64]{1,3,2,0:T(8,128)} %get-tuple-element.878, s32[]{:T(128)} %get-tuple-element.875, f32[512,512]{1,0:T(8,128)S(1)} %fusion.114, f32[16,512]{1,0:T(8,128)S(1)} %copy_bitcast_fusion.5, pred[512,512]{1,0:T(8,128)(4,1)S(1)} %fusion.115, ...), kind=kOutput, calls=%fused_computation.13.clone.1 | convolution fusion | flops 557842432 | bytes 4523008 | tf_op jit(solution)/shard_map/while/body/eval_jaxpr/hij,jhp->ihp/dot_general | solution.py:44
  127.8 2.7 fusion.113
  132.6 7.1 %bitcast_dynamic-update-slice_fusion.8 = f32[4,512,16,64]{1,3,2,0:T(8,128)} fusion(f32[4,512,16,64]{1,3,2,0:T(8,128)} %get-tuple-element.878, s32[]{:T(128)} %get-tuple-element.875, f32[512,512]{1,0:T(8,128)S(1)} %fusion.114, f32[16,512]{1,0:T(8,128)S(1)} %copy_bitcast_fusion.5, pred[512,512]{1,0:T(8,128)(4,1)S(1)} %fusion.115, ...), kind=kOutput, calls=%fused_computation.13.clone.1 | convolution fusion | flops 557842432 | bytes 4523008 | tf_op jit(solution)/shard_map/while/body/eval_jaxpr/hij,jhp->ihp/dot_general | solution.py:44
  140.8 2.7 fusion.113
  143.8 1.2 reduce-window.32
  145.6 7.1 %bitcast_dynamic-update-slice_fusion.8 = f32[4,512,16,64]{1,3,2,0:T(8,128)} fusion(f32[4,512,16,64]{1,3,2,0:T(8,128)} %get-tuple-element.878, s32[]{:T(128)} %get-tuple-element.875, f32[512,512]{1,0:T(8,128)S(1)} %fusion.114, f32[16,512]{1,0:T(8,128)S(1)} %copy_bitcast_fusion.5, pred[512,512]{1,0:T(8,128)(4,1)S(1)} %fusion.115, ...), kind=kOutput, calls=%fused_computation.13.clone.1 | convolution fusion | flops 557842432 | bytes 4523008 | tf_op jit(solution)/shard_map/while/body/eval_jaxpr/hij,jhp->ihp/dot_general | solution.py:44
  153.9 2.7 fusion.113
  156.8 1.2 reduce-window.32
  158.6 7.1 %bitcast_dynamic-update-slice_fusion.8 = f32[4,512,16,64]{1,3,2,0:T(8,128)} fusion(f32[4,512,16,64]{1,3,2,0:T(8,128)} %get-tuple-element.878, s32[]{:T(128)} %get-tuple-element.875, f32[512,512]{1,0:T(8,128)S(1)} %fusion.114, f32[16,512]{1,0:T(8,128)S(1)} %copy_bitcast_fusion.5, pred[512,512]{1,0:T(8,128)(4,1)S(1)} %fusion.115, ...), kind=kOutput, calls=%fused_computation.13.clone.1 | convolution fusion | flops 557842432 | bytes 4523008 | tf_op jit(solution)/shard_map/while/body/eval_jaxpr/hij,jhp->ihp/dot_general | solution.py:44
  166.9 2.7 fusion.113
  174.2 23.5 %all-reduce.2 = (f32[128]{0:T(128)S(1)}, f32[128]{0:T(128)S(1)}) all-reduce(f32[128]{0:T(128)S(1)} %exponential_dynamic-update-slice_fusion.1, f32[128]{0:T(128)S(1)} %exponential_dynamic-update-slice_fusion), channel_id=2, replica_groups=mesh['seq'=8,'ch'=4] {'seq'}, use_global_device_ids=true, to_apply=%add | all-reduce | flops 256 | bytes 2048
  198.1 6.4 %copy.61 = bf16[2048,1024]{0,1:T(8,128)(2,1)} copy(bf16[2048,1024]{1,0:T(8,128)(2,1)} %param.17) | data formatting | bytes 8388608 | tf_op args[1]
  204.5 4.9 %rev.26 = f32[8,16,64,128]{3,2,1,0:T(8,128)} reverse(f32[8,16,64,128]{3,2,1,0:T(8,128)} %bitcast.181), dimensions={0} | reverse | bytes 8388608 | tf_op jit(solution)/shard_map/rev | solution.py:14
  209.4 8.5 %while.73 = (s32[]{:T(128)}, f32[16,64,128]{2,1,0:T(8,128)S(1)}, s32[]{:T(128)}, f32[8,16]{1,0:T(8,128)S(1)}, f32[8,16,64,128]{3,2,1,0:T(8,128)}, /*index=5*/s32[]{:T(128)}, s32[]{:T(128)}) while((s32[]{:T(128)}, f32[16,64,128]{2,1,0:T(8,128)S(1)}, s32[]{:T(128)}, f32[8,16]{1,0:T(8,128)S(1)}, f32[8,16,64,128]{3,2,1,0:T(8,128)}, ...), condition=%wide.region_11.12_spmd.clone, body=%wide.region_10.11_spmd.clone.sunk | while | flops 524292 | bytes 1573161 | solution.py:24
  209.4 1.2 fusion.105
  210.6 1.2 fusion.105
  211.8 1.2 fusion.105
  213.0 1.2 fusion.105
  214.2 1.2 fusion.105
  215.5 1.2 fusion.105
  216.7 1.2 fusion.105
  217.9 22.6 %fusion.58 = f32[4,16,8,8,512]{4,3,2,1,0:T(8,128)S(1)} fusion(f32[4,512,16,64]{1,3,2,0:T(8,128)} %get-tuple-element.340, f32[4,512,128]{2,1,0:T(8,128)} %convert_element_type.40, f32[4,16,512]{2,1,0:T(8,128)S(1)} %exp.61, f32[4,16,64,128]{3,2,1,0:T(8,128)S(1)} %copy-done.2, f32[16,64,128]{2,1,0:T(8,128)S(1)} %get-tuple-element.345, f32[4,16]{1,0:T(4,128)S(1)} %exp.59), kind=kOutput, calls=%fused_computation.91 | convolution fusion | flops 3228565504 | bytes 20578560 | tf_op jit(solution)/shard_map/khin,khpn->kihp/dot_general | solution.py:67
  240.5 4.2 %copy.71 = f32[4,16,8,8,512]{4,3,0,2,1:T(8,128)} copy(f32[4,16,8,8,512]{4,3,2,1,0:T(8,128)S(1)} %fusion.58) | data formatting | bytes 16777216 | tf_op jit(solution)/shard_map/reshape | solution.py:68
  244.8 13.4 %rev.27 = f32[2048,16,64]{0,2,1:T(8,128)} reverse(f32[2048,16,64]{0,2,1:T(8,128)} %bitcast.174), dimensions={0} | reverse | bytes 16777216 | tf_op jit(solution)/shard_map/rev | solution.py:89
  258.1 8.5 %while.72 = (s32[]{:T(128)}, f32[16,64,128]{2,1,0:T(8,128)S(1)}, s32[]{:T(128)}, f32[8,16]{1,0:T(8,128)S(1)}, f32[8,16,64,128]{3,2,1,0:T(8,128)}, /*index=5*/s32[]{:T(128)}, s32[]{:T(128)}) while((s32[]{:T(128)}, f32[16,64,128]{2,1,0:T(8,128)S(1)}, s32[]{:T(128)}, f32[8,16]{1,0:T(8,128)S(1)}, f32[8,16,64,128]{3,2,1,0:T(8,128)}, ...), condition=%wide.region_5.6_spmd.clone, body=%wide.region_4.5_spmd.clone.sunk | while | flops 524292 | bytes 1573161 | solution.py:24
  258.2 1.2 fusion.104
  259.4 1.2 fusion.104
  260.6 1.2 fusion.104
  261.8 1.2 fusion.104
  263.0 1.2 fusion.104
  264.2 1.2 fusion.104
  265.4 1.2 fusion.104
  266.6 22.6 %fusion.59 = f32[4,16,8,8,512]{4,3,2,1,0:T(8,128)S(1)} fusion(f32[4,512,16,64]{1,3,2,0:T(8,128)} %get-tuple-element.333, f32[4,512,128]{2,1,0:T(8,128)} %convert_element_type.39, f32[4,16,512]{2,1,0:T(8,128)S(1)} %exp.58, f32[4,16,64,128]{3,2,1,0:T(8,128)S(1)} %copy-done.3, f32[16,64,128]{2,1,0:T(8,128)S(1)} %get-tuple-element.338, f32[4,16]{1,0:T(4,128)S(1)} %exp.56), kind=kOutput, calls=%fused_computation.93 | convolution fusion | flops 3228565504 | bytes 20578560 | tf_op jit(solution)/shard_map/khin,khpn->kihp/dot_general | solution.py:67
  289.3 4.2 %copy.70 = f32[4,16,8,8,512]{4,3,0,2,1:T(8,128)} copy(f32[4,16,8,8,512]{4,3,2,1,0:T(8,128)S(1)} %fusion.59) | data formatting | bytes 16777216 | tf_op jit(solution)/shard_map/reshape | solution.py:68
  293.5 13.4 %multiply_add_fusion = f32[2048,16,64]{0,2,1:T(8,128)} fusion(bf16[2048,16,64]{0,2,1:T(8,128)(2,1)} %bitcast.173, f32[2048,16,64]{0,2,1:T(8,128)} %bitcast.175, f32[2048,16,64]{0,2,1:T(8,128)} %rev.27, f32[16]{0:T(128)S(1)} %copy-done.9), kind=kLoop, calls=%fused_computation.96 | loop fusion | flops 8388608 | bytes 29360192 | tf_op jit(solution)/shard_map/add | solution.py:90
  307.0 6.0 %multiply_reduce_fusion = f32[2048]{0:T(1024)S(1)} fusion(bf16[2048,1024]{0,1:T(8,128)(2,1)} %copy.61, f32[2048,16,64]{0,2,1:T(8,128)} %multiply_add_fusion), kind=kLoop, calls=%fused_computation.95 | loop fusion | flops 16775168 | bytes 12591104 | tf_op jit(solution)/shard_map/reduce_sum | solution.py:92
  313.0 5.8 %psum.7 = f32[2048]{0:T(1024)S(1)} all-reduce(f32[2048]{0:T(1024)S(1)} %multiply_reduce_fusion), channel_id=1, replica_groups=mesh['seq'=8,'ch'=4] {'ch'}, use_global_device_ids=true, to_apply=%region_13.14 | all-reduce | flops 2048 | bytes 16384 | tf_op jit(solution)/shard_map/psum | solution.py:92
  318.8 7.7 %multiply_convert_fusion.16 = bf16[2048,1024]{0,1:T(8,128)(2,1)} fusion(f32[1024]{0:T(1024)S(1)} %copy-done.8, f32[2048]{0:T(1024)S(1)} %add_rsqrt_fusion, bf16[2048,1024]{0,1:T(8,128)(2,1)} %copy.61, f32[2048,16,64]{0,2,1:T(8,128)} %multiply_add_fusion), kind=kLoop, calls=%fused_computation.94 | loop fusion | flops 18874368 | bytes 16789504 | tf_op jit(solution)/shard_map/convert_element_type | solution.py:94
  326.5 6.4 %copy.62 = bf16[2048,1024]{1,0:T(8,128)(2,1)} copy(bf16[2048,1024]{0,1:T(8,128)(2,1)} %multiply_convert_fusion.16) | data formatting | bytes 8388608 | tf_op jit(solution)/shard_map/convert_element_type | solution.py:94
  (216 shorter events, 23.4 us)
Async XLA Ops:
  6.5 198.0 %all-gather.9.cloned.1.call-start = ((), (), s32[]{:S(2)}) async-start(), calls=%async_computation.1 | async-start | bytes 4718592 | tf_op jit(solution)/shard_map/all_gather | solution.py:12
  13.0 15.8 %copy-start.5 = (bf16[2048,128]{1,0:T(8,128)(2,1)S(1)}, bf16[2048,128]{1,0:T(8,128)(2,1)}, u32[]{:S(2)}) copy-start(bf16[2048,128]{1,0:T(8,128)(2,1)} %param.19) | copy-start | bytes 1572868
  13.0 16.3 %copy-start.4 = (bf16[2048,128]{1,0:T(8,128)(2,1)S(1)}, bf16[2048,128]{1,0:T(8,128)(2,1)}, u32[]{:S(2)}) copy-start(bf16[2048,128]{1,0:T(8,128)(2,1)} %param.18) | copy-start | bytes 1572868
  13.0 16.8 %copy-start.6 = (f32[16,2048]{1,0:T(8,128)S(1)}, f32[16,2048]{1,0:T(8,128)}, u32[]{:S(2)}) copy-start(f32[16,2048]{1,0:T(8,128)} %param.21) | copy-start | bytes 393220
  89.3 0.8 copy-start
  90.1 168.0 %all-gather.7.cloned.1.call-start = ((), (), s32[]{:S(2)}) async-start(), calls=%async_computation | async-start | bytes 4718592 | tf_op jit(solution)/shard_map/all_gather | solution.py:12
  101.9 9.8 %copy-start.7 = (f32[16,2048]{1,0:T(8,128)S(1)}, f32[16,2048]{1,0:T(8,128)}, u32[]{:S(2)}) copy-start(f32[16,2048]{1,0:T(8,128)} %param.20) | copy-start | bytes 393220
  117.6 55.0 %copy-start.10 = (u32[32]{0:T(128)S(1)}, u32[32]{0:T(128)}, u32[]{:S(2)}) copy-start(u32[32]{0:T(128)} %constant.113) | copy-start | bytes 388
  169.7 0.8 copy-start.1
  204.5 13.4 %copy-start.2 = (f32[4,16,64,128]{3,2,1,0:T(8,128)S(1)}, f32[4,16,64,128]{3,2,1,0:T(8,128)}, u32[]{:S(2)}) copy-start(f32[4,16,64,128]{3,2,1,0:T(8,128)} %get-tuple-element.341) | copy-start | bytes 6291460
  244.8 21.8 %copy-start.3 = (f32[4,16,64,128]{3,2,1,0:T(8,128)S(1)}, f32[4,16,64,128]{3,2,1,0:T(8,128)}, u32[]{:S(2)}) copy-start(f32[4,16,64,128]{3,2,1,0:T(8,128)} %get-tuple-element.334) | copy-start | bytes 6291460
  289.3 4.3 %copy-start.9 = (f32[16]{0:T(128)S(1)}, f32[16]{0:T(128)}, u32[]{:S(2)}) copy-start(f32[16]{0:T(128)} %param.22) | copy-start | bytes 196
  307.0 11.8 %copy-start.8 = (f32[1024]{0:T(1024)S(1)}, f32[1024]{0:T(1024)}, u32[]{:S(2)}) copy-start(f32[1024]{0:T(1024)} %param.23) | copy-start | bytes 12292
Sparse Core Ops, SparseCore 0:
  90.3 76.0 all-gather.8
  170.7 76.3 all-gather.6
where the time goes:
time: 342 us; the launch traced here: 340 us
  matrix products  126 us (37%)
  local copies, waits for them, and re-layouts  104 us (30%)
  other arithmetic  64.7 us (19%)
  blocking collectives  29.3 us (9%)
  between operations  14.3 us (4%)
    dot_general x8, matrix products, advance(): jnp.einsum('hij,jhp->ihp', weights, x_block, preferred_element_type=jnp.f...  57.1 us
    dot_general x2, matrix products, finish(): jnp.einsum('khin,khpn->kihp', c_scaled, full_states, precision=lax.Precis...  45.3 us
    unnamed x30, local copies, waits for them, and re-layouts  25.2 us
    unnamed x1, blocking collectives  23.5 us
    dot_general x8, matrix products, advance(): jnp.einsum('jhp,hjn->hpn', x_block, b_scaled, preferred_element_type=jnp....  21.3 us
    select_n x14, other arithmetic, hop(): jnp.where(position < mine, new, old)  16.4 us
    add x1, other arithmetic, shards(): forward + backward + skip[None, :, None] * x_heads.astype(jnp.float32)  13.4 us
    rev x1, local copies, waits for them, and re-layouts, shards(): backward = finish(rev_parts, c_flip, rev_in)[::-1]  13.4 us
  transfers between devices with their start and end apart: 2, of which 0 were waited for; matrix products, arithmetic and copies ran while one was open for 42% of the time, Pallas kernels for 0%

commit v1 on v0

v1 whole, which is shorter than its diff:
```python
import functools

import jax
import jax.numpy as jnp
from jax import lax
from jax.experimental import pallas as pl
from jax.experimental.pallas import tpu as pltpu
from jax.sharding import PartitionSpec as P

INNER = 4096
BLOCK = 512
TILE = 128
LOG2E = 1.4426950408889634
VMEM = 56 * 1024 * 1024
F32, BF16 = jnp.float32, jnp.bfloat16


def running_sum(log, reverse):
    length = log.shape[1]
    lane = lax.broadcasted_iota(jnp.int32, log.shape, 1)
    total, shift = log, 1
    while shift < length:
        if reverse:
            moved, inside = pltpu.roll(total, length - shift, 1), lane < length - shift
        else:
            moved, inside = pltpu.roll(total, shift, 1), lane >= shift
        total = total + jnp.where(inside, moved, 0.0)
        shift *= 2
    return total


def spread_heads(column, headdim):
    heads = column.shape[0]
    head = lax.broadcasted_iota(jnp.int32, (heads, heads * headdim), 0)
    lane = lax.broadcasted_iota(jnp.int32, (heads, heads * headdim), 1)
    return jnp.sum(jnp.where(lane // headdim == head, column, 0.0), axis=0, keepdims=True)


def states_kernel(headdim, x_ref, b_ref, lf_ref, lr_ref, cum_ref, fresh_ref, drow_ref, final_ref):
    k = pl.program_id(0)
    heads = lf_ref.shape[0]
    state = b_ref.shape[1]

    @pl.when(k == 0)
    def _():
        final_ref[:, :state] = jnp.zeros((2, state, final_ref.shape[2]), F32)
        final_ref[:, state:] = jnp.ones((2, 8, final_ref.shape[2]), F32)

    cf = running_sum(lf_ref[...], False) * LOG2E
    cr = running_sum(lr_ref[...], True) * LOG2E
    lf, lr = cf[:, BLOCK - 1 :], cr[:, :1]
    ef, er = jnp.exp2(lf - cf), jnp.exp2(lr - cr)
    df, dr = spread_heads(jnp.exp2(lf), headdim), spread_heads(jnp.exp2(lr), headdim)
    drow_ref[0] = jnp.concatenate([df, dr, jnp.zeros((6, df.shape[1]), F32)], axis=0)
    b_t = b_ref[...].astype(F32).T
    lane = lax.broadcasted_iota(jnp.int32, (state, 2 * headdim), 1)
    for p in range(heads // 2):
        h = 2 * p
        cum_ref[p] = jnp.concatenate(
            [cf[h : h + 2], cr[h : h + 2], jnp.zeros((4, BLOCK), F32)], axis=0
        )
        rows = jnp.concatenate(
            [(b_t * e[g : g + 1]).astype(BF16) for g in (h, h + 1) for e in (ef, er)], axis=0
        )
        cols = slice(2 * headdim * p, 2 * headdim * (p + 1))
        both = jnp.dot(rows, x_ref[:, cols], preferred_element_type=F32)
        fresh_f = jnp.where(lane < headdim, both[:state], both[2 * state : 3 * state])
        fresh_r = jnp.where(lane < headdim, both[state : 2 * state], both[3 * state :])
        fresh_ref[0, 0, :, cols] = fresh_f
        fresh_ref[1, 0, :, cols] = fresh_r
        final_ref[0, :state, cols] = final_ref[0, :state, cols] * df[:, cols] + fresh_f
        final_ref[1, :state, cols] += final_ref[1, state : state + 1, cols] * fresh_r
    final_ref[0, state:] = final_ref[0, state:] * df
    final_ref[1, state:] = final_ref[1, state:] * dr


def within_kernel(headdim, x_ref, b_ref, c_ref, cum_ref, skip_ref, out_ref, score_ref):
    tiles = BLOCK // TILE
    scores = lax.dot_general(
        c_ref[...], b_ref[...], (((1,), (1,)), ((), ())), preferred_element_type=F32
    )
    row = lax.broadcasted_iota(jnp.int32, (BLOCK, BLOCK), 0)
    col = lax.broadcasted_iota(jnp.int32, (BLOCK, BLOCK), 1)
    score_ref[...] = jnp.where(row == col, 2.0 * scores, scores)
    lane = lax.broadcasted_iota(jnp.int32, (BLOCK, 2 * headdim), 1)
    lower = lax.broadcasted_iota(jnp.int32, (TILE, TILE), 0) >= lax.broadcasted_iota(
        jnp.int32, (TILE, TILE), 1
    )

    @pl.loop(0, cum_ref.shape[0])
    def _(p):
        cum = cum_ref[p]
        cum_t = cum.T
        cols = pl.ds(pl.multiple_of(p * 2 * headdim, 2 * headdim), 2 * headdim)
        x = x_ref[:, cols]
        parts = []
        for q in range(2):
            lines = []
            for i in range(tiles):
                at = slice(i * TILE, (i + 1) * TILE)
                cf, cr = cum_t[at, q : q + 1], cum_t[at, 2 + q : 3 + q]
                pieces = []
                for j in range(tiles):
                    to = slice(j * TILE, (j + 1) * TILE)
                    rf, rr = cum[q : q + 1, to], cum[2 + q : 3 + q, to]
                    if j < i:
                        gap = cf - rf
                    elif j > i:
                        gap = cr - rr
                    else:
                        gap = jnp.where(lower, cf - rf, cr - rr)
                    pieces.append((jnp.exp2(gap) * score_ref[at, to]).astype(BF16))
                lines.append(jnp.concatenate(pieces, axis=1))
            weights = jnp.concatenate(lines, axis=0)
            parts.append(jnp.dot(weights, x, preferred_element_type=F32))
        y = jnp.where(lane < headdim, parts[0], parts[1])
        out_ref[:, cols] = y + skip_ref[:, cols] * x.astype(F32)


def halves(value):
    high = value.astype(BF16)
    return jnp.concatenate([high, (value - high.astype(F32)).astype(BF16)], axis=0)


def carried_kernel(
    headdim, a_ref, gate_ref, c_ref, cum_ref, drow_ref, fresh_ref, in_ref, out_ref, sq_ref, st_ref, hot_ref
):
    k = pl.program_id(0)
    blocks = fresh_ref.shape[1]
    pairs = cum_ref.shape[0]
    channels = a_ref.shape[1]

    @pl.when(k == 0)
    def _():
        row = lax.broadcasted_iota(jnp.int32, (16 * pairs, channels), 0)
        head = lax.broadcasted_iota(jnp.int32, (16 * pairs, channels), 1) // headdim
        row = lax.rem(row, 8 * pairs)
        for d in range(2):
            mine = row == 8 * (head // 2) + lax.rem(head, 2) + 2 * d
            hot_ref[d] = jnp.where(mine, 1.0, 0.0).astype(BF16)
        for d in range(2):
            total = in_ref[d]
            for step in range(blocks):
                at = step if d == 0 else blocks - 1 - step
                st_ref[d, at] = halves(total)
                if step < blocks - 1:
                    total = total * drow_ref[at, d : d + 1] + fresh_ref[d, at]

    decay = jnp.exp2(cum_ref[...].reshape(8 * pairs, BLOCK))
    high = decay.astype(BF16).astype(F32)
    decay_t = jnp.concatenate([high, decay - high], axis=0).T.astype(BF16)
    c = c_ref[...]
    cc = jnp.concatenate([c, c], axis=1)
    wide = 256
    squares = jnp.zeros((BLOCK, 128), F32)
    for n in range(channels // wide):
        cols = slice(n * wide, (n + 1) * wide)
        total = a_ref[:, cols]
        for d in range(2):
            scale = jnp.dot(decay_t, hot_ref[d, :, cols], preferred_element_type=F32)
            total = total + scale * jnp.dot(cc, st_ref[d, k, :, cols], preferred_element_type=F32)
        gate = gate_ref[:, cols].astype(F32)
        gated = total * (gate / (1.0 + jnp.exp(-gate)))
        out_ref[:, cols] = gated
        square = gated * gated
        for m in range(wide // 128):
            squares = squares + square[:, m * 128 : (m + 1) * 128]
    sq_ref[0] = jnp.sum(squares.T, axis=0, keepdims=True)


def norm_kernel(gated_ref, sq_ref, gain_ref, out_ref):
    factor = lax.rsqrt(sq_ref[0] * (1.0 / INNER) + 1e-05)
    factor = jnp.broadcast_to(factor, (128, factor.shape[1])).T
    for n in range(gated_ref.shape[1] // 128):
        cols = slice(n * 128, (n + 1) * 128)
        out_ref[:, cols] = (gated_ref[:, cols] * factor * gain_ref[:, cols]).astype(BF16)


def params():
    return pltpu.CompilerParams(vmem_limit_bytes=VMEM, dimension_semantics=("arbitrary",))


def across(value, pairs):
    return lax.ppermute(value, "seq", pairs)


def incoming(final):
    count, mine = lax.axis_size("seq"), lax.axis_index("seq")
    rows, row, side = count // 2, mine // 2, mine % 2
    state, half = final.shape[1] - 8, final.shape[2] // 2
    first, second = final[:, :, :half], final[:, :, half:]
    swap = [(i, i ^ 1) for i in range(count)]
    kept = jnp.where(side == 0, first, second)
    got = across(jnp.where(side == 0, second, first), swap)
    low, high = jnp.where(side == 0, kept, got), jnp.where(side == 0, got, kept)
    low_d, high_d = low[:, state : state + 1], high[:, state : state + 1]
    low, high = low[:, :state], high[:, :state]
    pair_f, pair_r = high_d[0] * low[0] + high[0], low_d[1] * high[1] + low[1]
    pair_d = low_d * high_d
    enter_f = jnp.zeros_like(pair_f)
    enter_r = jnp.zeros_like(pair_r)
    for hop in range(rows - 1):
        back = rows - 1 - hop
        send = jnp.where(row == hop, pair_d[0] * enter_f + pair_f, pair_d[1] * enter_r + pair_r)
        route = [(2 * hop + s, 2 * hop + 2 + s) for s in range(2)]
        route += [(2 * back + s, 2 * back - 2 + s) for s in range(2)]
        got = across(send, route)
        enter_f = jnp.where(row == hop + 1, got, enter_f)
        enter_r = jnp.where(row == back - 1, got, enter_r)
    at_low = jnp.stack([enter_f, high_d[1] * enter_r + high[1]])
    at_high = jnp.stack([low_d[0] * enter_f + low[0], enter_r])
    got = across(jnp.where(side == 0, at_high, at_low), swap)
    kept = jnp.where(side == 0, at_low, at_high)
    return jnp.concatenate(
        [jnp.where(side == 0, kept, got), jnp.where(side == 0, got, kept)], axis=2
    )


def shards(activations, gate_input, bmat, cmat, log_fwd, log_rev, skip, gain):
    length, channels = activations.shape
    heads = log_fwd.shape[0]
    headdim = channels // heads
    pairs = heads // 2
    state = bmat.shape[1]
    blocks = length // BLOCK
    tall = pl.BlockSpec((BLOCK, channels), lambda k: (k, 0))
    thin = pl.BlockSpec((BLOCK, state), lambda k: (k, 0))
    logs = pl.BlockSpec((heads, BLOCK), lambda k: (0, k))
    cums = pl.BlockSpec((pairs, 8, BLOCK), lambda k: (0, 0, k))
    line = pl.BlockSpec((1, channels), lambda k: (0, 0))
    tiny = pl.BlockSpec((1, 1, BLOCK), lambda k: (k, 0, 0))
    cum, fresh, drow, final = pl.pallas_call(
        functools.partial(states_kernel, headdim),
        grid=(blocks,),
        in_specs=[tall, thin, logs, logs],
        out_specs=[
            cums,
            pl.BlockSpec((2, 1, state, channels), lambda k: (0, k, 0, 0)),
            pl.BlockSpec((1, 8, channels), lambda k: (k, 0, 0)),
            pl.BlockSpec((2, state + 8, channels), lambda k: (0, 0, 0)),
        ],
        out_shape=[
            jax.ShapeDtypeStruct((pairs, 8, length), F32),
            jax.ShapeDtypeStruct((2, blocks, state, channels), F32),
            jax.ShapeDtypeStruct((blocks, 8, channels), F32),
            jax.ShapeDtypeStruct((2, state + 8, channels), F32),
        ],
        compiler_params=params(),
        name="states",
    )(activations, bmat, log_fwd, log_rev)
    skip_row = jnp.repeat(skip, headdim)[None]
    within = pl.pallas_call(
        functools.partial(within_kernel, headdim),
        grid=(blocks,),
        in_specs=[tall, thin, thin, cums, line],
        out_specs=tall,
        out_shape=jax.ShapeDtypeStruct((length, channels), F32),
        scratch_shapes=[pltpu.VMEM((BLOCK, BLOCK), F32)],
        compiler_params=params(),
        cost_estimate=pl.CostEstimate(
            flops=2 * heads * length * BLOCK * 128, bytes_accessed=6 * length * channels,
            transcendentals=heads * length * BLOCK,
        ),
        name="within",
    )(activations, bmat, cmat, cum, skip_row)
    enter = incoming(final)
    gated, squares = pl.pallas_call(
        functools.partial(carried_kernel, headdim),
        grid=(blocks,),
        in_specs=[
            tall,
            tall,
            thin,
            cums,
            pl.BlockSpec((blocks, 8, channels), lambda k: (0, 0, 0)),
            pl.BlockSpec((2, blocks, state, channels), lambda k: (0, 0, 0, 0)),
            pl.BlockSpec((2, state, channels), lambda k: (0, 0, 0)),
        ],
        out_specs=[tall, tiny],
        out_shape=[
            jax.ShapeDtypeStruct((length, channels), F32),
            jax.ShapeDtypeStruct((blocks, 1, BLOCK), F32),
        ],
        scratch_shapes=[
            pltpu.VMEM((2, blocks, 2 * state, channels), BF16),
            pltpu.VMEM((2, 16 * pairs, channels), BF16),
        ],
        compiler_params=params(),
        name="carried",
    )(within, gate_input, cmat, cum, drow, fresh, enter)
    step, size = 1, lax.axis_size("ch")
    while step < size:
        squares = squares + lax.ppermute(squares, "ch", [(i, i ^ step) for i in range(size)])
        step *= 2
    return pl.pallas_call(
        norm_kernel,
        grid=(blocks,),
        in_specs=[tall, tiny, line],
        out_specs=tall,
        out_shape=jax.ShapeDtypeStruct((length, channels), BF16),
        compiler_params=params(),
        name="norm",
    )(gated, squares, gain[None])


def solution(mesh):
    return jax.shard_map(
        shards,
        mesh=mesh,
        in_specs=(
            P("seq", "ch"),
            P("seq", "ch"),
            P("seq", None),
            P("seq", None),
            P("ch", "seq"),
            P("ch", "seq"),
            P("ch"),
            P("ch"),
        ),
        out_specs=P("seq", "ch"),
        check_vma=False,
    )
```

time: 342 us -> 112 us (0.33)
  matrix products: 126 us -> 0 us
  local copies, waits for them, and re-layouts: 104 us -> 0.76 us
  other arithmetic: 64.7 us -> 5.89 us
  Pallas kernels: 0 us -> 57.9 us
  waiting for transfers between devices: 0.04 us -> 35.2 us
  blocking collectives: 29.3 us -> 0 us
  between operations: 14.3 us -> 0.16 us
  starting transfers between devices: 0.04 us -> 11.9 us
    dot_general x26 -> x0, matrix products: 126 us -> none  [the longest x8 57.1 us: advance(): jnp.einsum('hij,jhp->ihp', weights, x_block, preferred_element_type=jnp.f...]
    pallas_call x0 -> x4, Pallas kernels: none -> 57.9 us  [the longest x1 27.6 us: shards(): pl.pallas_call(functools.partial(within_kernel, headdim), grid=(blocks,),...]
    ppermute x0 -> x7, waiting for transfers between devices: none -> 35.2 us  [the longest x5 31.7 us: across(): return lax.ppermute(value, 'seq', pairs)]
    rev x7 -> x0, local copies, waits for them, and re-layouts: 31.4 us -> none  [the longest x1 13.4 us: shards(): backward = finish(rev_parts, c_flip, rev_in)[::-1]]
    unnamed x30 -> x2, local copies, waits for them, and re-layouts: 25.2 us -> 0.01 us
    another operation x41 -> x1, local copies, waits for them, and re-layouts: 24.4 us -> 0.67 us  [shards(): skip_row = jnp.repeat(skip, headdim)[None]]
    unnamed x1 -> x0, blocking collectives: 23.5 us -> none
    reshape x9 -> x0, local copies, waits for them, and re-layouts: 13.5 us -> none  [the longest x2 8.49 us: finish(): return (within + carried).reshape(blocks * length, heads, headdim)]
  transfers between devices with their start and end apart: 2 -> 7, of which waited for: 0 -> 5; matrix products, arithmetic and copies ran while one was open for 42% -> 1% of each run, Pallas kernels for 0% -> 25%
where the time goes in v1:
time: 112 us
  Pallas kernels  57.9 us (52%)
  waiting for transfers between devices  35.2 us (31%)
  starting transfers between devices  11.9 us (11%)
  other arithmetic  5.89 us (5%)
    ppermute x5, waiting for transfers between devices, across(): return lax.ppermute(value, 'seq', pairs)  31.7 us
    pallas_call x1, Pallas kernels, shards(): pl.pallas_call(functools.partial(within_kernel, headdim), grid=(blocks,),...  27.6 us
    pallas_call x1, Pallas kernels, shards(): pl.pallas_call(functools.partial(carried_kernel, headdim), grid=(blocks,)...  13.6 us
    pallas_call x1, Pallas kernels, shards(): pl.pallas_call(functools.partial(states_kernel, headdim), grid=(blocks,),...  10.5 us
    ppermute x5, starting transfers between devices, across(): return lax.ppermute(value, 'seq', pairs)  10.3 us
    pallas_call x1, Pallas kernels, shards(): pl.pallas_call(norm_kernel, grid=(blocks,), in_specs=[tall, tiny, line],...  6.22 us
    ppermute x2, waiting for transfers between devices, shards(): lax.ppermute(squares, 'ch', [(i, i ^ step) for i in range(size)])  3.51 us
  transfers between devices with their start and end apart: 7, of which 5 were waited for; matrix products, arithmetic and copies ran while one was open for 1% of the time, Pallas kernels for 25%

profile of v1, /device:TPU:0, one launch (start us, length us, event | category | flops | bytes accessed | tf_op | source)
XLA Modules:
  0.0 111.8 jit_solution(14899894468276003842)
XLA Ops:
  0.0 10.5 %states.1 = (f32[8,8,2048]{2,1,0:T(8,128)}, f32[2,4,128,1024]{3,2,1,0:T(8,128)}, f32[4,8,1024]{2,1,0:T(8,128)}, f32[2,136,1024]{2,1,0:T(8,128)}) custom-call(bf16[2048,1024]{1,0:T(8,128)(2,1)} %x_ref.3, bf16[2048,128]{1,0:T(8,128)(2,1)} %b_ref.3, f32[16,2048]{1,0:T(8,128)} %lf_ref.1, f32[16,2048]{1,0:T(8,128)} %lr_ref.1), custom_call_target="tpu_custom_call" | custom-call | tf_op jit(solution)/shard_map/states/pallas_call | solution.py:232
  10.5 1.3 %slice_select_fusion = f32[2,136,512]{2,1,0:T(8,128)S(1)} fusion(f32[2,136,1024]{2,1,0:T(8,128)} %get-tuple-element.14, pred[]{:T(512)S(6)} %eq.12), kind=kLoop, calls=%fused_computation.3 | loop fusion | flops 139264 | bytes 1671169 | tf_op jit(solution)/shard_map/jit(_where)/select_n | solution.py:194
  11.8 3.0 %collective-permute-start = (f32[2,136,512]{2,1,0:T(8,128)S(1)}, f32[2,136,512]{2,1,0:T(8,128)S(1)}, u32[]{:S(2)}, u32[]{:S(2)}) collective-permute-start(f32[2,136,512]{2,1,0:T(8,128)S(1)} %slice_select_fusion), channel_id=1, source_target_pairs={{0,4},{4,0},{8,12},{12,8},{16,20},{20,16},{24,28},{28,24},{1,5},{5... | collective-permute-start | bytes 1671176 | tf_op jit(solution)/shard_map/ppermute | solution.py:184
  14.8 12.6 %collective-permute-done = f32[2,136,512]{2,1,0:T(8,128)S(1)} collective-permute-done((f32[2,136,512]{2,1,0:T(8,128)S(1)}, f32[2,136,512]{2,1,0:T(8,128)S(1)}, u32[]{:S(2)}, u32[]{:S(2)}) %collective-permute-start) | collective-permute-done | bytes 557088 | tf_op jit(solution)/shard_map/ppermute | solution.py:184
  27.5 1.4 %broadcast_select_fusion.1 = (f32[2,136,512]{2,1,0:T(8,128)S(1)}, f32[2,136,512]{2,1,0:T(8,128)S(1)}) fusion(f32[2,136,512]{2,1,0:T(8,128)S(1)} %collective-permute-done, pred[]{:T(512)S(6)} %eq.12, f32[2,136,1024]{2,1,0:T(8,128)} %get-tuple-element.14), kind=kLoop, calls=%fused_computation.8 | loop fusion | flops 417792 | bytes 2785281 | tf_op jit(solution)/shard_map/jit(_where)/select_n | solution.py:195
  28.9 0.0 copy-start
  29.0 0.1 add_select_fusion.2
  29.1 3.7 %collective-permute-start.1 = (f32[128,512]{1,0:T(8,128)S(1)}, f32[128,512]{1,0:T(8,128)S(1)}, u32[]{:S(2)}, u32[]{:S(2)}) collective-permute-start(f32[128,512]{1,0:T(8,128)S(1)} %get-tuple-element.20), channel_id=1, source_target_pairs={{0,8},{4,12},{24,16},{28,20},{1,9},{5,13},{25,17},{29,21},{2,10},{... | collective-permute-start | bytes 786440 | tf_op jit(solution)/shard_map/ppermute | solution.py:184
  32.9 4.7 %collective-permute-done.1 = f32[128,512]{1,0:T(8,128)S(1)} collective-permute-done((f32[128,512]{1,0:T(8,128)S(1)}, f32[128,512]{1,0:T(8,128)S(1)}, u32[]{:S(2)}, u32[]{:S(2)}) %collective-permute-start.1) | collective-permute-done | bytes 262176 | tf_op jit(solution)/shard_map/ppermute | solution.py:184
  37.5 0.1 add_select_fusion.1
  37.6 0.7 collective-permute-start.2
  38.3 0.0 collective-permute-done.2
  38.3 0.1 add_select_fusion
  38.4 1.3 %collective-permute-start.3 = (f32[128,512]{1,0:T(8,128)S(1)}, f32[128,512]{1,0:T(8,128)S(1)}, u32[]{:S(2)}, u32[]{:S(2)}) collective-permute-start(f32[128,512]{1,0:T(8,128)S(1)} %get-tuple-element.17), channel_id=1, source_target_pairs={{16,24},{20,28},{8,0},{12,4},{17,25},{21,29},{9,1},{13,5},{18,26},... | collective-permute-start | bytes 786440 | tf_op jit(solution)/shard_map/ppermute | solution.py:184
  39.7 14.4 %collective-permute-done.3 = f32[128,512]{1,0:T(8,128)S(1)} collective-permute-done((f32[128,512]{1,0:T(8,128)S(1)}, f32[128,512]{1,0:T(8,128)S(1)}, u32[]{:S(2)}, u32[]{:S(2)}) %collective-permute-start.3) | collective-permute-done | bytes 262176 | tf_op jit(solution)/shard_map/ppermute | solution.py:184
  54.1 0.2 fusion.4
  54.3 0.1 fusion
  54.4 1.6 %collective-permute-start.4 = (f32[2,128,512]{2,1,0:T(8,128)S(1)}, f32[2,128,512]{2,1,0:T(8,128)S(1)}, u32[]{:S(2)}, u32[]{:S(2)}) collective-permute-start(f32[2,128,512]{2,1,0:T(8,128)S(1)} %fusion), channel_id=1, source_target_pairs={{0,4},{4,0},{8,12},{12,8},{16,20},{20,16},{24,28},{28,24},{1,5},{5... | collective-permute-start | bytes 1572872 | tf_op jit(solution)/shard_map/ppermute | solution.py:184
  55.9 0.0 copy-done
  55.9 0.1 broadcast_in_dim.6
  56.0 0.7 broadcast_in_dim_reshape.3.skip_ref
  56.7 27.6 %within.1.a_ref = f32[2048,1024]{1,0:T(8,128)} custom-call(bf16[2048,1024]{1,0:T(8,128)(2,1)} %x_ref.3, bf16[2048,128]{1,0:T(8,128)(2,1)} %b_ref.3, bf16[2048,128]{1,0:T(8,128)(2,1)} %c_ref.3, f32[8,8,2048]{2,1,0:T(8,128)} %get-tuple-element.11.cum_ref, f32[1,1024]{1,0:T(1,128)} %broadcast_in_dim_reshape.3.skip_ref), custom_call_target="tpu_custom_call" | custom-call | flops 4294967296 | bytes 12582912 | tf_op jit(solution)/shard_map/within/pallas_call | solution.py:252
  84.2 0.0 collective-permute-done.4
  84.3 0.2 broadcast_select_fusion.3
  84.4 1.1 pad_maximum_fusion.in_ref
  85.5 13.6 %carried.1 = (f32[2048,1024]{1,0:T(8,128)}, f32[4,1,512]{2,1,0:T(1,128)}) custom-call(f32[2048,1024]{1,0:T(8,128)} %within.1.a_ref, bf16[2048,1024]{1,0:T(8,128)(2,1)} %gate_ref.1, bf16[2048,128]{1,0:T(8,128)(2,1)} %c_ref.3, f32[8,8,2048]{2,1,0:T(8,128)} %get-tuple-element.11.cum_ref, f32[4,8,1024]{2,1,0:T(8,128)} %get-tuple-element.12.drow_ref, ...), custom_call_target="tpu_custom_call" | custom-call | tf_op jit(solution)/shard_map/carried/pallas_call | solution.py:267
  99.1 0.0 collective-permute-start.5
  99.1 1.4 %collective-permute-done.5 = f32[4,1,512]{2,1,0:T(1,128)S(1)} collective-permute-done((f32[4,1,512]{2,1,0:T(1,128)}, f32[4,1,512]{2,1,0:T(1,128)S(1)}, u32[]{:S(2)}, u32[]{:S(2)}) %collective-permute-start.5) | collective-permute-done | bytes 8224 | tf_op jit(solution)/shard_map/ppermute | solution.py:293
  100.5 0.7 add.52
  101.2 1.6 %collective-permute-start.6 = (f32[4,1,512]{2,1,0:T(1,128)S(1)}, f32[4,1,512]{2,1,0:T(1,128)S(1)}, u32[]{:S(2)}, u32[]{:S(2)}) collective-permute-start(f32[4,1,512]{2,1,0:T(1,128)S(1)} %add.52), channel_id=1, source_target_pairs={{0,2},{1,3},{2,0},{3,1},{4,6},{5,7},{6,4},{7,5},{8,10},{9,11},{10,... | collective-permute-start | bytes 24584 | tf_op jit(solution)/shard_map/ppermute | solution.py:293
  102.8 2.1 %collective-permute-done.6 = f32[4,1,512]{2,1,0:T(1,128)S(1)} collective-permute-done((f32[4,1,512]{2,1,0:T(1,128)S(1)}, f32[4,1,512]{2,1,0:T(1,128)S(1)}, u32[]{:S(2)}, u32[]{:S(2)}) %collective-permute-start.6) | collective-permute-done | bytes 8224 | tf_op jit(solution)/shard_map/ppermute | solution.py:293
  104.9 0.6 add.53.sq_ref
  105.5 6.2 %norm.1 = bf16[2048,1024]{1,0:T(8,128)(2,1)} custom-call(f32[2048,1024]{1,0:T(8,128)} %get-tuple-element.15.gated_ref, f32[4,1,512]{2,1,0:T(1,128)} %add.53.sq_ref, f32[1,1024]{1,0:T(1,128)} %bitcast.49), custom_call_target="tpu_custom_call" | custom-call | tf_op jit(solution)/shard_map/norm/pallas_call | solution.py:295
  (4 shorter events, 0.0 us)
Async XLA Ops:
  11.8 15.6 %collective-permute-start = (f32[2,136,512]{2,1,0:T(8,128)S(1)}, f32[2,136,512]{2,1,0:T(8,128)S(1)}, u32[]{:S(2)}, u32[]{:S(2)}) collective-permute-start(f32[2,136,512]{2,1,0:T(8,128)S(1)} %slice_select_fusion), channel_id=1, source_target_pairs={{0,4},{4,0},{8,12},{12,8},{16,20},{20,16},{24,28},{28,24},{1,5},{5... | collective-permute-start | bytes 1671176 | tf_op jit(solution)/shard_map/ppermute | solution.py:184
  28.9 27.0 %copy-start = (f32[16]{0:T(128)S(1)}, f32[16]{0:T(128)}, u32[]{:S(2)}) copy-start(f32[16]{0:T(128)} %param.14) | copy-start | bytes 196
  29.1 8.4 %collective-permute-start.1 = (f32[128,512]{1,0:T(8,128)S(1)}, f32[128,512]{1,0:T(8,128)S(1)}, u32[]{:S(2)}, u32[]{:S(2)}) collective-permute-start(f32[128,512]{1,0:T(8,128)S(1)} %get-tuple-element.20), channel_id=1, source_target_pairs={{0,8},{4,12},{24,16},{28,20},{1,9},{5,13},{25,17},{29,21},{2,10},{... | collective-permute-start | bytes 786440 | tf_op jit(solution)/shard_map/ppermute | solution.py:184
  37.6 0.7 collective-permute-start.2
  38.4 15.7 %collective-permute-start.3 = (f32[128,512]{1,0:T(8,128)S(1)}, f32[128,512]{1,0:T(8,128)S(1)}, u32[]{:S(2)}, u32[]{:S(2)}) collective-permute-start(f32[128,512]{1,0:T(8,128)S(1)} %get-tuple-element.17), channel_id=1, source_target_pairs={{16,24},{20,28},{8,0},{12,4},{17,25},{21,29},{9,1},{13,5},{18,26},... | collective-permute-start | bytes 786440 | tf_op jit(solution)/shard_map/ppermute | solution.py:184
  54.4 29.9 %collective-permute-start.4 = (f32[2,128,512]{2,1,0:T(8,128)S(1)}, f32[2,128,512]{2,1,0:T(8,128)S(1)}, u32[]{:S(2)}, u32[]{:S(2)}) collective-permute-start(f32[2,128,512]{2,1,0:T(8,128)S(1)} %fusion), channel_id=1, source_target_pairs={{0,4},{4,0},{8,12},{12,8},{16,20},{20,16},{24,28},{28,24},{1,5},{5... | collective-permute-start | bytes 1572872 | tf_op jit(solution)/shard_map/ppermute | solution.py:184
  99.1 1.4 %collective-permute-start.5 = (f32[4,1,512]{2,1,0:T(1,128)}, f32[4,1,512]{2,1,0:T(1,128)S(1)}, u32[]{:S(2)}, u32[]{:S(2)}) collective-permute-start(f32[4,1,512]{2,1,0:T(1,128)} %get-tuple-element.16), channel_id=1, source_target_pairs={{0,1},{1,0},{2,3},{3,2},{4,5},{5,4},{6,7},{7,6},{8,9},{9,8},{10,11... | collective-permute-start | bytes 24584 | tf_op jit(solution)/shard_map/ppermute | solution.py:293
  101.2 3.7 %collective-permute-start.6 = (f32[4,1,512]{2,1,0:T(1,128)S(1)}, f32[4,1,512]{2,1,0:T(1,128)S(1)}, u32[]{:S(2)}, u32[]{:S(2)}) collective-permute-start(f32[4,1,512]{2,1,0:T(1,128)S(1)} %add.52), channel_id=1, source_target_pairs={{0,2},{1,3},{2,0},{3,1},{4,6},{5,7},{6,4},{7,5},{8,10},{9,11},{10,... | collective-permute-start | bytes 24584 | tf_op jit(solution)/shard_map/ppermute | solution.py:293

commit v2 on v0

v2 whole, which is shorter than its diff:
```python
import functools

import jax
import jax.numpy as jnp
from jax import lax
from jax.experimental import pallas as pl
from jax.experimental.pallas import tpu as pltpu
from jax.sharding import PartitionSpec as P

INNER = 4096
BLOCK = 512
TILE = 128
TILES = BLOCK // TILE
GROUPS = 1
LOG2E = 1.4426950408889634
F32, BF16 = jnp.float32, jnp.bfloat16
ANY = pl.BlockSpec(memory_space=pl.ANY)


def shape(*dims, dtype=F32):
    return jax.ShapeDtypeStruct(dims, dtype)


def far(*values):
    return [pltpu.with_memory_space_constraint(value, pltpu.HBM) for value in values]


def near(*values):
    return [pltpu.with_memory_space_constraint(value, pltpu.VMEM) for value in values]


def params(mib):
    return pltpu.CompilerParams(
        vmem_limit_bytes=mib * 1024 * 1024, dimension_semantics=("arbitrary",)
    )


def running_sums(log, reverse):
    heads, length = log.shape
    rows = jnp.concatenate(
        [log[:, at : at + BLOCK] for at in range(0, length, BLOCK)], axis=0
    )
    high = rows.astype(BF16)
    rest = rows - high.astype(F32)
    middle = rest.astype(BF16)
    low = (rest - middle.astype(F32)).astype(BF16)
    u = lax.broadcasted_iota(jnp.int32, (BLOCK, BLOCK), 0)
    t = lax.broadcasted_iota(jnp.int32, (BLOCK, BLOCK), 1)
    taken = jnp.where(u >= t if reverse else u <= t, 1.0, 0.0).astype(BF16)
    total = [jnp.dot(part, taken, preferred_element_type=F32) for part in (low, middle, high)]
    return total[0] + total[1] + total[2]


def halves(value):
    high = value.astype(BF16)
    return jnp.concatenate([high, (value - high.astype(F32)).astype(BF16)], axis=0)


def states_kernel(headdim, chained, x_ref, b_ref, lf_ref, lr_ref, *refs):
    cum_ref, dev_ref, st_ref, final_ref, bt_ref, sum_ref = refs[3 if chained else 0 :]
    p = pl.program_id(0)
    pairs, blocks = sum_ref.shape[:2]
    state = b_ref.shape[1]

    @pl.when(p == 0)
    def _():
        cf = running_sums(lf_ref[...], False) * LOG2E
        cr = running_sums(lr_ref[...], True) * LOG2E
        for k in range(blocks):
            bt_ref[k] = b_ref[k * BLOCK : (k + 1) * BLOCK].astype(F32).T
            for i in range(pairs):
                h = slice(2 * (k * pairs + i), 2 * (k * pairs + i) + 2)
                sum_ref[i, k, 0:2] = cf[h]
                sum_ref[i, k, 2:4] = cr[h]
                sum_ref[i, k, 4:8] = jnp.zeros((4, BLOCK), F32)

    first = lax.broadcasted_iota(jnp.int32, (1, 2 * headdim), 1) < headdim
    lane = lax.broadcasted_iota(jnp.int32, (state, 2 * headdim), 1)
    forward = lax.broadcasted_iota(jnp.int32, (8, 1), 0) < 2
    fresh, decay, total = [], [], []
    for k in range(blocks):
        at = slice(k * BLOCK, (k + 1) * BLOCK)
        cum = sum_ref[p, k]
        last = jnp.where(forward, cum[:, BLOCK - 1 :], cum[:, :1])
        to_end = jnp.exp2(last - cum)
        whole = jnp.exp2(last)
        rows = jnp.concatenate(
            [(bt_ref[k] * to_end[r : r + 1]).astype(BF16) for r in range(4)], axis=0
        )
        both = jnp.dot(rows, x_ref[at], preferred_element_type=F32)
        fresh.append(
            [
                jnp.where(
                    lane < headdim,
                    both[2 * d * state : (2 * d + 1) * state],
                    both[(2 * d + 1) * state : (2 * d + 2) * state],
                )
                for d in range(2)
            ]
        )
        decay.append(
            [
                jnp.where(first, whole[2 * d : 2 * d + 1], whole[2 * d + 1 : 2 * d + 2])
                for d in range(2)
            ]
        )
        total.append(last)
        cum_ref[0, :, at] = cum
    for d in range(2):
        order = range(blocks) if d == 0 else range(blocks - 1, -1, -1)
        held = jnp.zeros_like(fresh[0][0])
        through = jnp.ones_like(decay[0][0])
        for k in order:
            st_ref[d, k] = halves(held)
            held = held * decay[k][d] + fresh[k][d]
            through = through * decay[k][d]
        final_ref[d, :state] = held
        final_ref[d, state:] = jnp.broadcast_to(through, (8, 2 * headdim))
    before = jnp.zeros((8, 1), F32)
    after = jnp.zeros((8, 1), F32)
    for k in range(blocks):
        at = slice(k * BLOCK, (k + 1) * BLOCK)
        back = slice((blocks - 1 - k) * BLOCK, (blocks - k) * BLOCK)
        dev_ref[0, 0:2, at] = (sum_ref[p, k] + before)[0:2]
        dev_ref[0, 2:4, back] = (sum_ref[p, blocks - 1 - k] + after)[2:4]
        dev_ref[0, 4:8, at] = jnp.zeros((4, BLOCK), F32)
        before = before + total[k]
        after = after + total[blocks - 1 - k]


def within_kernel(headdim, chained, x_ref, b_ref, c_ref, cum_ref, st_ref, skip_ref, dep_ref, *refs):
    out_ref, zero_ref, score_ref, row_ref, col_ref = refs[1 if chained else 0 :]
    width = 2 * headdim
    pairs = cum_ref.shape[0]
    zero_ref[...] = jnp.zeros_like(zero_ref)

    @pl.when(pl.program_id(0) == 0)
    def _():
        scores = lax.dot_general(
            c_ref[...], b_ref[...], (((1,), (1,)), ((), ())), preferred_element_type=F32
        )
        row = lax.broadcasted_iota(jnp.int32, (BLOCK, BLOCK), 0)
        col = lax.broadcasted_iota(jnp.int32, (BLOCK, BLOCK), 1)
        score_ref[...] = jnp.where(row == col, 2.0 * scores, scores)

    first = lax.broadcasted_iota(jnp.int32, (1, width), 1) < headdim
    lower = lax.broadcasted_iota(jnp.int32, (TILE, TILE), 0) >= lax.broadcasted_iota(
        jnp.int32, (TILE, TILE), 1
    )
    forward = lax.broadcasted_iota(jnp.int32, (8, 1), 0) < 2
    none = jnp.zeros((8, 1), F32)
    c = c_ref[...]
    cc = jnp.concatenate([c, c], axis=1)
    for p in range(pairs):
        cum = cum_ref[p]
        starts = []
        for i in range(TILES):
            lo = cum[:, i * TILE - 1 : i * TILE] if i else none
            hi = cum[:, (i + 1) * TILE : (i + 1) * TILE + 1] if i < TILES - 1 else none
            base = jnp.where(forward, lo, hi)
            row_ref[p, i] = jnp.exp2(base - cum)
            at = slice(i * TILE, (i + 1) * TILE)
            col_ref[p, :, at] = jnp.exp2(cum[:, at] - base)
            starts.append(jnp.exp2(base))
        cols = slice(p * width, (p + 1) * width)
        x = x_ref[:, cols]
        tall = []
        for i in range(TILES):
            at = slice(i * TILE, (i + 1) * TILE)
            tall.append(
                [jnp.broadcast_to(col_ref[p, r : r + 1, at], (TILE, TILE)).T for r in range(4)]
            )
        parts = []
        for q in range(2):
            lines = []
            for i in range(TILES):
                at = slice(i * TILE, (i + 1) * TILE)
                cf, cr = tall[i][q], tall[i][2 + q]
                pieces = []
                for j in range(TILES):
                    to = slice(j * TILE, (j + 1) * TILE)
                    rf = row_ref[p, i, q : q + 1, to]
                    rr = row_ref[p, i, 2 + q : 3 + q, to]
                    score = score_ref[at, to]
                    if j < i:
                        weight = (score * rf) * cf
                    elif j > i:
                        weight = (score * rr) * cr
                    else:
                        weight = score * jnp.where(lower, rf * cf, rr * cr)
                    pieces.append(weight.astype(BF16))
                lines.append(jnp.concatenate(pieces, axis=1))
            weights = jnp.concatenate(lines, axis=0)
            parts.append(jnp.dot(weights, x, preferred_element_type=F32))
        held = jnp.concatenate([st_ref[0, 0, :, cols], st_ref[1, 0, :, cols]], axis=1)
        z = jnp.dot(cc, held, preferred_element_type=F32)
        for i in range(TILES):
            at = slice(i * TILE, (i + 1) * TILE)
            y = jnp.where(first, parts[0][at], parts[1][at])
            y = y + skip_ref[:, cols] * x[at].astype(F32)
            for d in range(2):
                scale = jnp.where(first, starts[i][2 * d : 2 * d + 1], starts[i][2 * d + 1 : 2 * d + 2])
                scale = scale * jnp.where(first, tall[i][2 * d], tall[i][2 * d + 1])
                y = y + scale * z[at, d * width : (d + 1) * width]
            out_ref[at, cols] = y


def carried_kernel(headdim, chained, a_ref, gate_ref, c_ref, dev_ref, in_ref, *refs):
    out_ref, sq_ref, st_ref, hot_ref = refs[1 if chained else 0 :]
    pairs = dev_ref.shape[0]
    width = 2 * headdim

    @pl.when(pl.program_id(0) == 0)
    def _():
        row = lax.rem(lax.broadcasted_iota(jnp.int32, (16 * pairs, 2 * width), 0), 8 * pairs)
        lane = lax.broadcasted_iota(jnp.int32, (16 * pairs, 2 * width), 1)
        for p in range(pairs):
            hot = jnp.where(row == 8 * p + lane // headdim, 1.0, 0.0)
            hot_ref[:, 2 * width * p : 2 * width * (p + 1)] = hot.astype(BF16)
            for d in range(2):
                at = 2 * width * p + width * d
                st_ref[:, at : at + width] = halves(in_ref[d, :, p * width : (p + 1) * width])

    decay = jnp.exp2(dev_ref[...].reshape(8 * pairs, BLOCK))
    high = decay.astype(BF16).astype(F32)
    decay_t = jnp.concatenate([high, decay - high], axis=0).T.astype(BF16)
    c = c_ref[...]
    cc = jnp.concatenate([c, c], axis=1)
    squares = jnp.zeros((BLOCK, width), F32)
    for p in range(pairs):
        cols = slice(p * width, (p + 1) * width)
        wide = slice(2 * p * width, 2 * (p + 1) * width)
        scale = jnp.dot(decay_t, hot_ref[:, wide], preferred_element_type=F32)
        both = scale * jnp.dot(cc, st_ref[:, wide], preferred_element_type=F32)
        total = a_ref[:, cols] + both[:, :width] + both[:, width:]
        gate = gate_ref[:, cols].astype(F32)
        gated = total * (gate / (1.0 + jnp.exp(-gate)))
        out_ref[:, cols] = gated
        squares = squares + gated * gated
    sq_ref[0] = jnp.sum(squares.T, axis=0, keepdims=True)


def norm_kernel(gated_ref, sq_ref, gain_ref, out_ref):
    factor = lax.rsqrt(sq_ref[0] * (1.0 / INNER) + 1e-05)
    factor = jnp.broadcast_to(factor, (128, factor.shape[1])).T
    for n in range(gated_ref.shape[1] // 128):
        cols = slice(n * 128, (n + 1) * 128)
        out_ref[:, cols] = (gated_ref[:, cols] * factor * gain_ref[:, cols]).astype(BF16)


def incoming(finals, beside):
    count, mine = lax.axis_size("seq"), lax.axis_index("seq")
    rows, row, side = count // 2, mine // 2, mine % 2
    left, early = side == 0, row < rows // 2
    swap = [(i, i ^ 1) for i in range(count)]
    send = lambda value, route: lax.ppermute(value, "seq", route)
    groups = range(len(finals))
    stages = [[] for _ in groups]
    state, half = finals[0].shape[1] - 8, finals[0].shape[2] // 2
    kept, given, got1, got2 = {}, {}, {}, {}
    for g in groups:
        first, second = finals[g][:, :, :half], finals[g][:, :, half:]
        kept[g] = jnp.where(left, first, second)
        other = jnp.where(left, second, first)
        given[g] = jnp.where(early, other[0], other[1]), jnp.where(early, other[1], other[0])
        stages[g].append(given[g][0])
        got1[g] = send(given[g][0], swap)
    enter = {g: [jnp.zeros((state, half), F32)] * 2 for g in groups}
    low, high, dl, dh = {}, {}, {}, {}
    got, out1, out2 = {}, {}, {}

    def parts(g, d, arrived):
        mine_d = kept[g][d]
        lo, hi = jnp.where(left, mine_d, arrived), jnp.where(left, arrived, mine_d)
        return lo[:state], hi[:state], lo[state : state + 1], hi[state : state + 1]

    def pair(g, d, pieces):
        lo, hi, decay_lo, decay_hi = pieces
        if d == 0:
            return decay_hi * lo + hi, decay_lo * decay_hi
        return decay_lo * hi + lo, decay_lo * decay_hi

    def both(d, pieces, held):
        lo, hi, decay_lo, decay_hi = pieces
        if d == 0:
            return held, decay_lo * held + lo
        return decay_hi * held + hi, held

    def pick(flag, a, b):
        return jax.tree.map(lambda u, v: jnp.where(flag, u, v), a, b)

    token = early_token = beside(stages[0][-1])
    known = {}
    for hop in range(rows - 1):
        back = rows - 1 - hop
        route = [(2 * hop + s, 2 * hop + 2 + s) for s in range(2)]
        route += [(2 * back + s, 2 * back - 2 + s) for s in range(2)]
        for g in groups:
            if hop == 0:
                known[g] = [parts(g, d, got1[g]) for d in range(2)]
            if hop == rows // 2:
                second = [parts(g, d, got2[g] + token) for d in range(2)]
                known[g] = [pick(early, known[g][0], second[0]), pick(early, second[1], known[g][1])]
            (pf, df), (pr, dr) = pair(g, 0, known[g][0]), pair(g, 1, known[g][1])
            payload = jnp.where(row == hop, df * enter[g][0] + pf, dr * enter[g][1] + pr)
            payload = payload + token[:state]
            stages[g].append(payload)
            got[g] = send(payload, route)
        token = beside(stages[0][-1])
        for g in groups:
            if hop == 0:
                later = given[g][1] + (0.0 * got1[g] + early_token)
                got2[g] = send(later, swap)
            enter[g] = [
                jnp.where(row == hop + 1, got[g], enter[g][0]),
                jnp.where(row == back - 1, got[g], enter[g][1]),
            ]
            if hop == max(rows // 2 - 2, 0):
                ends = pick(early, both(0, known[g][0], enter[g][0]), both(1, known[g][1], enter[g][1]))
                out1[g] = (jnp.where(left, ends[0], ends[1]), send(jnp.where(left, ends[1], ends[0]), swap))
    result = []
    for g in groups:
        ends = pick(early, both(1, known[g][1], enter[g][1]), both(0, known[g][0], enter[g][0]))
        payload = jnp.where(left, ends[1], ends[0]) + token[:state]
        stages[g].append(payload)
        out2[g] = (jnp.where(left, ends[0], ends[1]), send(payload, swap))
        whole = []
        for own, came in (out1[g], out2[g]):
            whole.append(
                jnp.concatenate([jnp.where(left, own, came), jnp.where(left, came, own)], axis=1)
            )
        result.append(
            jnp.stack([jnp.where(early, whole[0], whole[1]), jnp.where(early, whole[1], whole[0])])
        )
    return result


def shards(activations, gate_input, bmat, cmat, log_fwd, log_rev, skip, gain):
    length, channels = activations.shape
    heads = log_fwd.shape[0]
    headdim = channels // heads
    width = 2 * headdim
    state = bmat.shape[1]
    blocks = length // BLOCK
    pairs = heads // 2
    mine = pairs // GROUPS
    part = channels // GROUPS
    finals = []
    shared = []
    for g in range(GROUPS):
        done = list(shared)
        *shared, final = pl.pallas_call(
            functools.partial(states_kernel, headdim, bool(done)),
            grid=(mine,),
            in_specs=[
                pl.BlockSpec((length, width), lambda p, g=g: (0, g * mine + p)),
                pl.BlockSpec((length, state), lambda p: (0, 0)),
                pl.BlockSpec((2 * mine, length), lambda p, g=g: (g, 0)),
                pl.BlockSpec((2 * mine, length), lambda p, g=g: (g, 0)),
            ]
            + [ANY] * len(done),
            out_specs=[
                pl.BlockSpec((1, 8, length), lambda p, g=g: (g * mine + p, 0, 0)),
                pl.BlockSpec((1, 8, length), lambda p, g=g: (g * mine + p, 0, 0)),
                pl.BlockSpec((2, blocks, 2 * state, width), lambda p, g=g: (0, 0, 0, g * mine + p)),
                pl.BlockSpec((2, state + 8, width), lambda p: (0, 0, p)),
            ],
            out_shape=[
                pltpu.HBM((pairs, 8, length), F32),
                pltpu.HBM((pairs, 8, length), F32),
                pltpu.HBM((2, blocks, 2 * state, channels), BF16),
                shape(2, state + 8, part),
            ],
            scratch_shapes=[
                pltpu.VMEM((blocks, state, BLOCK), F32),
                pltpu.VMEM((mine, blocks, 8, BLOCK), F32),
            ],
            input_output_aliases={4 + i: i for i in range(len(done))},
            compiler_params=params(16),
            name="states",
        )(*far(activations, bmat, log_fwd, log_rev, *done))
        finals.append(final)
    cum, dev, held = shared
    skip_row = jnp.repeat(skip, headdim)[None]
    within = []
    some = 2
    left = list(range(blocks))

    def piece(dep):
        if not left:
            return jnp.zeros((state + 8, part // 2), F32)
        k = left.pop(0)
        done = list(within)
        within[:], zero = (lambda out: ([out[0]], [out[1]]))(
            pl.pallas_call(
                functools.partial(within_kernel, headdim, bool(done)),
                grid=(pairs // some,),
                in_specs=[
                    pl.BlockSpec((BLOCK, some * width), lambda n: (k, n)),
                    pl.BlockSpec((BLOCK, state), lambda n: (k, 0)),
                    pl.BlockSpec((BLOCK, state), lambda n: (k, 0)),
                    pl.BlockSpec((some, 8, BLOCK), lambda n: (n, 0, k)),
                    pl.BlockSpec((2, 1, 2 * state, some * width), lambda n: (0, k, 0, n)),
                    pl.BlockSpec((1, some * width), lambda n: (0, n)),
                    ANY,
                ]
                + [ANY] * len(done),
                out_specs=[
                    pl.BlockSpec((BLOCK, some * width), lambda n: (k, n)),
                    pl.BlockSpec((state + 8, part // 2), lambda n: (0, 0)),
                ],
                out_shape=[pltpu.HBM((length, channels), F32), shape(state + 8, part // 2)],
                scratch_shapes=[
                    pltpu.VMEM((BLOCK, BLOCK), F32),
                    pltpu.VMEM((some, TILES, 8, BLOCK), F32),
                    pltpu.VMEM((some, 8, BLOCK), F32),
                ],
                input_output_aliases={7: 0} if done else {},
                compiler_params=params(16),
                cost_estimate=pl.CostEstimate(
                    flops=2 * heads * BLOCK * BLOCK * 512,
                    bytes_accessed=6 * BLOCK * channels,
                    transcendentals=heads * BLOCK * 8,
                ),
                name="within",
            )(*far(activations, bmat, cmat, cum, held), skip_row, dep, *far(*done))
        )
        return zero[0]

    enters = incoming(finals, piece)
    while left:
        piece(finals[0])
    gated = []
    squares = 0.0
    for g in range(GROUPS):
        tall = pl.BlockSpec((BLOCK, part), lambda k, g=g: (k, g))
        gated, square = pl.pallas_call(
            functools.partial(carried_kernel, headdim, bool(gated)),
            grid=(blocks,),
            in_specs=[
                tall,
                tall,
                pl.BlockSpec((BLOCK, state), lambda k: (k, 0)),
                pl.BlockSpec((mine, 8, BLOCK), lambda k, g=g: (g, 0, k)),
                pl.BlockSpec((2, state, part), lambda k: (0, 0, 0)),
            ]
            + [ANY] * len(gated),
            out_specs=[tall, pl.BlockSpec((1, 1, BLOCK), lambda k: (k, 0, 0))],
            out_shape=[pltpu.VMEM((length, channels), F32), shape(blocks, 1, BLOCK)],
            scratch_shapes=[
                pltpu.VMEM((2 * state, 2 * part), BF16),
                pltpu.VMEM((16 * mine, 2 * part), BF16),
            ],
            input_output_aliases={5: 0} if gated else {},
            compiler_params=params(24),
            name="carried",
        )(*far(within[0], gate_input, cmat, dev), enters[g], *near(*gated))
        gated = [gated]
        squares = squares + square
    step, size = 1, lax.axis_size("ch")
    while step < size:
        squares = squares + lax.ppermute(squares, "ch", [(i, i ^ step) for i in range(size)])
        step *= 2
    tall = pl.BlockSpec((BLOCK, channels), lambda k: (k, 0))
    return pl.pallas_call(
        norm_kernel,
        grid=(blocks,),
        in_specs=[
            tall,
            pl.BlockSpec((1, 1, BLOCK), lambda k: (k, 0, 0)),
            pl.BlockSpec((1, channels), lambda k: (0, 0)),
        ],
        out_specs=tall,
        out_shape=shape(length, channels, dtype=BF16),
        compiler_params=params(16),
        name="norm",
    )(*near(gated[0]), squares, gain[None])


def solution(mesh):
    return jax.shard_map(
        shards,
        mesh=mesh,
        in_specs=(
            P("seq", "ch"),
            P("seq", "ch"),
            P("seq", None),
            P("seq", None),
            P("ch", "seq"),
            P("ch", "seq"),
            P("ch"),
            P("ch"),
        ),
        out_specs=P("seq", "ch"),
        check_vma=False,
    )
```

time: 342 us -> 77.6 us (0.23)
  matrix products: 126 us -> 0 us
  local copies, waits for them, and re-layouts: 104 us -> 0.16 us
  other arithmetic: 64.7 us -> 1.8 us
  Pallas kernels: 0 us -> 52.4 us
  blocking collectives: 29.3 us -> 0 us
  between operations: 14.3 us -> 0.2 us
  starting transfers between devices: 0.04 us -> 13 us
  waiting for transfers between devices: 0.04 us -> 9.45 us
    dot_general x26 -> x0, matrix products: 126 us -> none  [the longest x8 57.1 us: advance(): jnp.einsum('hij,jhp->ihp', weights, x_block, preferred_element_type=jnp.f...]
    pallas_call x0 -> x7, Pallas kernels: none -> 52.4 us  [the longest x4 29.6 us: piece(): pl.pallas_call(functools.partial(within_kernel, headdim, bool(done)), gri...]
    rev x7 -> x0, local copies, waits for them, and re-layouts: 31.4 us -> none  [the longest x1 13.4 us: shards(): backward = finish(rev_parts, c_flip, rev_in)[::-1]]
    unnamed x30 -> x4, local copies, waits for them, and re-layouts: 25.2 us -> 0.01 us
    another operation x41 -> x1, local copies, waits for them, and re-layouts: 24.4 us -> 0.08 us  [shards(): skip_row = jnp.repeat(skip, headdim)[None]]
    unnamed x1 -> x0, blocking collectives: 23.5 us -> none
    select_n x14 -> x7, other arithmetic: 16.4 us -> 0.8 us  [the longest x2 0.27 us: parts(): jnp.where(left, mine_d, arrived)]
    reshape x9 -> x0, local copies, waits for them, and re-layouts: 13.5 us -> none  [the longest x2 8.49 us: finish(): return (within + carried).reshape(blocks * length, heads, headdim)]
  transfers between devices with their start and end apart: 2 -> 9, of which waited for: 0 -> 4; matrix products, arithmetic and copies ran while one was open for 42% -> 2% of each run, Pallas kernels for 0% -> 38%
where the time goes in v2:
time: 77.6 us; the launch traced here: 77.1 us
  Pallas kernels  52.4 us (68%)
  starting transfers between devices  13 us (17%)
  waiting for transfers between devices  9.45 us (12%)
  other arithmetic  1.8 us (2%)
    pallas_call x4, Pallas kernels, piece(): pl.pallas_call(functools.partial(within_kernel, headdim, bool(done)), gri...  29.6 us
    ppermute x7, starting transfers between devices, incoming(): send = lambda value, route: lax.ppermute(value, 'seq', route)  11.4 us
    pallas_call x1, Pallas kernels, shards(): pl.pallas_call(functools.partial(states_kernel, headdim, bool(done)), gri...  11 us
    pallas_call x1, Pallas kernels, shards(): pl.pallas_call(functools.partial(carried_kernel, headdim, bool(gated)), g...  8.87 us
    ppermute x7, waiting for transfers between devices, incoming(): send = lambda value, route: lax.ppermute(value, 'seq', route)  6.16 us
    ppermute x2, waiting for transfers between devices, shards(): lax.ppermute(squares, 'ch', [(i, i ^ step) for i in range(size)])  3.29 us
    pallas_call x1, Pallas kernels, shards(): pl.pallas_call(norm_kernel, grid=(blocks,), in_specs=[tall, pl.BlockSpec(...  2.94 us
    ppermute x2, starting transfers between devices, shards(): lax.ppermute(squares, 'ch', [(i, i ^ step) for i in range(size)])  1.65 us
  transfers between devices with their start and end apart: 9, of which 4 were waited for; matrix products, arithmetic and copies ran while one was open for 2% of the time, Pallas kernels for 38%

profile of v2, /device:TPU:0, one launch (start us, length us, event | category | flops | bytes accessed | tf_op | source)
XLA Modules:
  0.0 77.1 jit_solution(950974069465010242)
XLA Ops:
  0.0 0.0 copy-start.1
  0.0 11.0 %states.1 = (f32[8,8,2048]{2,1,0:T(8,128)}, f32[8,8,2048]{2,1,0:T(8,128)}, bf16[2,4,256,1024]{3,2,1,0:T(8,128)(2,1)}, f32[2,136,1024]{2,1,0:T(8,128)S(1)}) custom-call(bf16[2048,1024]{1,0:T(8,128)(2,1)} %x_ref.9, bf16[2048,128]{1,0:T(8,128)(2,1)} %b_ref.9, f32[16,2048]{1,0:T(8,128)} %lf_ref.1, f32[16,2048]{1,0:T(8,128)} %lr_ref.1), custom_call_target="tpu_custom_call" | custom-call | tf_op jit(solution)/shard_map/states/pallas_call | solution.py:352
  11.0 0.1 slice_select_fusion
  11.1 3.0 %collective-permute-start = (f32[136,512]{1,0:T(8,128)S(1)}, f32[136,512]{1,0:T(8,128)S(1)}, u32[]{:S(2)}, u32[]{:S(2)}) collective-permute-start(f32[136,512]{1,0:T(8,128)S(1)} %select_bitcast_fusion.dep_ref), channel_id=1, source_target_pairs={{0,4},{4,0},{8,12},{12,8},{16,20},{20,16},{24,28},{28,24},{1,5},{5... | collective-permute-start | bytes 835592 | tf_op jit(solution)/shard_map/ppermute | solution.py:256
  14.1 0.0 copy-done.1
  14.1 0.1 broadcast_in_dim.11
  14.2 0.1 broadcast_in_dim_reshape.3.skip_ref
  14.3 7.4 %within.4 = (f32[2048,1024]{1,0:T(8,128)}, f32[136,512]{1,0:T(8,128)S(1)}) custom-call(bf16[2048,1024]{1,0:T(8,128)(2,1)} %x_ref.9, bf16[2048,128]{1,0:T(8,128)(2,1)} %b_ref.9, bf16[2048,128]{1,0:T(8,128)(2,1)} %c_ref.9, f32[8,8,2048]{2,1,0:T(8,128)} %get-tuple-element.19.cum_ref, bf16[2,4,256,1024]{3,2,1,0:T(8,128)(2,1)} %get-tuple-element.20.st_ref, ...), custom_call_target="tpu_custom_call" | custom-call | flops 4294967296 | bytes 3145728 | tf_op jit(solution)/shard_map/within/pallas_call | solution.py:395
  21.7 0.0 collective-permute-done
  21.7 0.2 fusion.11
  22.0 0.1 slice_add_fusion.2.dep_ref
  22.1 3.5 %collective-permute-start.2 = (f32[128,512]{1,0:T(8,128)S(1)}, f32[128,512]{1,0:T(8,128)S(1)}, u32[]{:S(2)}, u32[]{:S(2)}) collective-permute-start(f32[128,512]{1,0:T(8,128)S(1)} %slice_add_fusion.2.dep_ref), channel_id=1, source_target_pairs={{0,8},{4,12},{24,16},{28,20},{1,9},{5,13},{25,17},{29,21},{2,10},{... | collective-permute-start | bytes 786440 | tf_op jit(solution)/shard_map/ppermute | solution.py:256
  25.6 0.9 %collective-permute-start.1 = (f32[136,512]{1,0:T(8,128)S(1)}, f32[136,512]{1,0:T(8,128)S(1)}, u32[]{:S(2)}, u32[]{:S(2)}) collective-permute-start(f32[136,512]{1,0:T(8,128)S(1)} %get-tuple-element.72), channel_id=1, source_target_pairs={{0,4},{4,0},{8,12},{12,8},{16,20},{20,16},{24,28},{28,24},{1,5},{5... | collective-permute-start | bytes 835592 | tf_op jit(solution)/shard_map/ppermute | solution.py:256
  26.5 7.4 %within.5 = (f32[2048,1024]{1,0:T(8,128)}, f32[136,512]{1,0:T(8,128)S(1)}) custom-call(bf16[2048,1024]{1,0:T(8,128)(2,1)} %x_ref.9, bf16[2048,128]{1,0:T(8,128)(2,1)} %b_ref.9, bf16[2048,128]{1,0:T(8,128)(2,1)} %c_ref.9, f32[8,8,2048]{2,1,0:T(8,128)} %get-tuple-element.19.cum_ref, ...), custom_call_target="tpu_custom_call", output_to_operand_aliasing={{0}: (7, {})} | custom-call | flops 4294967296 | bytes 3145728 | tf_op jit(solution)/shard_map/within/pallas_call | solution.py:395
  33.9 0.0 collective-permute-done.2
  33.9 0.2 broadcast_select_fusion.2
  34.1 1.3 %collective-permute-start.4 = (f32[128,512]{1,0:T(8,128)S(1)}, f32[128,512]{1,0:T(8,128)S(1)}, u32[]{:S(2)}, u32[]{:S(2)}) collective-permute-start(f32[128,512]{1,0:T(8,128)S(1)} %get-tuple-element.33), channel_id=1, source_target_pairs={{0,4},{4,0},{8,12},{12,8},{16,20},{20,16},{24,28},{28,24},{1,5},{5... | collective-permute-start | bytes 786440 | tf_op jit(solution)/shard_map/ppermute | solution.py:256
  35.4 0.7 collective-permute-start.3
  36.1 7.4 %within.6 = (f32[2048,1024]{1,0:T(8,128)}, f32[136,512]{1,0:T(8,128)S(1)}) custom-call(bf16[2048,1024]{1,0:T(8,128)(2,1)} %x_ref.9, bf16[2048,128]{1,0:T(8,128)(2,1)} %b_ref.9, bf16[2048,128]{1,0:T(8,128)(2,1)} %c_ref.9, f32[8,8,2048]{2,1,0:T(8,128)} %get-tuple-element.19.cum_ref, ...), custom_call_target="tpu_custom_call", output_to_operand_aliasing={{0}: (7, {})} | custom-call | flops 4294967296 | bytes 3145728 | tf_op jit(solution)/shard_map/within/pallas_call | solution.py:395
  43.5 0.0 collective-permute-done.1
  43.5 0.1 fusion.9
  43.6 0.1 fusion.12
  43.7 0.0 collective-permute-done.3
  43.7 0.3 fusion.5
  44.0 1.3 %collective-permute-start.5 = (f32[128,512]{1,0:T(8,128)S(1)}, f32[128,512]{1,0:T(8,128)S(1)}, u32[]{:S(2)}, u32[]{:S(2)}) collective-permute-start(f32[128,512]{1,0:T(8,128)S(1)} %get-tuple-element.39.dep_ref), channel_id=1, source_target_pairs={{16,24},{20,28},{8,0},{12,4},{17,25},{21,29},{9,1},{13,5},{18,26},... | collective-permute-start | bytes 786440 | tf_op jit(solution)/shard_map/ppermute | solution.py:256
  45.3 7.4 %within.7 = (f32[2048,1024]{1,0:T(8,128)}, f32[136,512]{1,0:T(8,128)S(1)}) custom-call(bf16[2048,1024]{1,0:T(8,128)(2,1)} %x_ref.9, bf16[2048,128]{1,0:T(8,128)(2,1)} %b_ref.9, bf16[2048,128]{1,0:T(8,128)(2,1)} %c_ref.9, f32[8,8,2048]{2,1,0:T(8,128)} %get-tuple-element.19.cum_ref, ...), custom_call_target="tpu_custom_call", output_to_operand_aliasing={{0}: (7, {})} | custom-call | flops 4294967296 | bytes 3145728 | tf_op jit(solution)/shard_map/within/pallas_call | solution.py:395
  52.7 0.1 collective-permute-done.5
  52.9 0.3 slice_add_fusion
  53.1 0.8 %collective-permute-start.6 = (f32[128,512]{1,0:T(8,128)S(1)}, f32[128,512]{1,0:T(8,128)S(1)}, u32[]{:S(2)}, u32[]{:S(2)}) collective-permute-start(f32[128,512]{1,0:T(8,128)S(1)} %get-tuple-element.36), channel_id=1, source_target_pairs={{0,4},{4,0},{8,12},{12,8},{16,20},{20,16},{24,28},{28,24},{1,5},{5... | collective-permute-start | bytes 786440 | tf_op jit(solution)/shard_map/ppermute | solution.py:256
  53.9 0.0 collective-permute-done.4
  53.9 0.1 select_bitcast_fusion.4
  54.0 6.0 %collective-permute-done.6 = f32[128,512]{1,0:T(8,128)S(1)} collective-permute-done((f32[128,512]{1,0:T(8,128)S(1)}, f32[128,512]{1,0:T(8,128)S(1)}, u32[]{:S(2)}, u32[]{:S(2)}) %collective-permute-start.6) | collective-permute-done | bytes 262176 | tf_op jit(solution)/shard_map/ppermute | solution.py:256
  60.0 0.1 select_bitcast_fusion.2
  60.1 0.1 fusion.1
  60.2 0.1 pad_maximum_fusion.in_ref
  60.3 0.0 copy-start
  60.3 8.9 %carried.1 = (f32[2048,1024]{1,0:T(8,128)S(1)}, f32[4,1,512]{2,1,0:T(1,128)S(1)}) custom-call(f32[2048,1024]{1,0:T(8,128)} %get-tuple-element.28.a_ref, bf16[2048,1024]{1,0:T(8,128)(2,1)} %gate_ref.1, bf16[2048,128]{1,0:T(8,128)(2,1)} %c_ref.9, f32[8,8,2048]{2,1,0:T(8,128)} %get-tuple-element.29.dev_ref, f32[2,128,1024]{2,1,0:T(8,128)S(1)} %pad_maximum_fusion.in_ref), custom_call_target="tpu_custom_call" | custom-call | tf_op jit(solution)/shard_map/carried/pallas_call | solution.py:437
  69.2 0.1 collective-permute-start.7
  69.2 1.2 %collective-permute-done.7 = f32[4,1,512]{2,1,0:T(1,128)S(1)} collective-permute-done((f32[4,1,512]{2,1,0:T(1,128)S(1)}, f32[4,1,512]{2,1,0:T(1,128)S(1)}, u32[]{:S(2)}, u32[]{:S(2)}) %collective-permute-start.7) | collective-permute-done | bytes 8224 | tf_op jit(solution)/shard_map/ppermute | solution.py:462
  70.4 1.6 %collective-permute-start.8 = (f32[4,1,512]{2,1,0:T(1,128)S(1)}, f32[4,1,512]{2,1,0:T(1,128)S(1)}, u32[]{:S(2)}, u32[]{:S(2)}) collective-permute-start(f32[4,1,512]{2,1,0:T(1,128)S(1)} %add.99), channel_id=1, source_target_pairs={{0,2},{1,3},{2,0},{3,1},{4,6},{5,7},{6,4},{7,5},{8,10},{9,11},{10,... | collective-permute-start | bytes 24584 | tf_op jit(solution)/shard_map/ppermute | solution.py:462
  72.0 2.1 %collective-permute-done.8 = f32[4,1,512]{2,1,0:T(1,128)S(1)} collective-permute-done((f32[4,1,512]{2,1,0:T(1,128)S(1)}, f32[4,1,512]{2,1,0:T(1,128)S(1)}, u32[]{:S(2)}, u32[]{:S(2)}) %collective-permute-start.8) | collective-permute-done | bytes 8224 | tf_op jit(solution)/shard_map/ppermute | solution.py:462
  74.1 0.0 copy-done
  74.1 2.9 %norm.1 = bf16[2048,1024]{1,0:T(8,128)(2,1)} custom-call(f32[2048,1024]{1,0:T(8,128)S(1)} %get-tuple-element.31.gated_ref, f32[4,1,512]{2,1,0:T(1,128)S(1)} %add.100.sq_ref, f32[1,1024]{1,0:T(1,128)S(1)} %bitcast.45), custom_call_target="tpu_custom_call" | custom-call | tf_op jit(solution)/shard_map/norm/pallas_call | solution.py:465
  (8 shorter events, 0.1 us)
Async XLA Ops:
  0.0 14.1 %copy-start.1 = (f32[16]{0:T(128)S(1)}, f32[16]{0:T(128)}, u32[]{:S(2)}) copy-start(f32[16]{0:T(128)} %param.14) | copy-start | bytes 196
  11.1 10.6 %collective-permute-start = (f32[136,512]{1,0:T(8,128)S(1)}, f32[136,512]{1,0:T(8,128)S(1)}, u32[]{:S(2)}, u32[]{:S(2)}) collective-permute-start(f32[136,512]{1,0:T(8,128)S(1)} %select_bitcast_fusion.dep_ref), channel_id=1, source_target_pairs={{0,4},{4,0},{8,12},{12,8},{16,20},{20,16},{24,28},{28,24},{1,5},{5... | collective-permute-start | bytes 835592 | tf_op jit(solution)/shard_map/ppermute | solution.py:256
  22.1 11.8 %collective-permute-start.2 = (f32[128,512]{1,0:T(8,128)S(1)}, f32[128,512]{1,0:T(8,128)S(1)}, u32[]{:S(2)}, u32[]{:S(2)}) collective-permute-start(f32[128,512]{1,0:T(8,128)S(1)} %slice_add_fusion.2.dep_ref), channel_id=1, source_target_pairs={{0,8},{4,12},{24,16},{28,20},{1,9},{5,13},{25,17},{29,21},{2,10},{... | collective-permute-start | bytes 786440 | tf_op jit(solution)/shard_map/ppermute | solution.py:256
  25.6 17.8 %collective-permute-start.1 = (f32[136,512]{1,0:T(8,128)S(1)}, f32[136,512]{1,0:T(8,128)S(1)}, u32[]{:S(2)}, u32[]{:S(2)}) collective-permute-start(f32[136,512]{1,0:T(8,128)S(1)} %get-tuple-element.72), channel_id=1, source_target_pairs={{0,4},{4,0},{8,12},{12,8},{16,20},{20,16},{24,28},{28,24},{1,5},{5... | collective-permute-start | bytes 835592 | tf_op jit(solution)/shard_map/ppermute | solution.py:256
  34.1 19.8 %collective-permute-start.4 = (f32[128,512]{1,0:T(8,128)S(1)}, f32[128,512]{1,0:T(8,128)S(1)}, u32[]{:S(2)}, u32[]{:S(2)}) collective-permute-start(f32[128,512]{1,0:T(8,128)S(1)} %get-tuple-element.33), channel_id=1, source_target_pairs={{0,4},{4,0},{8,12},{12,8},{16,20},{20,16},{24,28},{28,24},{1,5},{5... | collective-permute-start | bytes 786440 | tf_op jit(solution)/shard_map/ppermute | solution.py:256
  35.4 8.3 %collective-permute-start.3 = (f32[128,512]{1,0:T(8,128)S(1)}, f32[128,512]{1,0:T(8,128)S(1)}, u32[]{:S(2)}, u32[]{:S(2)}) collective-permute-start(f32[128,512]{1,0:T(8,128)S(1)} %get-tuple-element.61.dep_ref), channel_id=1, source_target_pairs={{8,16},{12,20},{16,8},{20,12},{9,17},{13,21},{17,9},{21,13},{10,18... | collective-permute-start | bytes 786440 | tf_op jit(solution)/shard_map/ppermute | solution.py:256
  44.0 8.8 %collective-permute-start.5 = (f32[128,512]{1,0:T(8,128)S(1)}, f32[128,512]{1,0:T(8,128)S(1)}, u32[]{:S(2)}, u32[]{:S(2)}) collective-permute-start(f32[128,512]{1,0:T(8,128)S(1)} %get-tuple-element.39.dep_ref), channel_id=1, source_target_pairs={{16,24},{20,28},{8,0},{12,4},{17,25},{21,29},{9,1},{13,5},{18,26},... | collective-permute-start | bytes 786440 | tf_op jit(solution)/shard_map/ppermute | solution.py:256
  53.1 6.9 %collective-permute-start.6 = (f32[128,512]{1,0:T(8,128)S(1)}, f32[128,512]{1,0:T(8,128)S(1)}, u32[]{:S(2)}, u32[]{:S(2)}) collective-permute-start(f32[128,512]{1,0:T(8,128)S(1)} %get-tuple-element.36), channel_id=1, source_target_pairs={{0,4},{4,0},{8,12},{12,8},{16,20},{20,16},{24,28},{28,24},{1,5},{5... | collective-permute-start | bytes 786440 | tf_op jit(solution)/shard_map/ppermute | solution.py:256
  60.3 13.9 %copy-start = (f32[1024]{0:T(1024)S(1)}, f32[1024]{0:T(1024)}, u32[]{:S(2)}) copy-start(f32[1024]{0:T(1024)} %param.15) | copy-start | bytes 12292
  69.2 1.2 %collective-permute-start.7 = (f32[4,1,512]{2,1,0:T(1,128)S(1)}, f32[4,1,512]{2,1,0:T(1,128)S(1)}, u32[]{:S(2)}, u32[]{:S(2)}) collective-permute-start(f32[4,1,512]{2,1,0:T(1,128)S(1)} %get-tuple-element.32), channel_id=1, source_target_pairs={{0,1},{1,0},{2,3},{3,2},{4,5},{5,4},{6,7},{7,6},{8,9},{9,8},{10,11... | collective-permute-start | bytes 24584 | tf_op jit(solution)/shard_map/ppermute | solution.py:462
  70.4 3.7 %collective-permute-start.8 = (f32[4,1,512]{2,1,0:T(1,128)S(1)}, f32[4,1,512]{2,1,0:T(1,128)S(1)}, u32[]{:S(2)}, u32[]{:S(2)}) collective-permute-start(f32[4,1,512]{2,1,0:T(1,128)S(1)} %add.99), channel_id=1, source_target_pairs={{0,2},{1,3},{2,0},{3,1},{4,6},{5,7},{6,4},{7,5},{8,10},{9,11},{10,... | collective-permute-start | bytes 24584 | tf_op jit(solution)/shard_map/ppermute | solution.py:462

commit v3 on v2

v3 whole, which is shorter than its diff:
```python
import functools

import jax
import jax.numpy as jnp
from jax import lax
from jax.experimental import pallas as pl
from jax.experimental.pallas import tpu as pltpu
from jax.sharding import PartitionSpec as P

INNER = 4096
BLOCK = 512
TILE = 128
TILES = BLOCK // TILE
GROUPS = 1
PIECES = 5
LOG2E = 1.4426950408889634
F32, BF16 = jnp.float32, jnp.bfloat16
ANY = pl.BlockSpec(memory_space=pl.ANY)


def shape(*dims, dtype=F32):
    return jax.ShapeDtypeStruct(dims, dtype)


def far(*values):
    return [pltpu.with_memory_space_constraint(value, pltpu.HBM) for value in values]


def near(*values):
    return [pltpu.with_memory_space_constraint(value, pltpu.VMEM) for value in values]


def params(mib):
    return pltpu.CompilerParams(
        vmem_limit_bytes=mib * 1024 * 1024, dimension_semantics=("arbitrary",)
    )


def running_sums(log, reverse):
    heads, length = log.shape
    rows = jnp.concatenate(
        [log[:, at : at + BLOCK] for at in range(0, length, BLOCK)], axis=0
    )
    high = rows.astype(BF16)
    rest = rows - high.astype(F32)
    middle = rest.astype(BF16)
    low = (rest - middle.astype(F32)).astype(BF16)
    u = lax.broadcasted_iota(jnp.int32, (BLOCK, BLOCK), 0)
    t = lax.broadcasted_iota(jnp.int32, (BLOCK, BLOCK), 1)
    taken = jnp.where(u >= t if reverse else u <= t, 1.0, 0.0).astype(BF16)
    total = [jnp.dot(part, taken, preferred_element_type=F32) for part in (low, middle, high)]
    return total[0] + total[1] + total[2]


def halves(value):
    high = value.astype(BF16)
    return jnp.concatenate([high, (value - high.astype(F32)).astype(BF16)], axis=0)


def states_kernel(headdim, chained, x_ref, b_ref, lf_ref, lr_ref, *refs):
    cum_ref, before_ref, off_ref, final_ref, bt_ref, sum_ref = refs[3 if chained else 0 :]
    step = pl.program_id(0)
    pairs, blocks = sum_ref.shape[:2]
    state = b_ref.shape[1]

    @pl.when(step == 0)
    def _():
        cf = running_sums(lf_ref[...], False) * LOG2E
        cr = running_sums(lr_ref[...], True) * LOG2E
        for k in range(blocks):
            bt_ref[k] = b_ref[k * BLOCK : (k + 1) * BLOCK].astype(F32).T
            for i in range(pairs):
                h = slice(2 * (k * pairs + i), 2 * (k * pairs + i) + 2)
                sum_ref[i, k, 0:2] = cf[h]
                sum_ref[i, k, 2:4] = cr[h]
                sum_ref[i, k, 4:8] = jnp.zeros((4, BLOCK), F32)

    first = lax.broadcasted_iota(jnp.int32, (1, 2 * headdim), 1) < headdim
    lane = lax.broadcasted_iota(jnp.int32, (state, 2 * headdim), 1)
    forward = lax.broadcasted_iota(jnp.int32, (8, 1), 0) < 2
    for one in range(cum_ref.shape[0]):
        p = step * cum_ref.shape[0] + one
        cols = slice(2 * headdim * one, 2 * headdim * (one + 1))
        fresh, decay = [], []
        for k in range(blocks):
            at = slice(k * BLOCK, (k + 1) * BLOCK)
            cum = sum_ref[p, k]
            last = jnp.where(forward, cum[:, BLOCK - 1 :], cum[:, :1])
            to_end = jnp.exp2(last - cum)
            whole = jnp.exp2(last)
            rows = jnp.concatenate(
                [(bt_ref[k] * to_end[r : r + 1]).astype(BF16) for r in range(4)], axis=0
            )
            both = jnp.dot(rows, x_ref[at, cols], preferred_element_type=F32)
            fresh.append(
                [
                    jnp.where(
                        lane < headdim,
                        both[2 * d * state : (2 * d + 1) * state],
                        both[(2 * d + 1) * state : (2 * d + 2) * state],
                    )
                    for d in range(2)
                ]
            )
            decay.append(
                [
                    jnp.where(first, whole[2 * d : 2 * d + 1], whole[2 * d + 1 : 2 * d + 2])
                    for d in range(2)
                ]
            )
            cum_ref[one, :, at] = cum
        for d in range(2):
            order = range(blocks) if d == 0 else range(blocks - 1, -1, -1)
            held = jnp.zeros_like(fresh[0][0])
            through = jnp.ones_like(decay[0][0])
            for k in order:
                before_ref[k, d, :, cols] = held
                off_ref[k, d : d + 1, cols] = through
                held = held * decay[k][d] + fresh[k][d]
                through = through * decay[k][d]
            final_ref[d, :state, cols] = held
            final_ref[d, state:, cols] = jnp.broadcast_to(through, (8, 2 * headdim))


def within_kernel(headdim, chunks, first_unit, chained, x_ref, b_ref, c_ref, cum_ref, skip_ref, dep_ref, *refs):
    out_ref, zero_ref, score_ref, row_ref, col_ref = refs[1 if chained else 0 :]
    width = 2 * headdim
    pairs = cum_ref.shape[0]
    zero_ref[...] = jnp.zeros_like(zero_ref)

    unit = first_unit + pl.program_id(0)

    @pl.when((pl.program_id(0) == 0) | (lax.rem(unit, chunks) == 0))
    def _():
        scores = lax.dot_general(
            c_ref[...], b_ref[...], (((1,), (1,)), ((), ())), preferred_element_type=F32
        )
        row = lax.broadcasted_iota(jnp.int32, (BLOCK, BLOCK), 0)
        col = lax.broadcasted_iota(jnp.int32, (BLOCK, BLOCK), 1)
        score_ref[...] = jnp.where(row == col, 2.0 * scores, scores)

    first = lax.broadcasted_iota(jnp.int32, (1, width), 1) < headdim
    lower = lax.broadcasted_iota(jnp.int32, (TILE, TILE), 0) >= lax.broadcasted_iota(
        jnp.int32, (TILE, TILE), 1
    )
    forward = lax.broadcasted_iota(jnp.int32, (8, 1), 0) < 2
    none = jnp.zeros((8, 1), F32)
    for p in range(pairs):
        cum = cum_ref[p]
        for i in range(TILES):
            lo = cum[:, i * TILE - 1 : i * TILE] if i else none
            hi = cum[:, (i + 1) * TILE : (i + 1) * TILE + 1] if i < TILES - 1 else none
            base = jnp.where(forward, lo, hi)
            row_ref[p, i] = jnp.exp2(base - cum)
            at = slice(i * TILE, (i + 1) * TILE)
            col_ref[p, :, at] = jnp.exp2(cum[:, at] - base)
        cols = slice(p * width, (p + 1) * width)
        x = x_ref[:, cols]
        parts = []
        for q in range(2):
            done = []
            for i in range(TILES):
                at = slice(i * TILE, (i + 1) * TILE)
                cf, cr = [
                    jnp.broadcast_to(col_ref[p, r : r + 1, at], (TILE, TILE)).T for r in (q, 2 + q)
                ]
                pieces = []
                for j in range(TILES):
                    to = slice(j * TILE, (j + 1) * TILE)
                    rf = row_ref[p, i, q : q + 1, to]
                    rr = row_ref[p, i, 2 + q : 3 + q, to]
                    score = score_ref[at, to]
                    if j < i:
                        weight = (score * rf) * cf
                    elif j > i:
                        weight = (score * rr) * cr
                    else:
                        weight = score * jnp.where(lower, rf * cf, rr * cr)
                    pieces.append(weight.astype(BF16))
                line = jnp.concatenate(pieces, axis=1)
                if i % 2:
                    both = jnp.concatenate([line_before, line], axis=0)
                    done.append(jnp.dot(both, x, preferred_element_type=F32))
                line_before = line
            parts.append(jnp.concatenate(done, axis=0))
        y = jnp.where(first, parts[0], parts[1])
        out_ref[:, cols] = y + skip_ref[:, cols] * x.astype(F32)


def carried_kernel(headdim, chained, a_ref, gate_ref, c_ref, cum_ref, before_ref, off_ref, in_ref, *refs):
    out_ref, sq_ref, hot_ref = refs[1 if chained else 0 :]
    pairs = cum_ref.shape[0]
    width = 2 * headdim

    @pl.when(pl.program_id(0) == 0)
    def _():
        row = lax.broadcasted_iota(jnp.int32, (16 * pairs, 1), 0)
        row = jnp.where(row < 8 * pairs, row, row - 8 * pairs)
        lane = lax.broadcasted_iota(jnp.int32, (1, width), 1)
        for p in range(pairs):
            hot = jnp.where(row == 8 * p + 2 + jnp.where(lane < headdim, 0, 1), 1.0, 0.0)
            hot_ref[:, p * width : (p + 1) * width] = hot.astype(BF16)

    every = jnp.exp2(cum_ref[...].reshape(8 * pairs, BLOCK))
    high = every.astype(BF16).astype(F32)
    every_t = jnp.concatenate([high, every - high], axis=0).T.astype(BF16)
    c = c_ref[...]
    cc = jnp.concatenate([c, c], axis=1)
    squares = [jnp.zeros((TILE, width), F32)] * TILES
    for p in range(pairs):
        cols = slice(p * width, (p + 1) * width)
        decay = every[8 * p : 8 * p + 8]
        if p % 2 == 0:
            scales = jnp.dot(every_t, hot_ref[:, p * width : (p + 2) * width], preferred_element_type=F32)
        held = [
            halves(before_ref[0, d, :, cols] + off_ref[0, d : d + 1, cols] * in_ref[d, :, cols])
            for d in range(2)
        ]
        z = jnp.dot(cc, jnp.concatenate(held, axis=1), preferred_element_type=F32)
        for i in range(TILES):
            at = slice(i * TILE, (i + 1) * TILE)
            rows = [jnp.broadcast_to(decay[r : r + 1, at], (headdim, TILE)) for r in range(2)]
            total = a_ref[at, cols] + jnp.concatenate(rows, axis=0).T * z[at, :width]
            total = total + scales[at, p % 2 * width : (p % 2 + 1) * width] * z[at, width:]
            half = 0.5 * gate_ref[at, cols].astype(F32)
            gated = total * (half + half * jnp.tanh(half))
            out_ref[at, cols] = gated
            squares[i] = squares[i] + gated * gated
    for i in range(TILES):
        sq_ref[0, :, i * TILE : (i + 1) * TILE] = jnp.sum(squares[i].T, axis=0, keepdims=True)


def norm_kernel(gated_ref, sq_ref, gain_ref, out_ref):
    factor = lax.rsqrt(sq_ref[0] * (1.0 / INNER) + 1e-05)
    factor = jnp.broadcast_to(factor, (128, factor.shape[1])).T
    for n in range(gated_ref.shape[1] // 128):
        cols = slice(n * 128, (n + 1) * 128)
        out_ref[:, cols] = (gated_ref[:, cols] * factor * gain_ref[:, cols]).astype(BF16)


def incoming(finals, beside):
    count, mine = lax.axis_size("seq"), lax.axis_index("seq")
    rows, row, side = count // 2, mine // 2, mine % 2
    left, early = side == 0, row < rows // 2
    swap = [(i, i ^ 1) for i in range(count)]
    send = lambda value, route: lax.ppermute(value, "seq", route)
    groups = range(len(finals))
    stages = [[] for _ in groups]
    state, half = finals[0].shape[1] - 8, finals[0].shape[2] // 2
    kept, given, got1, got2 = {}, {}, {}, {}
    for g in groups:
        first, second = finals[g][:, :, :half], finals[g][:, :, half:]
        kept[g] = jnp.where(left, first, second)
        other = jnp.where(left, second, first)
        given[g] = jnp.where(early, other[0], other[1]), jnp.where(early, other[1], other[0])
        stages[g].append(given[g][0])
        got1[g] = send(given[g][0], swap)
    enter = {g: [jnp.zeros((state, half), F32)] * 2 for g in groups}
    low, high, dl, dh = {}, {}, {}, {}
    got, out1, out2 = {}, {}, {}

    def parts(g, d, arrived):
        mine_d = kept[g][d]
        lo, hi = jnp.where(left, mine_d, arrived), jnp.where(left, arrived, mine_d)
        return lo[:state], hi[:state], lo[state : state + 1], hi[state : state + 1]

    def pair(g, d, pieces):
        lo, hi, decay_lo, decay_hi = pieces
        if d == 0:
            return decay_hi * lo + hi, decay_lo * decay_hi
        return decay_lo * hi + lo, decay_lo * decay_hi

    def both(d, pieces, held):
        lo, hi, decay_lo, decay_hi = pieces
        if d == 0:
            return held, decay_lo * held + lo
        return decay_hi * held + hi, held

    def pick(flag, a, b):
        return jax.tree.map(lambda u, v: jnp.where(flag, u, v), a, b)

    token = early_token = beside(stages[0][-1])
    known = {}
    for hop in range(rows - 1):
        back = rows - 1 - hop
        route = [(2 * hop + s, 2 * hop + 2 + s) for s in range(2)]
        route += [(2 * back + s, 2 * back - 2 + s) for s in range(2)]
        for g in groups:
            if hop == 0:
                known[g] = [parts(g, d, got1[g]) for d in range(2)]
            if hop == rows // 2:
                second = [parts(g, d, got2[g] + token) for d in range(2)]
                known[g] = [pick(early, known[g][0], second[0]), pick(early, second[1], known[g][1])]
            (pf, df), (pr, dr) = pair(g, 0, known[g][0]), pair(g, 1, known[g][1])
            payload = jnp.where(row == hop, df * enter[g][0] + pf, dr * enter[g][1] + pr)
            payload = payload + token
            stages[g].append(payload)
            got[g] = send(payload, route)
        token = beside(stages[0][-1])
        for g in groups:
            if hop == 0:
                later = given[g][1] + (0.0 * got1[g] + early_token)
                got2[g] = send(later, swap)
            enter[g] = [
                jnp.where(row == hop + 1, got[g], enter[g][0]),
                jnp.where(row == back - 1, got[g], enter[g][1]),
            ]
            if hop == max(rows // 2 - 2, 0):
                ends = pick(early, both(0, known[g][0], enter[g][0]), both(1, known[g][1], enter[g][1]))
                out1[g] = (jnp.where(left, ends[0], ends[1]), send(jnp.where(left, ends[1], ends[0]), swap))
    result = []
    for g in groups:
        ends = pick(early, both(1, known[g][1], enter[g][1]), both(0, known[g][0], enter[g][0]))
        payload = jnp.where(left, ends[1], ends[0]) + token
        stages[g].append(payload)
        out2[g] = (jnp.where(left, ends[0], ends[1]), send(payload, swap))
    beside(stages[0][-1])
    for g in groups:
        whole = []
        for own, came in (out1[g], out2[g]):
            whole.append(
                jnp.concatenate([jnp.where(left, own, came), jnp.where(left, came, own)], axis=1)
            )
        result.append(
            jnp.stack([jnp.where(early, whole[0], whole[1]), jnp.where(early, whole[1], whole[0])])
        )
    return result


def shards(activations, gate_input, bmat, cmat, log_fwd, log_rev, skip, gain):
    length, channels = activations.shape
    heads = log_fwd.shape[0]
    headdim = channels // heads
    width = 2 * headdim
    state = bmat.shape[1]
    blocks = length // BLOCK
    pairs = heads // 2
    mine = pairs // GROUPS
    part = channels // GROUPS
    many = 2
    finals = []
    shared = []
    for g in range(GROUPS):
        done = list(shared)
        *shared, final = pl.pallas_call(
            functools.partial(states_kernel, headdim, bool(done)),
            grid=(mine // many,),
            in_specs=[
                pl.BlockSpec((length, many * width), lambda n, g=g: (0, g * mine // many + n)),
                pl.BlockSpec((length, state), lambda n: (0, 0)),
                pl.BlockSpec((2 * mine, length), lambda n, g=g: (g, 0)),
                pl.BlockSpec((2 * mine, length), lambda n, g=g: (g, 0)),
            ]
            + [ANY] * len(done),
            out_specs=[
                pl.BlockSpec((many, 8, length), lambda n, g=g: (g * mine // many + n, 0, 0)),
                pl.BlockSpec(
                    (blocks, 2, state, many * width),
                    lambda n, g=g: (0, 0, 0, g * mine // many + n),
                ),
                pl.BlockSpec((blocks, 8, many * width), lambda n, g=g: (0, 0, g * mine // many + n)),
                pl.BlockSpec((2, state + 8, many * width), lambda n: (0, 0, n)),
            ],
            out_shape=[
                pltpu.HBM((pairs, 8, length), F32),
                pltpu.HBM((blocks, 2, state, channels), F32),
                pltpu.HBM((blocks, 8, channels), F32),
                shape(2, state + 8, part),
            ],
            scratch_shapes=[
                pltpu.VMEM((blocks, state, BLOCK), F32),
                pltpu.VMEM((mine, blocks, 8, BLOCK), F32),
            ],
            input_output_aliases={4 + i: i for i in range(len(done))},
            compiler_params=params(24),
            name="states",
        )(*far(activations, bmat, log_fwd, log_rev, *done))
        finals.append(final)
    cum, before, off = shared
    skip_row = jnp.repeat(skip, headdim)[None]
    within = []
    some = 2
    chunks = pairs // some
    units = blocks * chunks
    cuts = [units * i // PIECES for i in range(PIECES + 1)]
    plan = list(zip(cuts[:-1], cuts[1:]))[::-1]

    def piece(dep):
        if not plan:
            return jnp.zeros((1, part // 2), F32)
        start, stop = plan.pop()
        block, chunk = lambda n: (start + n) // chunks, lambda n: lax.rem(start + n, chunks)
        done = list(within)
        within[:1], zero = (lambda out: ([out[0]], out[1]))(
            pl.pallas_call(
                functools.partial(within_kernel, headdim, chunks, start, bool(done)),
                grid=(stop - start,),
                in_specs=[
                    pl.BlockSpec((BLOCK, some * width), lambda n: (block(n), chunk(n))),
                    pl.BlockSpec((BLOCK, state), lambda n: (block(n), 0)),
                    pl.BlockSpec((BLOCK, state), lambda n: (block(n), 0)),
                    pl.BlockSpec((some, 8, BLOCK), lambda n: (chunk(n), 0, block(n))),
                    pl.BlockSpec((1, some * width), lambda n: (0, chunk(n))),
                    ANY,
                ]
                + [ANY] * len(done),
                out_specs=[
                    pl.BlockSpec((BLOCK, some * width), lambda n: (block(n), chunk(n))),
                    pl.BlockSpec((8, part // 2), lambda n: (0, 0)),
                ],
                out_shape=[pltpu.HBM((length, channels), F32), shape(8, part // 2)],
                scratch_shapes=[
                    pltpu.VMEM((BLOCK, BLOCK), F32),
                    pltpu.VMEM((some, TILES, 8, BLOCK), F32),
                    pltpu.VMEM((some, 8, BLOCK), F32),
                ],
                input_output_aliases={6: 0} if done else {},
                compiler_params=params(16),
                cost_estimate=pl.CostEstimate(
                    flops=2 * heads * BLOCK * BLOCK * 512,
                    bytes_accessed=6 * BLOCK * channels,
                    transcendentals=heads * BLOCK * 8,
                ),
                name="within",
            )(*far(activations, bmat, cmat, cum), skip_row, dep, *far(*done))
        )
        return zero[:1]

    enters = incoming(finals, piece)
    while plan:
        piece(finals[0])
    gated = []
    squares = 0.0
    for g in range(GROUPS):
        tall = pl.BlockSpec((BLOCK, part), lambda k, g=g: (k, g))
        gated, square = pl.pallas_call(
            functools.partial(carried_kernel, headdim, bool(gated)),
            grid=(blocks,),
            in_specs=[
                tall,
                tall,
                pl.BlockSpec((BLOCK, state), lambda k: (k, 0)),
                pl.BlockSpec((mine, 8, BLOCK), lambda k, g=g: (g, 0, k)),
                pl.BlockSpec((1, 2, state, part), lambda k, g=g: (k, 0, 0, g)),
                pl.BlockSpec((1, 8, part), lambda k, g=g: (k, 0, g)),
                pl.BlockSpec((2, state, part), lambda k: (0, 0, 0)),
            ]
            + [ANY] * len(gated),
            out_specs=[tall, pl.BlockSpec((1, 1, BLOCK), lambda k: (k, 0, 0))],
            out_shape=[pltpu.VMEM((length, channels), F32), shape(blocks, 1, BLOCK)],
            scratch_shapes=[
                pltpu.VMEM((16 * mine, part), BF16),
            ],
            input_output_aliases={7: 0} if gated else {},
            compiler_params=params(24),
            name="carried",
        )(*far(within[0], gate_input, cmat, cum, before, off), enters[g], *near(*gated))
        gated = [gated]
        squares = squares + square
    step, size = 1, lax.axis_size("ch")
    while step < size:
        squares = squares + lax.ppermute(squares, "ch", [(i, i ^ step) for i in range(size)])
        step *= 2
    tall = pl.BlockSpec((BLOCK, channels), lambda k: (k, 0))
    return pl.pallas_call(
        norm_kernel,
        grid=(blocks,),
        in_specs=[
            tall,
            pl.BlockSpec((1, 1, BLOCK), lambda k: (k, 0, 0)),
            pl.BlockSpec((1, channels), lambda k: (0, 0)),
        ],
        out_specs=tall,
        out_shape=shape(length, channels, dtype=BF16),
        compiler_params=params(16),
        name="norm",
    )(*near(gated[0]), squares, gain[None])


def solution(mesh):
    return jax.shard_map(
        shards,
        mesh=mesh,
        in_specs=(
            P("seq", "ch"),
            P("seq", "ch"),
            P("seq", None),
            P("seq", None),
            P("ch", "seq"),
            P("ch", "seq"),
            P("ch"),
            P("ch"),
        ),
        out_specs=P("seq", "ch"),
        check_vma=False,
    )
```

time: 77.6 us -> 73.8 us (0.951)
  waiting for transfers between devices: 9.45 us -> 5.1 us
  starting transfers between devices: 13 us -> 14 us
  Pallas kernels: 52.4 us -> 51.6 us
    ppermute x7, waiting for transfers between devices: 6.16 us -> 1.81 us  [incoming(): send = lambda value, route: lax.ppermute(value, 'seq', route)]
    pallas_call x1, Pallas kernels: 11 us -> 9.14 us  [shards(): pl.pallas_call(functools.partial(states_kernel, headdim, bool(done)), gri...]
    pallas_call x4 -> x5, Pallas kernels: 29.6 us -> 30.6 us  [piece(): pl.pallas_call(functools.partial(within_kernel, headdim, chunks, start, b...]
    ppermute x7, starting transfers between devices: 11.4 us -> 12.3 us  [incoming(): send = lambda value, route: lax.ppermute(value, 'seq', route)]
  transfers between devices with their start and end apart: 9 -> 9, of which waited for: 4 -> 5; matrix products, arithmetic and copies ran while one was open for 2% -> 2% of each run, Pallas kernels for 38% -> 42%
where the time goes in v3:
time: 73.8 us; the launch traced here: 73.4 us
  Pallas kernels  51.6 us (70%)
  starting transfers between devices  14 us (19%)
  waiting for transfers between devices  5.1 us (7%)
  other arithmetic  1.62 us (2%)
  local copies, waits for them, and re-layouts  0.82 us (1%)
    pallas_call x5, Pallas kernels, piece(): pl.pallas_call(functools.partial(within_kernel, headdim, chunks, start, b...  30.6 us
    ppermute x7, starting transfers between devices, incoming(): send = lambda value, route: lax.ppermute(value, 'seq', route)  12.3 us
    pallas_call x1, Pallas kernels, shards(): pl.pallas_call(functools.partial(states_kernel, headdim, bool(done)), gri...  9.14 us
    pallas_call x1, Pallas kernels, shards(): pl.pallas_call(functools.partial(carried_kernel, headdim, bool(gated)), g...  8.96 us
    ppermute x2, waiting for transfers between devices, shards(): lax.ppermute(squares, 'ch', [(i, i ^ step) for i in range(size)])  3.29 us
    pallas_call x1, Pallas kernels, shards(): pl.pallas_call(norm_kernel, grid=(blocks,), in_specs=[tall, pl.BlockSpec(...  2.94 us
    ppermute x7, waiting for transfers between devices, incoming(): send = lambda value, route: lax.ppermute(value, 'seq', route)  1.81 us
    ppermute x2, starting transfers between devices, shards(): lax.ppermute(squares, 'ch', [(i, i ^ step) for i in range(size)])  1.66 us
  transfers between devices with their start and end apart: 9, of which 5 were waited for; matrix products, arithmetic and copies ran while one was open for 2% of the time, Pallas kernels for 42%

profile of v3, /device:TPU:0, one launch (start us, length us, event | category | flops | bytes accessed | tf_op | source)
XLA Modules:
  0.0 73.4 jit_solution(15688350827177776325)
XLA Ops:
  0.0 9.1 %states.1 = (f32[8,8,2048]{2,1,0:T(8,128)}, f32[4,2,128,1024]{3,2,1,0:T(8,128)}, f32[4,8,1024]{2,1,0:T(8,128)}, f32[2,136,1024]{2,1,0:T(8,128)S(1)}) custom-call(bf16[2048,1024]{1,0:T(8,128)(2,1)} %x_ref.11, bf16[2048,128]{1,0:T(8,128)(2,1)} %b_ref.11, f32[16,2048]{1,0:T(8,128)} %lf_ref.1, f32[16,2048]{1,0:T(8,128)} %lr_ref.1), custom_call_target="tpu_custom_call" | custom-call | tf_op jit(solution)/shard_map/states/pallas_call | solution.py:345
  9.1 0.1 slice_select_fusion
  9.3 3.0 %collective-permute-start = (f32[136,512]{1,0:T(8,128)S(1)}, f32[136,512]{1,0:T(8,128)S(1)}, u32[]{:S(2)}, u32[]{:S(2)}) collective-permute-start(f32[136,512]{1,0:T(8,128)S(1)} %select_bitcast_fusion.dep_ref), channel_id=1, source_target_pairs={{0,4},{4,0},{8,12},{12,8},{16,20},{20,16},{24,28},{28,24},{1,5},{5... | collective-permute-start | bytes 835592 | tf_op jit(solution)/shard_map/ppermute | solution.py:246
  12.3 0.7 broadcast_in_dim.11
  13.0 0.1 broadcast_in_dim_reshape.3.skip_ref
  13.1 5.7 %within.5 = (f32[2048,1024]{1,0:T(8,128)}, f32[8,512]{1,0:T(8,128)S(1)}) custom-call(bf16[2048,1024]{1,0:T(8,128)(2,1)} %x_ref.11, bf16[2048,128]{1,0:T(8,128)(2,1)} %b_ref.11, bf16[2048,128]{1,0:T(8,128)(2,1)} %c_ref.11, f32[8,8,2048]{2,1,0:T(8,128)} %get-tuple-element.20.cum_ref, f32[1,1024]{1,0:T(1,128)S(1)} %broadcast_in_dim_reshape.3.skip_ref, ...), custom_call_target="tpu_custom_call" | custom-call | flops 4294967296 | bytes 3145728 | tf_op jit(solution)/shard_map/within/pallas_call | solution.py:395
  18.9 0.1 collective-permute-done
  19.0 0.2 fusion.11
  19.2 0.1 select_add_fusion.2.dep_ref
  19.3 3.7 %collective-permute-start.2 = (f32[128,512]{1,0:T(8,128)S(1)}, f32[128,512]{1,0:T(8,128)S(1)}, u32[]{:S(2)}, u32[]{:S(2)}) collective-permute-start(f32[128,512]{1,0:T(8,128)S(1)} %select_add_fusion.2.dep_ref), channel_id=1, source_target_pairs={{0,8},{4,12},{24,16},{28,20},{1,9},{5,13},{25,17},{29,21},{2,10},{... | collective-permute-start | bytes 786440 | tf_op jit(solution)/shard_map/ppermute | solution.py:246
  23.1 6.0 %within.6 = (f32[2048,1024]{1,0:T(8,128)}, f32[8,512]{1,0:T(8,128)S(1)}) custom-call(bf16[2048,1024]{1,0:T(8,128)(2,1)} %x_ref.11, bf16[2048,128]{1,0:T(8,128)(2,1)} %b_ref.11, bf16[2048,128]{1,0:T(8,128)(2,1)} %c_ref.11, f32[8,8,2048]{2,1,0:T(8,128)} %get-tuple-element.20.cum_ref, ...), custom_call_target="tpu_custom_call", output_to_operand_aliasing={{0}: (6, {})} | custom-call | flops 4294967296 | bytes 3145728 | tf_op jit(solution)/shard_map/within/pallas_call | solution.py:395
  29.1 1.5 %collective-permute-start.1 = (f32[136,512]{1,0:T(8,128)S(1)}, f32[136,512]{1,0:T(8,128)S(1)}, u32[]{:S(2)}, u32[]{:S(2)}) collective-permute-start(f32[136,512]{1,0:T(8,128)S(1)} %get-tuple-element.73), channel_id=1, source_target_pairs={{0,4},{4,0},{8,12},{12,8},{16,20},{20,16},{24,28},{28,24},{1,5},{5... | collective-permute-start | bytes 835592 | tf_op jit(solution)/shard_map/ppermute | solution.py:246
  30.6 0.0 collective-permute-done.2
  30.6 0.2 broadcast_select_fusion.3
  30.8 0.6 collective-permute-start.5
  31.4 0.7 collective-permute-start.3
  32.0 6.1 %within.7 = (f32[2048,1024]{1,0:T(8,128)}, f32[8,512]{1,0:T(8,128)S(1)}) custom-call(bf16[2048,1024]{1,0:T(8,128)(2,1)} %x_ref.11, bf16[2048,128]{1,0:T(8,128)(2,1)} %b_ref.11, bf16[2048,128]{1,0:T(8,128)(2,1)} %c_ref.11, f32[8,8,2048]{2,1,0:T(8,128)} %get-tuple-element.20.cum_ref, ...), custom_call_target="tpu_custom_call", output_to_operand_aliasing={{0}: (6, {})} | custom-call | flops 4294967296 | bytes 3145728 | tf_op jit(solution)/shard_map/within/pallas_call | solution.py:395
  38.1 0.5 collective-permute-done.1
  38.7 0.1 fusion.9
  38.9 0.0 collective-permute-done.3
  38.9 0.3 fusion.5
  39.2 1.5 %collective-permute-start.4 = (f32[128,512]{1,0:T(8,128)S(1)}, f32[128,512]{1,0:T(8,128)S(1)}, u32[]{:S(2)}, u32[]{:S(2)}) collective-permute-start(f32[128,512]{1,0:T(8,128)S(1)} %get-tuple-element.41.dep_ref), channel_id=1, source_target_pairs={{16,24},{20,28},{8,0},{12,4},{17,25},{21,29},{9,1},{13,5},{18,26},... | collective-permute-start | bytes 786440 | tf_op jit(solution)/shard_map/ppermute | solution.py:246
  40.7 5.8 %within.8 = (f32[2048,1024]{1,0:T(8,128)}, f32[8,512]{1,0:T(8,128)S(1)}) custom-call(bf16[2048,1024]{1,0:T(8,128)(2,1)} %x_ref.11, bf16[2048,128]{1,0:T(8,128)(2,1)} %b_ref.11, bf16[2048,128]{1,0:T(8,128)(2,1)} %c_ref.11, f32[8,8,2048]{2,1,0:T(8,128)} %get-tuple-element.20.cum_ref, ...), custom_call_target="tpu_custom_call", output_to_operand_aliasing={{0}: (6, {})} | custom-call | flops 4294967296 | bytes 3145728 | tf_op jit(solution)/shard_map/within/pallas_call | solution.py:395
  46.4 0.0 collective-permute-done.5
  46.4 0.1 select_bitcast_fusion.4
  46.5 1.1 %collective-permute-done.4 = f32[128,512]{1,0:T(8,128)S(1)} collective-permute-done((f32[128,512]{1,0:T(8,128)S(1)}, f32[128,512]{1,0:T(8,128)S(1)}, u32[]{:S(2)}, u32[]{:S(2)}) %collective-permute-start.4) | collective-permute-done | bytes 262176 | tf_op jit(solution)/shard_map/ppermute | solution.py:246
  47.7 0.2 select_add_fusion
  47.9 1.4 %collective-permute-start.6 = (f32[128,512]{1,0:T(8,128)S(1)}, f32[128,512]{1,0:T(8,128)S(1)}, u32[]{:S(2)}, u32[]{:S(2)}) collective-permute-start(f32[128,512]{1,0:T(8,128)S(1)} %get-tuple-element.38.dep_ref), channel_id=1, source_target_pairs={{0,4},{4,0},{8,12},{12,8},{16,20},{20,16},{24,28},{28,24},{1,5},{5... | collective-permute-start | bytes 786440 | tf_op jit(solution)/shard_map/ppermute | solution.py:246
  49.2 7.0 %within.9 = (f32[2048,1024]{1,0:T(8,128)}, f32[8,512]{1,0:T(8,128)}) custom-call(bf16[2048,1024]{1,0:T(8,128)(2,1)} %x_ref.11, bf16[2048,128]{1,0:T(8,128)(2,1)} %b_ref.11, bf16[2048,128]{1,0:T(8,128)(2,1)} %c_ref.11, f32[8,8,2048]{2,1,0:T(8,128)} %get-tuple-element.20.cum_ref, ...), custom_call_target="tpu_custom_call", output_to_operand_aliasing={{0}: (6, {})} | custom-call | flops 4294967296 | bytes 3145728 | tf_op jit(solution)/shard_map/within/pallas_call | solution.py:395
  56.2 0.0 collective-permute-done.6
  56.2 0.1 select_bitcast_fusion.2
  56.3 0.1 fusion.1
  56.4 0.1 pad_maximum_fusion.in_ref
  56.5 0.0 copy-start
  56.5 9.0 %carried.1 = (f32[2048,1024]{1,0:T(8,128)S(1)}, f32[4,1,512]{2,1,0:T(1,128)S(1)}) custom-call(f32[2048,1024]{1,0:T(8,128)} %get-tuple-element.30.a_ref, bf16[2048,1024]{1,0:T(8,128)(2,1)} %gate_ref.1, bf16[2048,128]{1,0:T(8,128)(2,1)} %c_ref.11, f32[8,8,2048]{2,1,0:T(8,128)} %get-tuple-element.20.cum_ref, f32[4,2,128,1024]{3,2,1,0:T(8,128)} %get-tuple-element.31.before_ref, ...), custom_call_target="tpu_custom_call" | custom-call | tf_op jit(solution)/shard_map/carried/pallas_call | solution.py:436
  65.4 0.1 collective-permute-start.7
  65.5 1.2 %collective-permute-done.7 = f32[4,1,512]{2,1,0:T(1,128)S(1)} collective-permute-done((f32[4,1,512]{2,1,0:T(1,128)S(1)}, f32[4,1,512]{2,1,0:T(1,128)S(1)}, u32[]{:S(2)}, u32[]{:S(2)}) %collective-permute-start.7) | collective-permute-done | bytes 8224 | tf_op jit(solution)/shard_map/ppermute | solution.py:462
  66.7 1.6 %collective-permute-start.8 = (f32[4,1,512]{2,1,0:T(1,128)S(1)}, f32[4,1,512]{2,1,0:T(1,128)S(1)}, u32[]{:S(2)}, u32[]{:S(2)}) collective-permute-start(f32[4,1,512]{2,1,0:T(1,128)S(1)} %add.150), channel_id=1, source_target_pairs={{0,2},{1,3},{2,0},{3,1},{4,6},{5,7},{6,4},{7,5},{8,10},{9,11},{10,... | collective-permute-start | bytes 24584 | tf_op jit(solution)/shard_map/ppermute | solution.py:462
  68.3 2.1 %collective-permute-done.8 = f32[4,1,512]{2,1,0:T(1,128)S(1)} collective-permute-done((f32[4,1,512]{2,1,0:T(1,128)S(1)}, f32[4,1,512]{2,1,0:T(1,128)S(1)}, u32[]{:S(2)}, u32[]{:S(2)}) %collective-permute-start.8) | collective-permute-done | bytes 8224 | tf_op jit(solution)/shard_map/ppermute | solution.py:462
  70.4 0.0 copy-done
  70.4 2.9 %norm.1 = bf16[2048,1024]{1,0:T(8,128)(2,1)} custom-call(f32[2048,1024]{1,0:T(8,128)S(1)} %get-tuple-element.33.gated_ref, f32[4,1,512]{2,1,0:T(1,128)S(1)} %add.151.sq_ref, f32[1,1024]{1,0:T(1,128)S(1)} %bitcast.49), custom_call_target="tpu_custom_call" | custom-call | tf_op jit(solution)/shard_map/norm/pallas_call | solution.py:465
  (12 shorter events, 0.1 us)
Async XLA Ops:
  9.3 9.7 %collective-permute-start = (f32[136,512]{1,0:T(8,128)S(1)}, f32[136,512]{1,0:T(8,128)S(1)}, u32[]{:S(2)}, u32[]{:S(2)}) collective-permute-start(f32[136,512]{1,0:T(8,128)S(1)} %select_bitcast_fusion.dep_ref), channel_id=1, source_target_pairs={{0,4},{4,0},{8,12},{12,8},{16,20},{20,16},{24,28},{28,24},{1,5},{5... | collective-permute-start | bytes 835592 | tf_op jit(solution)/shard_map/ppermute | solution.py:246
  19.3 11.3 %collective-permute-start.2 = (f32[128,512]{1,0:T(8,128)S(1)}, f32[128,512]{1,0:T(8,128)S(1)}, u32[]{:S(2)}, u32[]{:S(2)}) collective-permute-start(f32[128,512]{1,0:T(8,128)S(1)} %select_add_fusion.2.dep_ref), channel_id=1, source_target_pairs={{0,8},{4,12},{24,16},{28,20},{1,9},{5,13},{25,17},{29,21},{2,10},{... | collective-permute-start | bytes 786440 | tf_op jit(solution)/shard_map/ppermute | solution.py:246
  29.1 9.6 %collective-permute-start.1 = (f32[136,512]{1,0:T(8,128)S(1)}, f32[136,512]{1,0:T(8,128)S(1)}, u32[]{:S(2)}, u32[]{:S(2)}) collective-permute-start(f32[136,512]{1,0:T(8,128)S(1)} %get-tuple-element.73), channel_id=1, source_target_pairs={{0,4},{4,0},{8,12},{12,8},{16,20},{20,16},{24,28},{28,24},{1,5},{5... | collective-permute-start | bytes 835592 | tf_op jit(solution)/shard_map/ppermute | solution.py:246
  30.8 15.7 %collective-permute-start.5 = (f32[128,512]{1,0:T(8,128)S(1)}, f32[128,512]{1,0:T(8,128)S(1)}, u32[]{:S(2)}, u32[]{:S(2)}) collective-permute-start(f32[128,512]{1,0:T(8,128)S(1)} %get-tuple-element.35), channel_id=1, source_target_pairs={{0,4},{4,0},{8,12},{12,8},{16,20},{20,16},{24,28},{28,24},{1,5},{5... | collective-permute-start | bytes 786440 | tf_op jit(solution)/shard_map/ppermute | solution.py:246
  31.4 7.5 %collective-permute-start.3 = (f32[128,512]{1,0:T(8,128)S(1)}, f32[128,512]{1,0:T(8,128)S(1)}, u32[]{:S(2)}, u32[]{:S(2)}) collective-permute-start(f32[128,512]{1,0:T(8,128)S(1)} %get-tuple-element.62.dep_ref), channel_id=1, source_target_pairs={{8,16},{12,20},{16,8},{20,12},{9,17},{13,21},{17,9},{21,13},{10,18... | collective-permute-start | bytes 786440 | tf_op jit(solution)/shard_map/ppermute | solution.py:246
  39.2 8.5 %collective-permute-start.4 = (f32[128,512]{1,0:T(8,128)S(1)}, f32[128,512]{1,0:T(8,128)S(1)}, u32[]{:S(2)}, u32[]{:S(2)}) collective-permute-start(f32[128,512]{1,0:T(8,128)S(1)} %get-tuple-element.41.dep_ref), channel_id=1, source_target_pairs={{16,24},{20,28},{8,0},{12,4},{17,25},{21,29},{9,1},{13,5},{18,26},... | collective-permute-start | bytes 786440 | tf_op jit(solution)/shard_map/ppermute | solution.py:246
  47.9 8.3 %collective-permute-start.6 = (f32[128,512]{1,0:T(8,128)S(1)}, f32[128,512]{1,0:T(8,128)S(1)}, u32[]{:S(2)}, u32[]{:S(2)}) collective-permute-start(f32[128,512]{1,0:T(8,128)S(1)} %get-tuple-element.38.dep_ref), channel_id=1, source_target_pairs={{0,4},{4,0},{8,12},{12,8},{16,20},{20,16},{24,28},{28,24},{1,5},{5... | collective-permute-start | bytes 786440 | tf_op jit(solution)/shard_map/ppermute | solution.py:246
  56.5 14.0 %copy-start = (f32[1024]{0:T(1024)S(1)}, f32[1024]{0:T(1024)}, u32[]{:S(2)}) copy-start(f32[1024]{0:T(1024)} %param.15) | copy-start | bytes 12292
  65.4 1.2 %collective-permute-start.7 = (f32[4,1,512]{2,1,0:T(1,128)S(1)}, f32[4,1,512]{2,1,0:T(1,128)S(1)}, u32[]{:S(2)}, u32[]{:S(2)}) collective-permute-start(f32[4,1,512]{2,1,0:T(1,128)S(1)} %get-tuple-element.34), channel_id=1, source_target_pairs={{0,1},{1,0},{2,3},{3,2},{4,5},{5,4},{6,7},{7,6},{8,9},{9,8},{10,11... | collective-permute-start | bytes 24584 | tf_op jit(solution)/shard_map/ppermute | solution.py:462
  66.7 3.7 %collective-permute-start.8 = (f32[4,1,512]{2,1,0:T(1,128)S(1)}, f32[4,1,512]{2,1,0:T(1,128)S(1)}, u32[]{:S(2)}, u32[]{:S(2)}) collective-permute-start(f32[4,1,512]{2,1,0:T(1,128)S(1)} %add.150), channel_id=1, source_target_pairs={{0,2},{1,3},{2,0},{3,1},{4,6},{5,7},{6,4},{7,5},{8,10},{9,11},{10,... | collective-permute-start | bytes 24584 | tf_op jit(solution)/shard_map/ppermute | solution.py:462

commit v4 on v3

--- a/solution.py
+++ b/solution.py
@@ -12,10 +12,11 @@
 TILE = 128
 TILES = BLOCK // TILE
 GROUPS = 1
-PIECES = 5
+SHARES = (4, 8, 11, 13, 16)
 LOG2E = 1.4426950408889634
 F32, BF16 = jnp.float32, jnp.bfloat16
 ANY = pl.BlockSpec(memory_space=pl.ANY)
+WHOLE = pl.BlockSpec(memory_space=pltpu.VMEM)
 
 
 def shape(*dims, dtype=F32):
@@ -88,16 +89,19 @@
             last = jnp.where(forward, cum[:, BLOCK - 1 :], cum[:, :1])
             to_end = jnp.exp2(last - cum)
             whole = jnp.exp2(last)
-            rows = jnp.concatenate(
-                [(bt_ref[k] * to_end[r : r + 1]).astype(BF16) for r in range(4)], axis=0
-            )
-            both = jnp.dot(rows, x_ref[at, cols], preferred_element_type=F32)
+            x = x_ref[at, cols]
+            both = []
+            for q in range(2):
+                rows = [(bt_ref[k] * to_end[r : r + 1]).astype(BF16) for r in (q, 2 + q)]
+                both.append(
+                    jnp.dot(jnp.concatenate(rows, axis=0), x, preferred_element_type=F32)
+                )
             fresh.append(
                 [
                     jnp.where(
                         lane < headdim,
-                        both[2 * d * state : (2 * d + 1) * state],
-                        both[(2 * d + 1) * state : (2 * d + 2) * state],
+                        both[0][d * state : (d + 1) * state],
+                        both[1][d * state : (d + 1) * state],
                     )
                     for d in range(2)
                 ]
@@ -187,55 +191,104 @@
         out_ref[:, cols] = y + skip_ref[:, cols] * x.astype(F32)
 
 
-def carried_kernel(headdim, chained, a_ref, gate_ref, c_ref, cum_ref, before_ref, off_ref, in_ref, *refs):
-    out_ref, sq_ref, hot_ref = refs[1 if chained else 0 :]
-    pairs = cum_ref.shape[0]
+def fetch(source, target, sem):
+    copy = pltpu.make_async_copy(source, target, sem)
+    copy.start()
+    return copy
+
+
+def carried_kernel(headdim, a_hbm, gate_hbm, c_hbm, cum_hbm, before_hbm, off_hbm, in_ref, out_ref, sq_ref, *refs):
+    a_buf, gate_buf, c_buf, cum_buf, before_buf, off_buf, hot_ref, sems = refs
+    blocks, pairs = a_buf.shape[0], cum_buf.shape[1]
     width = 2 * headdim
 
-    @pl.when(pl.program_id(0) == 0)
-    def _():
-        row = lax.broadcasted_iota(jnp.int32, (16 * pairs, 1), 0)
-        row = jnp.where(row < 8 * pairs, row, row - 8 * pairs)
-        lane = lax.broadcasted_iota(jnp.int32, (1, width), 1)
+    def copies(k):
+        at = pl.ds(pl.multiple_of(k * BLOCK, BLOCK), BLOCK)
+        pieces = [
+            (before_hbm.at[k], before_buf.at[k]),
+            (off_hbm.at[k], off_buf.at[k]),
+            (c_hbm.at[at], c_buf.at[k]),
+            (cum_hbm.at[:, :, at], cum_buf.at[k]),
+            (gate_hbm.at[at], gate_buf.at[k]),
+            (a_hbm.at[at], a_buf.at[k]),
+        ]
+        return [pltpu.make_async_copy(f, t, sems.at[n, k]) for n, (f, t) in enumerate(pieces)]
+
+    for k in range(blocks):
+        for copy in copies(k):
+            copy.start()
+    row = lax.broadcasted_iota(jnp.int32, (16 * pairs, 1), 0)
+    row = jnp.where(row < 8 * pairs, row, row - 8 * pairs)
+    lane = lax.broadcasted_iota(jnp.int32, (1, width), 1)
+    for p in range(pairs):
+        hot = jnp.where(row == 8 * p + 2 + jnp.where(lane < headdim, 0, 1), 1.0, 0.0)
+        hot_ref[:, p * width : (p + 1) * width] = hot.astype(BF16)
+
+    @pl.loop(0, blocks)
+    def _(k):
+        for copy in copies(k):
+            copy.wait()
+        every = jnp.exp2(cum_buf[k].reshape(8 * pairs, BLOCK))
+        high = every.astype(BF16).astype(F32)
+        every_t = jnp.concatenate([high, every - high], axis=0).T.astype(BF16)
+        c = c_buf[k]
+        cc = jnp.concatenate([c, c], axis=1)
+        squares = [jnp.zeros((TILE, width), F32)] * TILES
+        scales = [None, None]
         for p in range(pairs):
-            hot = jnp.where(row == 8 * p + 2 + jnp.where(lane < headdim, 0, 1), 1.0, 0.0)
-            hot_ref[:, p * width : (p + 1) * width] = hot.astype(BF16)
-
-    every = jnp.exp2(cum_ref[...].reshape(8 * pairs, BLOCK))
-    high = every.astype(BF16).astype(F32)
-    every_t = jnp.concatenate([high, every - high], axis=0).T.astype(BF16)
-    c = c_ref[...]
-    cc = jnp.concatenate([c, c], axis=1)
-    squares = [jnp.zeros((TILE, width), F32)] * TILES
-    for p in range(pairs):
-        cols = slice(p * width, (p + 1) * width)
-        decay = every[8 * p : 8 * p + 8]
-        if p % 2 == 0:
-            scales = jnp.dot(every_t, hot_ref[:, p * width : (p + 2) * width], preferred_element_type=F32)
-        held = [
-            halves(before_ref[0, d, :, cols] + off_ref[0, d : d + 1, cols] * in_ref[d, :, cols])
-            for d in range(2)
-        ]
-        z = jnp.dot(cc, jnp.concatenate(held, axis=1), preferred_element_type=F32)
+            cols = slice(p * width, (p + 1) * width)
+            decay = every[8 * p : 8 * p + 8]
+            held = [
+                halves(before_buf[k, d, :, cols] + off_buf[k, d : d + 1, cols] * in_ref[d, :, cols])
+                for d in range(2)
+            ]
+            held = jnp.concatenate(held, axis=1)
+            for part in range(2):
+                some = slice(part * BLOCK // 2, (part + 1) * BLOCK // 2)
+                if p % 2 == 0:
+                    scales[part] = jnp.dot(
+                        every_t[some],
+                        hot_ref[:, p * width : (p + 2) * width],
+                        preferred_element_type=F32,
+                    )
+                z = jnp.dot(cc[some], held, preferred_element_type=F32)
+                for j in range(TILES // 2):
+                    i = part * TILES // 2 + j
+                    at = slice(i * TILE, (i + 1) * TILE)
+                    to = slice(j * TILE, (j + 1) * TILE)
+                    rows = [jnp.broadcast_to(decay[r : r + 1, at], (headdim, TILE)) for r in range(2)]
+                    total = a_buf[k, at, cols] + jnp.concatenate(rows, axis=0).T * z[to, :width]
+                    other = scales[part][to, p % 2 * width : (p % 2 + 1) * width]
+                    total = total + other * z[to, width:]
+                    half = 0.5 * gate_buf[k, at, cols].astype(F32)
+                    gated = total * (half + half * jnp.tanh(half))
+                    out_ref[pl.ds(pl.multiple_of(k * BLOCK + i * TILE, TILE), TILE), cols] = gated
+                    squares[i] = squares[i] + gated * gated
         for i in range(TILES):
-            at = slice(i * TILE, (i + 1) * TILE)
-            rows = [jnp.broadcast_to(decay[r : r + 1, at], (headdim, TILE)) for r in range(2)]
-            total = a_ref[at, cols] + jnp.concatenate(rows, axis=0).T * z[at, :width]
-            total = total + scales[at, p % 2 * width : (p % 2 + 1) * width] * z[at, width:]
-            half = 0.5 * gate_ref[at, cols].astype(F32)
-            gated = total * (half + half * jnp.tanh(half))
-            out_ref[at, cols] = gated
-            squares[i] = squares[i] + gated * gated
-    for i in range(TILES):
-        sq_ref[0, :, i * TILE : (i + 1) * TILE] = jnp.sum(squares[i].T, axis=0, keepdims=True)
-
-
-def norm_kernel(gated_ref, sq_ref, gain_ref, out_ref):
-    factor = lax.rsqrt(sq_ref[0] * (1.0 / INNER) + 1e-05)
-    factor = jnp.broadcast_to(factor, (128, factor.shape[1])).T
-    for n in range(gated_ref.shape[1] // 128):
-        cols = slice(n * 128, (n + 1) * 128)
-        out_ref[:, cols] = (gated_ref[:, cols] * factor * gain_ref[:, cols]).astype(BF16)
+            sq_ref[k, :, i * TILE : (i + 1) * TILE] = jnp.sum(squares[i].T, axis=0, keepdims=True)
+
+
+def norm_kernel(gated_ref, sq_ref, gain_hbm, out_hbm, out_buf, gain_buf, sems, gain_sem):
+    blocks = out_buf.shape[0]
+    gain = fetch(gain_hbm, gain_buf, gain_sem)
+    copy = lambda k: pltpu.make_async_copy(
+        out_buf.at[k], out_hbm.at[pl.ds(pl.multiple_of(k * BLOCK, BLOCK), BLOCK)], sems.at[k]
+    )
+    gain.wait()
+
+    @pl.loop(0, blocks)
+    def _(k):
+        factor = lax.rsqrt(sq_ref[k] * (1.0 / INNER) + 1e-05)
+        factor = jnp.broadcast_to(factor, (128, factor.shape[1])).T
+        rows = pl.ds(pl.multiple_of(k * BLOCK, BLOCK), BLOCK)
+        for n in range(gated_ref.shape[1] // 128):
+            cols = slice(n * 128, (n + 1) * 128)
+            out_buf[k, :, cols] = (gated_ref[rows, cols] * factor * gain_buf[:, cols]).astype(BF16)
+        copy(k).start()
+
+    @pl.loop(0, blocks)
+    def _(k):
+        copy(k).wait()
 
 
 def incoming(finals, beside):
@@ -382,7 +435,7 @@
     some = 2
     chunks = pairs // some
     units = blocks * chunks
-    cuts = [units * i // PIECES for i in range(PIECES + 1)]
+    cuts = [0] + [units * share // SHARES[-1] for share in SHARES]
     plan = list(zip(cuts[:-1], cuts[1:]))[::-1]
 
     def piece(dep):
@@ -429,52 +482,42 @@
     enters = incoming(finals, piece)
     while plan:
         piece(finals[0])
-    gated = []
-    squares = 0.0
-    for g in range(GROUPS):
-        tall = pl.BlockSpec((BLOCK, part), lambda k, g=g: (k, g))
-        gated, square = pl.pallas_call(
-            functools.partial(carried_kernel, headdim, bool(gated)),
-            grid=(blocks,),
-            in_specs=[
-                tall,
-                tall,
-                pl.BlockSpec((BLOCK, state), lambda k: (k, 0)),
-                pl.BlockSpec((mine, 8, BLOCK), lambda k, g=g: (g, 0, k)),
-                pl.BlockSpec((1, 2, state, part), lambda k, g=g: (k, 0, 0, g)),
-                pl.BlockSpec((1, 8, part), lambda k, g=g: (k, 0, g)),
-                pl.BlockSpec((2, state, part), lambda k: (0, 0, 0)),
-            ]
-            + [ANY] * len(gated),
-            out_specs=[tall, pl.BlockSpec((1, 1, BLOCK), lambda k: (k, 0, 0))],
-            out_shape=[pltpu.VMEM((length, channels), F32), shape(blocks, 1, BLOCK)],
-            scratch_shapes=[
-                pltpu.VMEM((16 * mine, part), BF16),
-            ],
-            input_output_aliases={7: 0} if gated else {},
-            compiler_params=params(24),
-            name="carried",
-        )(*far(within[0], gate_input, cmat, cum, before, off), enters[g], *near(*gated))
-        gated = [gated]
-        squares = squares + square
+    gated, squares = pl.pallas_call(
+        functools.partial(carried_kernel, headdim),
+        in_specs=[ANY] * 6 + [WHOLE],
+        out_specs=[WHOLE, WHOLE],
+        out_shape=[pltpu.VMEM((length, channels), F32), shape(blocks, 1, BLOCK)],
+        scratch_shapes=[
+            pltpu.VMEM((blocks, BLOCK, channels), F32),
+            pltpu.VMEM((blocks, BLOCK, channels), BF16),
+            pltpu.VMEM((blocks, BLOCK, state), BF16),
+            pltpu.VMEM((blocks, pairs, 8, BLOCK), F32),
+            pltpu.VMEM((blocks, 2, state, channels), F32),
+            pltpu.VMEM((blocks, 8, channels), F32),
+            pltpu.VMEM((16 * pairs, channels), BF16),
+            pltpu.SemaphoreType.DMA((6, blocks)),
+        ],
+        compiler_params=pltpu.CompilerParams(vmem_limit_bytes=40 * 1024 * 1024),
+        name="carried",
+    )(*far(within[0], gate_input, cmat, cum, before, off), enters[0])
     step, size = 1, lax.axis_size("ch")
     while step < size:
         squares = squares + lax.ppermute(squares, "ch", [(i, i ^ step) for i in range(size)])
         step *= 2
-    tall = pl.BlockSpec((BLOCK, channels), lambda k: (k, 0))
     return pl.pallas_call(
         norm_kernel,
-        grid=(blocks,),
-        in_specs=[
-            tall,
-            pl.BlockSpec((1, 1, BLOCK), lambda k: (k, 0, 0)),
-            pl.BlockSpec((1, channels), lambda k: (0, 0)),
+        in_specs=[WHOLE, WHOLE, ANY],
+        out_specs=ANY,
+        out_shape=shape(length, channels, dtype=BF16),
+        scratch_shapes=[
+            pltpu.VMEM((blocks, BLOCK, channels), BF16),
+            pltpu.VMEM((1, channels), F32),
+            pltpu.SemaphoreType.DMA((blocks,)),
+            pltpu.SemaphoreType.DMA(()),
         ],
-        out_specs=tall,
-        out_shape=shape(length, channels, dtype=BF16),
-        compiler_params=params(16),
+        compiler_params=pltpu.CompilerParams(vmem_limit_bytes=24 * 1024 * 1024),
         name="norm",
-    )(*near(gated[0]), squares, gain[None])
+    )(*near(gated), squares, *far(gain[None]))
 
 
 def solution(mesh):

time: 73.8 us -> 72.9 us (0.988)
  Pallas kernels: 51.6 us -> 50.6 us
  starting transfers between devices: 14 us -> 13.1 us
  waiting for transfers between devices: 5.1 us -> 6 us
    ppermute x7, waiting for transfers between devices: 1.81 us -> 2.71 us  [incoming(): send = lambda value, route: lax.ppermute(value, 'seq', route)]
    ppermute x7, starting transfers between devices: 12.3 us -> 11.5 us  [incoming(): send = lambda value, route: lax.ppermute(value, 'seq', route)]
  transfers between devices with their start and end apart: 9 -> 9, of which waited for: 5 -> 4; matrix products, arithmetic and copies ran while one was open for 2% -> 2% of each run, Pallas kernels for 42% -> 42%
where the time goes in v4:
time: 72.9 us; the launch traced here: 72.5 us
  Pallas kernels  50.6 us (69%)
  starting transfers between devices  13.1 us (18%)
  waiting for transfers between devices  6 us (8%)
  other arithmetic  1.62 us (2%)
  local copies, waits for them, and re-layouts  0.81 us (1%)
    pallas_call x5, Pallas kernels, piece(): pl.pallas_call(functools.partial(within_kernel, headdim, chunks, start, b...  30.2 us
    ppermute x7, starting transfers between devices, incoming(): send = lambda value, route: lax.ppermute(value, 'seq', route)  11.5 us
    pallas_call x1, Pallas kernels, shards(): pl.pallas_call(functools.partial(states_kernel, headdim, bool(done)), gri...  8.92 us
    pallas_call x1, Pallas kernels, shards(): pl.pallas_call(functools.partial(carried_kernel, headdim), in_specs=[ANY]...  8.43 us
    ppermute x2, waiting for transfers between devices, shards(): lax.ppermute(squares, 'ch', [(i, i ^ step) for i in range(size)])  3.29 us
    pallas_call x1, Pallas kernels, shards(): pl.pallas_call(norm_kernel, in_specs=[WHOLE, WHOLE, ANY], out_specs=ANY,...  3.05 us
    ppermute x7, waiting for transfers between devices, incoming(): send = lambda value, route: lax.ppermute(value, 'seq', route)  2.71 us
    ppermute x2, starting transfers between devices, shards(): lax.ppermute(squares, 'ch', [(i, i ^ step) for i in range(size)])  1.65 us
  transfers between devices with their start and end apart: 9, of which 4 were waited for; matrix products, arithmetic and copies ran while one was open for 2% of the time, Pallas kernels for 42%

profile of v4, /device:TPU:0, one launch (start us, length us, event | category | flops | bytes accessed | tf_op | source)
XLA Modules:
  0.0 72.5 jit_solution(13954612291538658367)
XLA Ops:
  0.0 8.9 %states.1 = (f32[8,8,2048]{2,1,0:T(8,128)}, f32[4,2,128,1024]{3,2,1,0:T(8,128)}, f32[4,8,1024]{2,1,0:T(8,128)}, f32[2,136,1024]{2,1,0:T(8,128)S(1)}) custom-call(bf16[2048,1024]{1,0:T(8,128)(2,1)} %x_ref.11, bf16[2048,128]{1,0:T(8,128)(2,1)} %b_ref.11, f32[16,2048]{1,0:T(8,128)} %lf_ref.1, f32[16,2048]{1,0:T(8,128)} %lr_ref.1), custom_call_target="tpu_custom_call" | custom-call | tf_op jit(solution)/shard_map/states/pallas_call | solution.py:398
  8.9 0.1 slice_select_fusion
  9.1 3.0 %collective-permute-start = (f32[136,512]{1,0:T(8,128)S(1)}, f32[136,512]{1,0:T(8,128)S(1)}, u32[]{:S(2)}, u32[]{:S(2)}) collective-permute-start(f32[136,512]{1,0:T(8,128)S(1)} %select_bitcast_fusion.dep_ref), channel_id=1, source_target_pairs={{0,4},{4,0},{8,12},{12,8},{16,20},{20,16},{24,28},{28,24},{1,5},{5... | collective-permute-start | bytes 835592 | tf_op jit(solution)/shard_map/ppermute | solution.py:299
  12.1 0.7 broadcast_in_dim.11
  12.8 0.1 broadcast_in_dim_reshape.3.skip_ref
  12.9 6.9 %within.5 = (f32[2048,1024]{1,0:T(8,128)}, f32[8,512]{1,0:T(8,128)S(1)}) custom-call(bf16[2048,1024]{1,0:T(8,128)(2,1)} %x_ref.11, bf16[2048,128]{1,0:T(8,128)(2,1)} %b_ref.11, bf16[2048,128]{1,0:T(8,128)(2,1)} %c_hbm.1, f32[8,8,2048]{2,1,0:T(8,128)} %get-tuple-element.20.cum_ref.cum_hbm, f32[1,1024]{1,0:T(1,128)S(1)} %broadcast_in_dim_reshape.3.skip_ref, ...), custom_call_target="tpu_custom_call" | custom-call | flops 4294967296 | bytes 3145728 | tf_op jit(solution)/shard_map/within/pallas_call | solution.py:448
  19.8 0.0 collective-permute-done
  19.8 0.2 fusion.11
  20.1 0.1 select_add_fusion.2.dep_ref
  20.2 3.5 %collective-permute-start.2 = (f32[128,512]{1,0:T(8,128)S(1)}, f32[128,512]{1,0:T(8,128)S(1)}, u32[]{:S(2)}, u32[]{:S(2)}) collective-permute-start(f32[128,512]{1,0:T(8,128)S(1)} %select_add_fusion.2.dep_ref), channel_id=1, source_target_pairs={{0,8},{4,12},{24,16},{28,20},{1,9},{5,13},{25,17},{29,21},{2,10},{... | collective-permute-start | bytes 786440 | tf_op jit(solution)/shard_map/ppermute | solution.py:299
  23.7 6.9 %within.6 = (f32[2048,1024]{1,0:T(8,128)}, f32[8,512]{1,0:T(8,128)S(1)}) custom-call(bf16[2048,1024]{1,0:T(8,128)(2,1)} %x_ref.11, bf16[2048,128]{1,0:T(8,128)(2,1)} %b_ref.11, bf16[2048,128]{1,0:T(8,128)(2,1)} %c_hbm.1, f32[8,8,2048]{2,1,0:T(8,128)} %get-tuple-element.20.cum_ref.cum_hbm, ...), custom_call_target="tpu_custom_call", output_to_operand_aliasing={{0}: (6, {})} | custom-call | flops 4294967296 | bytes 3145728 | tf_op jit(solution)/shard_map/within/pallas_call | solution.py:448
  30.6 0.7 collective-permute-start.1
  31.3 0.0 collective-permute-done.2
  31.3 0.2 broadcast_select_fusion.3
  31.5 1.4 %collective-permute-start.5 = (f32[128,512]{1,0:T(8,128)S(1)}, f32[128,512]{1,0:T(8,128)S(1)}, u32[]{:S(2)}, u32[]{:S(2)}) collective-permute-start(f32[128,512]{1,0:T(8,128)S(1)} %get-tuple-element.35), channel_id=1, source_target_pairs={{0,4},{4,0},{8,12},{12,8},{16,20},{20,16},{24,28},{28,24},{1,5},{5... | collective-permute-start | bytes 786440 | tf_op jit(solution)/shard_map/ppermute | solution.py:299
  32.9 0.7 collective-permute-start.3
  33.6 5.8 %within.7 = (f32[2048,1024]{1,0:T(8,128)}, f32[8,512]{1,0:T(8,128)S(1)}) custom-call(bf16[2048,1024]{1,0:T(8,128)(2,1)} %x_ref.11, bf16[2048,128]{1,0:T(8,128)(2,1)} %b_ref.11, bf16[2048,128]{1,0:T(8,128)(2,1)} %c_hbm.1, f32[8,8,2048]{2,1,0:T(8,128)} %get-tuple-element.20.cum_ref.cum_hbm, ...), custom_call_target="tpu_custom_call", output_to_operand_aliasing={{0}: (6, {})} | custom-call | flops 4294967296 | bytes 3145728 | tf_op jit(solution)/shard_map/within/pallas_call | solution.py:448
  39.3 0.9 %collective-permute-done.1 = f32[136,512]{1,0:T(8,128)S(1)} collective-permute-done((f32[136,512]{1,0:T(8,128)S(1)}, f32[136,512]{1,0:T(8,128)S(1)}, u32[]{:S(2)}, u32[]{:S(2)}) %collective-permute-start.1) | collective-permute-done | bytes 278560 | tf_op jit(solution)/shard_map/ppermute | solution.py:299
  40.2 0.1 fusion.9
  40.4 0.0 collective-permute-done.3
  40.4 0.3 fusion.5
  40.7 1.5 %collective-permute-start.4 = (f32[128,512]{1,0:T(8,128)S(1)}, f32[128,512]{1,0:T(8,128)S(1)}, u32[]{:S(2)}, u32[]{:S(2)}) collective-permute-start(f32[128,512]{1,0:T(8,128)S(1)} %get-tuple-element.41.dep_ref), channel_id=1, source_target_pairs={{16,24},{20,28},{8,0},{12,4},{17,25},{21,29},{9,1},{13,5},{18,26},... | collective-permute-start | bytes 786440 | tf_op jit(solution)/shard_map/ppermute | solution.py:299
  42.2 4.9 %within.8 = (f32[2048,1024]{1,0:T(8,128)}, f32[8,512]{1,0:T(8,128)S(1)}) custom-call(bf16[2048,1024]{1,0:T(8,128)(2,1)} %x_ref.11, bf16[2048,128]{1,0:T(8,128)(2,1)} %b_ref.11, bf16[2048,128]{1,0:T(8,128)(2,1)} %c_hbm.1, f32[8,8,2048]{2,1,0:T(8,128)} %get-tuple-element.20.cum_ref.cum_hbm, ...), custom_call_target="tpu_custom_call", output_to_operand_aliasing={{0}: (6, {})} | custom-call | flops 4294967296 | bytes 3145728 | tf_op jit(solution)/shard_map/within/pallas_call | solution.py:448
  47.1 0.0 collective-permute-done.5
  47.1 0.1 select_bitcast_fusion.4
  47.1 1.8 %collective-permute-done.4 = f32[128,512]{1,0:T(8,128)S(1)} collective-permute-done((f32[128,512]{1,0:T(8,128)S(1)}, f32[128,512]{1,0:T(8,128)S(1)}, u32[]{:S(2)}, u32[]{:S(2)}) %collective-permute-start.4) | collective-permute-done | bytes 262176 | tf_op jit(solution)/shard_map/ppermute | solution.py:299
  49.0 0.2 select_add_fusion
  49.2 0.7 collective-permute-start.6
  49.9 5.7 %within.9 = (f32[2048,1024]{1,0:T(8,128)}, f32[8,512]{1,0:T(8,128)}) custom-call(bf16[2048,1024]{1,0:T(8,128)(2,1)} %x_ref.11, bf16[2048,128]{1,0:T(8,128)(2,1)} %b_ref.11, bf16[2048,128]{1,0:T(8,128)(2,1)} %c_hbm.1, f32[8,8,2048]{2,1,0:T(8,128)} %get-tuple-element.20.cum_ref.cum_hbm, ...), custom_call_target="tpu_custom_call", output_to_operand_aliasing={{0}: (6, {})} | custom-call | flops 4294967296 | bytes 3145728 | tf_op jit(solution)/shard_map/within/pallas_call | solution.py:448
  55.6 0.0 collective-permute-done.6
  55.6 0.1 select_bitcast_fusion.2
  55.7 0.1 fusion.1
  55.8 0.1 pad_maximum_fusion.in_ref
  55.9 8.4 %carried.1 = (f32[2048,1024]{1,0:T(8,128)S(1)}, f32[4,1,512]{2,1,0:T(1,128)S(1)}) custom-call(f32[2048,1024]{1,0:T(8,128)} %get-tuple-element.30.a_hbm, bf16[2048,1024]{1,0:T(8,128)(2,1)} %gate_hbm.1, bf16[2048,128]{1,0:T(8,128)(2,1)} %c_hbm.1, f32[8,8,2048]{2,1,0:T(8,128)} %get-tuple-element.20.cum_ref.cum_hbm, ...), custom_call_target="tpu_custom_call" | custom-call | tf_op jit(solution)/shard_map/carried/pallas_call | solution.py:485
  64.3 0.1 collective-permute-start.7
  64.4 1.2 %collective-permute-done.7 = f32[4,1,512]{2,1,0:T(1,128)S(1)} collective-permute-done((f32[4,1,512]{2,1,0:T(1,128)S(1)}, f32[4,1,512]{2,1,0:T(1,128)S(1)}, u32[]{:S(2)}, u32[]{:S(2)}) %collective-permute-start.7) | collective-permute-done | bytes 8224 | tf_op jit(solution)/shard_map/ppermute | solution.py:505
  65.6 1.6 %collective-permute-start.8 = (f32[4,1,512]{2,1,0:T(1,128)S(1)}, f32[4,1,512]{2,1,0:T(1,128)S(1)}, u32[]{:S(2)}, u32[]{:S(2)}) collective-permute-start(f32[4,1,512]{2,1,0:T(1,128)S(1)} %add.150), channel_id=1, source_target_pairs={{0,2},{1,3},{2,0},{3,1},{4,6},{5,7},{6,4},{7,5},{8,10},{9,11},{10,... | collective-permute-start | bytes 24584 | tf_op jit(solution)/shard_map/ppermute | solution.py:505
  67.1 2.1 %collective-permute-done.8 = f32[4,1,512]{2,1,0:T(1,128)S(1)} collective-permute-done((f32[4,1,512]{2,1,0:T(1,128)S(1)}, f32[4,1,512]{2,1,0:T(1,128)S(1)}, u32[]{:S(2)}, u32[]{:S(2)}) %collective-permute-start.8) | collective-permute-done | bytes 8224 | tf_op jit(solution)/shard_map/ppermute | solution.py:505
  69.3 3.1 %norm.1 = bf16[2048,1024]{1,0:T(8,128)(2,1)} custom-call(f32[2048,1024]{1,0:T(8,128)S(1)} %get-tuple-element.33.gated_ref, f32[4,1,512]{2,1,0:T(1,128)S(1)} %add.151.sq_ref, f32[1,1024]{1,0:T(1,128)} %bitcast.71), custom_call_target="tpu_custom_call" | custom-call | tf_op jit(solution)/shard_map/norm/pallas_call | solution.py:507
  (12 shorter events, 0.1 us)
Async XLA Ops:
  9.1 10.7 %collective-permute-start = (f32[136,512]{1,0:T(8,128)S(1)}, f32[136,512]{1,0:T(8,128)S(1)}, u32[]{:S(2)}, u32[]{:S(2)}) collective-permute-start(f32[136,512]{1,0:T(8,128)S(1)} %select_bitcast_fusion.dep_ref), channel_id=1, source_target_pairs={{0,4},{4,0},{8,12},{12,8},{16,20},{20,16},{24,28},{28,24},{1,5},{5... | collective-permute-start | bytes 835592 | tf_op jit(solution)/shard_map/ppermute | solution.py:299
  20.2 11.1 %collective-permute-start.2 = (f32[128,512]{1,0:T(8,128)S(1)}, f32[128,512]{1,0:T(8,128)S(1)}, u32[]{:S(2)}, u32[]{:S(2)}) collective-permute-start(f32[128,512]{1,0:T(8,128)S(1)} %select_add_fusion.2.dep_ref), channel_id=1, source_target_pairs={{0,8},{4,12},{24,16},{28,20},{1,9},{5,13},{25,17},{29,21},{2,10},{... | collective-permute-start | bytes 786440 | tf_op jit(solution)/shard_map/ppermute | solution.py:299
  30.6 9.6 %collective-permute-start.1 = (f32[136,512]{1,0:T(8,128)S(1)}, f32[136,512]{1,0:T(8,128)S(1)}, u32[]{:S(2)}, u32[]{:S(2)}) collective-permute-start(f32[136,512]{1,0:T(8,128)S(1)} %get-tuple-element.73), channel_id=1, source_target_pairs={{0,4},{4,0},{8,12},{12,8},{16,20},{20,16},{24,28},{28,24},{1,5},{5... | collective-permute-start | bytes 835592 | tf_op jit(solution)/shard_map/ppermute | solution.py:299
  31.5 15.6 %collective-permute-start.5 = (f32[128,512]{1,0:T(8,128)S(1)}, f32[128,512]{1,0:T(8,128)S(1)}, u32[]{:S(2)}, u32[]{:S(2)}) collective-permute-start(f32[128,512]{1,0:T(8,128)S(1)} %get-tuple-element.35), channel_id=1, source_target_pairs={{0,4},{4,0},{8,12},{12,8},{16,20},{20,16},{24,28},{28,24},{1,5},{5... | collective-permute-start | bytes 786440 | tf_op jit(solution)/shard_map/ppermute | solution.py:299
  32.9 7.5 %collective-permute-start.3 = (f32[128,512]{1,0:T(8,128)S(1)}, f32[128,512]{1,0:T(8,128)S(1)}, u32[]{:S(2)}, u32[]{:S(2)}) collective-permute-start(f32[128,512]{1,0:T(8,128)S(1)} %get-tuple-element.62.dep_ref), channel_id=1, source_target_pairs={{8,16},{12,20},{16,8},{20,12},{9,17},{13,21},{17,9},{21,13},{10,18... | collective-permute-start | bytes 786440 | tf_op jit(solution)/shard_map/ppermute | solution.py:299
  40.7 8.3 %collective-permute-start.4 = (f32[128,512]{1,0:T(8,128)S(1)}, f32[128,512]{1,0:T(8,128)S(1)}, u32[]{:S(2)}, u32[]{:S(2)}) collective-permute-start(f32[128,512]{1,0:T(8,128)S(1)} %get-tuple-element.41.dep_ref), channel_id=1, source_target_pairs={{16,24},{20,28},{8,0},{12,4},{17,25},{21,29},{9,1},{13,5},{18,26},... | collective-permute-start | bytes 786440 | tf_op jit(solution)/shard_map/ppermute | solution.py:299
  49.2 6.4 %collective-permute-start.6 = (f32[128,512]{1,0:T(8,128)S(1)}, f32[128,512]{1,0:T(8,128)S(1)}, u32[]{:S(2)}, u32[]{:S(2)}) collective-permute-start(f32[128,512]{1,0:T(8,128)S(1)} %get-tuple-element.38.dep_ref), channel_id=1, source_target_pairs={{0,4},{4,0},{8,12},{12,8},{16,20},{20,16},{24,28},{28,24},{1,5},{5... | collective-permute-start | bytes 786440 | tf_op jit(solution)/shard_map/ppermute | solution.py:299
  64.3 1.2 %collective-permute-start.7 = (f32[4,1,512]{2,1,0:T(1,128)S(1)}, f32[4,1,512]{2,1,0:T(1,128)S(1)}, u32[]{:S(2)}, u32[]{:S(2)}) collective-permute-start(f32[4,1,512]{2,1,0:T(1,128)S(1)} %get-tuple-element.34), channel_id=1, source_target_pairs={{0,1},{1,0},{2,3},{3,2},{4,5},{5,4},{6,7},{7,6},{8,9},{9,8},{10,11... | collective-permute-start | bytes 24584 | tf_op jit(solution)/shard_map/ppermute | solution.py:505
  65.6 3.7 %collective-permute-start.8 = (f32[4,1,512]{2,1,0:T(1,128)S(1)}, f32[4,1,512]{2,1,0:T(1,128)S(1)}, u32[]{:S(2)}, u32[]{:S(2)}) collective-permute-start(f32[4,1,512]{2,1,0:T(1,128)S(1)} %add.150), channel_id=1, source_target_pairs={{0,2},{1,3},{2,0},{3,1},{4,6},{5,7},{6,4},{7,5},{8,10},{9,11},{10,... | collective-permute-start | bytes 24584 | tf_op jit(solution)/shard_map/ppermute | solution.py:505

commit v5 on v4

--- a/solution.py
+++ b/solution.py
@@ -12,7 +12,7 @@
 TILE = 128
 TILES = BLOCK // TILE
 GROUPS = 1
-SHARES = (4, 8, 11, 13, 16)
+SHARES = (2, 3, 4, 6, 8)
 LOG2E = 1.4426950408889634
 F32, BF16 = jnp.float32, jnp.bfloat16
 ANY = pl.BlockSpec(memory_space=pl.ANY)
@@ -432,7 +432,7 @@
     cum, before, off = shared
     skip_row = jnp.repeat(skip, headdim)[None]
     within = []
-    some = 2
+    some = 4
     chunks = pairs // some
     units = blocks * chunks
     cuts = [0] + [units * share // SHARES[-1] for share in SHARES]

time: 72.9 us -> 71.4 us (0.979)
  Pallas kernels: 50.6 us -> 47.5 us
  starting transfers between devices: 13.1 us -> 14 us
  waiting for transfers between devices: 6 us -> 6.76 us
    pallas_call x5, Pallas kernels: 30.2 us -> 27.1 us  [piece(): pl.pallas_call(functools.partial(within_kernel, headdim, chunks, start, b...]
    ppermute x7, starting transfers between devices: 11.5 us -> 12.3 us  [incoming(): send = lambda value, route: lax.ppermute(value, 'seq', route)]
    ppermute x7, waiting for transfers between devices: 2.71 us -> 3.46 us  [incoming(): send = lambda value, route: lax.ppermute(value, 'seq', route)]
  transfers between devices with their start and end apart: 9 -> 9, of which waited for: 4 -> 4; matrix products, arithmetic and copies ran while one was open for 2% -> 2% of each run, Pallas kernels for 42% -> 38%
where the time goes in v5:
time: 71.4 us; the launch traced here: 71 us
  Pallas kernels  47.5 us (67%)
  starting transfers between devices  14 us (20%)
  waiting for transfers between devices  6.76 us (9%)
  other arithmetic  1.62 us (2%)
  local copies, waits for them, and re-layouts  0.81 us (1%)
    pallas_call x5, Pallas kernels, piece(): pl.pallas_call(functools.partial(within_kernel, headdim, chunks, start, b...  27.1 us
    ppermute x7, starting transfers between devices, incoming(): send = lambda value, route: lax.ppermute(value, 'seq', route)  12.3 us
    pallas_call x1, Pallas kernels, shards(): pl.pallas_call(functools.partial(states_kernel, headdim, bool(done)), gri...  8.92 us
    pallas_call x1, Pallas kernels, shards(): pl.pallas_call(functools.partial(carried_kernel, headdim), in_specs=[ANY]...  8.43 us
    ppermute x7, waiting for transfers between devices, incoming(): send = lambda value, route: lax.ppermute(value, 'seq', route)  3.46 us
    ppermute x2, waiting for transfers between devices, shards(): lax.ppermute(squares, 'ch', [(i, i ^ step) for i in range(size)])  3.3 us
    pallas_call x1, Pallas kernels, shards(): pl.pallas_call(norm_kernel, in_specs=[WHOLE, WHOLE, ANY], out_specs=ANY,...  3.05 us
    ppermute x2, starting transfers between devices, shards(): lax.ppermute(squares, 'ch', [(i, i ^ step) for i in range(size)])  1.65 us
  transfers between devices with their start and end apart: 9, of which 4 were waited for; matrix products, arithmetic and copies ran while one was open for 2% of the time, Pallas kernels for 38%

profile of v5, /device:TPU:0, one launch (start us, length us, event | category | flops | bytes accessed | tf_op | source)
XLA Modules:
  0.0 71.0 jit_solution(14142402330599473147)
XLA Ops:
  0.0 8.9 %states.1 = (f32[8,8,2048]{2,1,0:T(8,128)}, f32[4,2,128,1024]{3,2,1,0:T(8,128)}, f32[4,8,1024]{2,1,0:T(8,128)}, f32[2,136,1024]{2,1,0:T(8,128)S(1)}) custom-call(bf16[2048,1024]{1,0:T(8,128)(2,1)} %x_ref.11, bf16[2048,128]{1,0:T(8,128)(2,1)} %b_ref.11, f32[16,2048]{1,0:T(8,128)} %lf_ref.1, f32[16,2048]{1,0:T(8,128)} %lr_ref.1), custom_call_target="tpu_custom_call" | custom-call | tf_op jit(solution)/shard_map/states/pallas_call | solution.py:398
  8.9 0.1 slice_select_fusion
  9.1 3.0 %collective-permute-start = (f32[136,512]{1,0:T(8,128)S(1)}, f32[136,512]{1,0:T(8,128)S(1)}, u32[]{:S(2)}, u32[]{:S(2)}) collective-permute-start(f32[136,512]{1,0:T(8,128)S(1)} %select_bitcast_fusion.dep_ref), channel_id=1, source_target_pairs={{0,4},{4,0},{8,12},{12,8},{16,20},{20,16},{24,28},{28,24},{1,5},{5... | collective-permute-start | bytes 835592 | tf_op jit(solution)/shard_map/ppermute | solution.py:299
  12.1 0.7 %broadcast_in_dim.11 = f32[16,64]{1,0:T(8,128)S(1)} broadcast(f32[16]{0:T(128)} %param.14), dimensions={0} | broadcast | bytes 4160 | tf_op jit(solution)/shard_map/broadcast_in_dim | solution.py:433
  12.8 0.1 broadcast_in_dim_reshape.3.skip_ref
  12.9 6.3 %within.5 = (f32[2048,1024]{1,0:T(8,128)}, f32[8,512]{1,0:T(8,128)S(1)}) custom-call(bf16[2048,1024]{1,0:T(8,128)(2,1)} %x_ref.11, bf16[2048,128]{1,0:T(8,128)(2,1)} %b_ref.11, bf16[2048,128]{1,0:T(8,128)(2,1)} %c_hbm.1, f32[8,8,2048]{2,1,0:T(8,128)} %get-tuple-element.20.cum_ref.cum_hbm, f32[1,1024]{1,0:T(1,128)S(1)} %broadcast_in_dim_reshape.3.skip_ref, ...), custom_call_target="tpu_custom_call" | custom-call | flops 4294967296 | bytes 3145728 | tf_op jit(solution)/shard_map/within/pallas_call | solution.py:448
  19.2 0.0 collective-permute-done
  19.2 0.2 fusion.11
  19.4 0.1 select_add_fusion.2.dep_ref
  19.6 3.5 %collective-permute-start.2 = (f32[128,512]{1,0:T(8,128)S(1)}, f32[128,512]{1,0:T(8,128)S(1)}, u32[]{:S(2)}, u32[]{:S(2)}) collective-permute-start(f32[128,512]{1,0:T(8,128)S(1)} %select_add_fusion.2.dep_ref), channel_id=1, source_target_pairs={{0,8},{4,12},{24,16},{28,20},{1,9},{5,13},{25,17},{29,21},{2,10},{... | collective-permute-start | bytes 786440 | tf_op jit(solution)/shard_map/ppermute | solution.py:299
  23.1 4.0 %within.6 = (f32[2048,1024]{1,0:T(8,128)}, f32[8,512]{1,0:T(8,128)S(1)}) custom-call(bf16[2048,1024]{1,0:T(8,128)(2,1)} %x_ref.11, bf16[2048,128]{1,0:T(8,128)(2,1)} %b_ref.11, bf16[2048,128]{1,0:T(8,128)(2,1)} %c_hbm.1, f32[8,8,2048]{2,1,0:T(8,128)} %get-tuple-element.20.cum_ref.cum_hbm, ...), custom_call_target="tpu_custom_call", output_to_operand_aliasing={{0}: (6, {})} | custom-call | flops 4294967296 | bytes 3145728 | tf_op jit(solution)/shard_map/within/pallas_call | solution.py:448
  27.1 1.3 %collective-permute-start.1 = (f32[136,512]{1,0:T(8,128)S(1)}, f32[136,512]{1,0:T(8,128)S(1)}, u32[]{:S(2)}, u32[]{:S(2)}) collective-permute-start(f32[136,512]{1,0:T(8,128)S(1)} %get-tuple-element.73), channel_id=1, source_target_pairs={{0,4},{4,0},{8,12},{12,8},{16,20},{20,16},{24,28},{28,24},{1,5},{5... | collective-permute-start | bytes 835592 | tf_op jit(solution)/shard_map/ppermute | solution.py:299
  28.4 0.0 collective-permute-done.2
  28.4 0.2 broadcast_select_fusion.3
  28.5 0.8 %collective-permute-start.5 = (f32[128,512]{1,0:T(8,128)S(1)}, f32[128,512]{1,0:T(8,128)S(1)}, u32[]{:S(2)}, u32[]{:S(2)}) collective-permute-start(f32[128,512]{1,0:T(8,128)S(1)} %get-tuple-element.35), channel_id=1, source_target_pairs={{0,4},{4,0},{8,12},{12,8},{16,20},{20,16},{24,28},{28,24},{1,5},{5... | collective-permute-start | bytes 786440 | tf_op jit(solution)/shard_map/ppermute | solution.py:299
  29.4 0.7 collective-permute-start.3
  30.0 4.1 %within.7 = (f32[2048,1024]{1,0:T(8,128)}, f32[8,512]{1,0:T(8,128)S(1)}) custom-call(bf16[2048,1024]{1,0:T(8,128)(2,1)} %x_ref.11, bf16[2048,128]{1,0:T(8,128)(2,1)} %b_ref.11, bf16[2048,128]{1,0:T(8,128)(2,1)} %c_hbm.1, f32[8,8,2048]{2,1,0:T(8,128)} %get-tuple-element.20.cum_ref.cum_hbm, ...), custom_call_target="tpu_custom_call", output_to_operand_aliasing={{0}: (6, {})} | custom-call | flops 4294967296 | bytes 3145728 | tf_op jit(solution)/shard_map/within/pallas_call | solution.py:448
  34.1 2.6 %collective-permute-done.1 = f32[136,512]{1,0:T(8,128)S(1)} collective-permute-done((f32[136,512]{1,0:T(8,128)S(1)}, f32[136,512]{1,0:T(8,128)S(1)}, u32[]{:S(2)}, u32[]{:S(2)}) %collective-permute-start.1) | collective-permute-done | bytes 278560 | tf_op jit(solution)/shard_map/ppermute | solution.py:299
  36.7 0.1 fusion.9
  36.8 0.0 collective-permute-done.3
  36.9 0.3 fusion.5
  37.2 1.5 %collective-permute-start.4 = (f32[128,512]{1,0:T(8,128)S(1)}, f32[128,512]{1,0:T(8,128)S(1)}, u32[]{:S(2)}, u32[]{:S(2)}) collective-permute-start(f32[128,512]{1,0:T(8,128)S(1)} %get-tuple-element.41.dep_ref), channel_id=1, source_target_pairs={{16,24},{20,28},{8,0},{12,4},{17,25},{21,29},{9,1},{13,5},{18,26},... | collective-permute-start | bytes 786440 | tf_op jit(solution)/shard_map/ppermute | solution.py:299
  38.7 6.3 %within.8 = (f32[2048,1024]{1,0:T(8,128)}, f32[8,512]{1,0:T(8,128)S(1)}) custom-call(bf16[2048,1024]{1,0:T(8,128)(2,1)} %x_ref.11, bf16[2048,128]{1,0:T(8,128)(2,1)} %b_ref.11, bf16[2048,128]{1,0:T(8,128)(2,1)} %c_hbm.1, f32[8,8,2048]{2,1,0:T(8,128)} %get-tuple-element.20.cum_ref.cum_hbm, ...), custom_call_target="tpu_custom_call", output_to_operand_aliasing={{0}: (6, {})} | custom-call | flops 4294967296 | bytes 3145728 | tf_op jit(solution)/shard_map/within/pallas_call | solution.py:448
  45.0 0.0 collective-permute-done.5
  45.0 0.1 select_bitcast_fusion.4
  45.1 0.9 %collective-permute-done.4 = f32[128,512]{1,0:T(8,128)S(1)} collective-permute-done((f32[128,512]{1,0:T(8,128)S(1)}, f32[128,512]{1,0:T(8,128)S(1)}, u32[]{:S(2)}, u32[]{:S(2)}) %collective-permute-start.4) | collective-permute-done | bytes 262176 | tf_op jit(solution)/shard_map/ppermute | solution.py:299
  45.9 0.2 select_add_fusion
  46.1 1.6 %collective-permute-start.6 = (f32[128,512]{1,0:T(8,128)S(1)}, f32[128,512]{1,0:T(8,128)S(1)}, u32[]{:S(2)}, u32[]{:S(2)}) collective-permute-start(f32[128,512]{1,0:T(8,128)S(1)} %get-tuple-element.38.dep_ref), channel_id=1, source_target_pairs={{0,4},{4,0},{8,12},{12,8},{16,20},{20,16},{24,28},{28,24},{1,5},{5... | collective-permute-start | bytes 786440 | tf_op jit(solution)/shard_map/ppermute | solution.py:299
  47.7 6.4 %within.9 = (f32[2048,1024]{1,0:T(8,128)}, f32[8,512]{1,0:T(8,128)}) custom-call(bf16[2048,1024]{1,0:T(8,128)(2,1)} %x_ref.11, bf16[2048,128]{1,0:T(8,128)(2,1)} %b_ref.11, bf16[2048,128]{1,0:T(8,128)(2,1)} %c_hbm.1, f32[8,8,2048]{2,1,0:T(8,128)} %get-tuple-element.20.cum_ref.cum_hbm, ...), custom_call_target="tpu_custom_call", output_to_operand_aliasing={{0}: (6, {})} | custom-call | flops 4294967296 | bytes 3145728 | tf_op jit(solution)/shard_map/within/pallas_call | solution.py:448
  54.1 0.0 collective-permute-done.6
  54.1 0.1 select_bitcast_fusion.2
  54.2 0.1 fusion.1
  54.3 0.1 pad_maximum_fusion.in_ref
  54.4 8.4 %carried.1 = (f32[2048,1024]{1,0:T(8,128)S(1)}, f32[4,1,512]{2,1,0:T(1,128)S(1)}) custom-call(f32[2048,1024]{1,0:T(8,128)} %get-tuple-element.30.a_hbm, bf16[2048,1024]{1,0:T(8,128)(2,1)} %gate_hbm.1, bf16[2048,128]{1,0:T(8,128)(2,1)} %c_hbm.1, f32[8,8,2048]{2,1,0:T(8,128)} %get-tuple-element.20.cum_ref.cum_hbm, ...), custom_call_target="tpu_custom_call" | custom-call | tf_op jit(solution)/shard_map/carried/pallas_call | solution.py:485
  62.8 0.1 collective-permute-start.7
  62.9 1.2 %collective-permute-done.7 = f32[4,1,512]{2,1,0:T(1,128)S(1)} collective-permute-done((f32[4,1,512]{2,1,0:T(1,128)S(1)}, f32[4,1,512]{2,1,0:T(1,128)S(1)}, u32[]{:S(2)}, u32[]{:S(2)}) %collective-permute-start.7) | collective-permute-done | bytes 8224 | tf_op jit(solution)/shard_map/ppermute | solution.py:505
  64.0 1.6 %collective-permute-start.8 = (f32[4,1,512]{2,1,0:T(1,128)S(1)}, f32[4,1,512]{2,1,0:T(1,128)S(1)}, u32[]{:S(2)}, u32[]{:S(2)}) collective-permute-start(f32[4,1,512]{2,1,0:T(1,128)S(1)} %add.150), channel_id=1, source_target_pairs={{0,2},{1,3},{2,0},{3,1},{4,6},{5,7},{6,4},{7,5},{8,10},{9,11},{10,... | collective-permute-start | bytes 24584 | tf_op jit(solution)/shard_map/ppermute | solution.py:505
  65.6 2.1 %collective-permute-done.8 = f32[4,1,512]{2,1,0:T(1,128)S(1)} collective-permute-done((f32[4,1,512]{2,1,0:T(1,128)S(1)}, f32[4,1,512]{2,1,0:T(1,128)S(1)}, u32[]{:S(2)}, u32[]{:S(2)}) %collective-permute-start.8) | collective-permute-done | bytes 8224 | tf_op jit(solution)/shard_map/ppermute | solution.py:505
  67.8 3.1 %norm.1 = bf16[2048,1024]{1,0:T(8,128)(2,1)} custom-call(f32[2048,1024]{1,0:T(8,128)S(1)} %get-tuple-element.33.gated_ref, f32[4,1,512]{2,1,0:T(1,128)S(1)} %add.151.sq_ref, f32[1,1024]{1,0:T(1,128)} %bitcast.71), custom_call_target="tpu_custom_call" | custom-call | tf_op jit(solution)/shard_map/norm/pallas_call | solution.py:507
  (12 shorter events, 0.1 us)
Async XLA Ops:
  9.1 10.1 %collective-permute-start = (f32[136,512]{1,0:T(8,128)S(1)}, f32[136,512]{1,0:T(8,128)S(1)}, u32[]{:S(2)}, u32[]{:S(2)}) collective-permute-start(f32[136,512]{1,0:T(8,128)S(1)} %select_bitcast_fusion.dep_ref), channel_id=1, source_target_pairs={{0,4},{4,0},{8,12},{12,8},{16,20},{20,16},{24,28},{28,24},{1,5},{5... | collective-permute-start | bytes 835592 | tf_op jit(solution)/shard_map/ppermute | solution.py:299
  19.6 8.8 %collective-permute-start.2 = (f32[128,512]{1,0:T(8,128)S(1)}, f32[128,512]{1,0:T(8,128)S(1)}, u32[]{:S(2)}, u32[]{:S(2)}) collective-permute-start(f32[128,512]{1,0:T(8,128)S(1)} %select_add_fusion.2.dep_ref), channel_id=1, source_target_pairs={{0,8},{4,12},{24,16},{28,20},{1,9},{5,13},{25,17},{29,21},{2,10},{... | collective-permute-start | bytes 786440 | tf_op jit(solution)/shard_map/ppermute | solution.py:299
  27.1 9.6 %collective-permute-start.1 = (f32[136,512]{1,0:T(8,128)S(1)}, f32[136,512]{1,0:T(8,128)S(1)}, u32[]{:S(2)}, u32[]{:S(2)}) collective-permute-start(f32[136,512]{1,0:T(8,128)S(1)} %get-tuple-element.73), channel_id=1, source_target_pairs={{0,4},{4,0},{8,12},{12,8},{16,20},{20,16},{24,28},{28,24},{1,5},{5... | collective-permute-start | bytes 835592 | tf_op jit(solution)/shard_map/ppermute | solution.py:299
  28.5 16.4 %collective-permute-start.5 = (f32[128,512]{1,0:T(8,128)S(1)}, f32[128,512]{1,0:T(8,128)S(1)}, u32[]{:S(2)}, u32[]{:S(2)}) collective-permute-start(f32[128,512]{1,0:T(8,128)S(1)} %get-tuple-element.35), channel_id=1, source_target_pairs={{0,4},{4,0},{8,12},{12,8},{16,20},{20,16},{24,28},{28,24},{1,5},{5... | collective-permute-start | bytes 786440 | tf_op jit(solution)/shard_map/ppermute | solution.py:299
  29.4 7.5 %collective-permute-start.3 = (f32[128,512]{1,0:T(8,128)S(1)}, f32[128,512]{1,0:T(8,128)S(1)}, u32[]{:S(2)}, u32[]{:S(2)}) collective-permute-start(f32[128,512]{1,0:T(8,128)S(1)} %get-tuple-element.62.dep_ref), channel_id=1, source_target_pairs={{8,16},{12,20},{16,8},{20,12},{9,17},{13,21},{17,9},{21,13},{10,18... | collective-permute-start | bytes 786440 | tf_op jit(solution)/shard_map/ppermute | solution.py:299
  37.2 8.7 %collective-permute-start.4 = (f32[128,512]{1,0:T(8,128)S(1)}, f32[128,512]{1,0:T(8,128)S(1)}, u32[]{:S(2)}, u32[]{:S(2)}) collective-permute-start(f32[128,512]{1,0:T(8,128)S(1)} %get-tuple-element.41.dep_ref), channel_id=1, source_target_pairs={{16,24},{20,28},{8,0},{12,4},{17,25},{21,29},{9,1},{13,5},{18,26},... | collective-permute-start | bytes 786440 | tf_op jit(solution)/shard_map/ppermute | solution.py:299
  46.1 8.0 %collective-permute-start.6 = (f32[128,512]{1,0:T(8,128)S(1)}, f32[128,512]{1,0:T(8,128)S(1)}, u32[]{:S(2)}, u32[]{:S(2)}) collective-permute-start(f32[128,512]{1,0:T(8,128)S(1)} %get-tuple-element.38.dep_ref), channel_id=1, source_target_pairs={{0,4},{4,0},{8,12},{12,8},{16,20},{20,16},{24,28},{28,24},{1,5},{5... | collective-permute-start | bytes 786440 | tf_op jit(solution)/shard_map/ppermute | solution.py:299
  62.8 1.2 %collective-permute-start.7 = (f32[4,1,512]{2,1,0:T(1,128)S(1)}, f32[4,1,512]{2,1,0:T(1,128)S(1)}, u32[]{:S(2)}, u32[]{:S(2)}) collective-permute-start(f32[4,1,512]{2,1,0:T(1,128)S(1)} %get-tuple-element.34), channel_id=1, source_target_pairs={{0,1},{1,0},{2,3},{3,2},{4,5},{5,4},{6,7},{7,6},{8,9},{9,8},{10,11... | collective-permute-start | bytes 24584 | tf_op jit(solution)/shard_map/ppermute | solution.py:505
  64.0 3.7 %collective-permute-start.8 = (f32[4,1,512]{2,1,0:T(1,128)S(1)}, f32[4,1,512]{2,1,0:T(1,128)S(1)}, u32[]{:S(2)}, u32[]{:S(2)}) collective-permute-start(f32[4,1,512]{2,1,0:T(1,128)S(1)} %add.150), channel_id=1, source_target_pairs={{0,2},{1,3},{2,0},{3,1},{4,6},{5,7},{6,4},{7,5},{8,10},{9,11},{10,... | collective-permute-start | bytes 24584 | tf_op jit(solution)/shard_map/ppermute | solution.py:505

commit v6 on v5

--- a/solution.py
+++ b/solution.py
@@ -203,7 +203,7 @@
     width = 2 * headdim
 
     def copies(k):
-        at = pl.ds(pl.multiple_of(k * BLOCK, BLOCK), BLOCK)
+        at = pl.ds(k * BLOCK, BLOCK)
         pieces = [
             (before_hbm.at[k], before_buf.at[k]),
             (off_hbm.at[k], off_buf.at[k]),
@@ -224,8 +224,7 @@
         hot = jnp.where(row == 8 * p + 2 + jnp.where(lane < headdim, 0, 1), 1.0, 0.0)
         hot_ref[:, p * width : (p + 1) * width] = hot.astype(BF16)
 
-    @pl.loop(0, blocks)
-    def _(k):
+    for k in range(blocks):
         for copy in copies(k):
             copy.wait()
         every = jnp.exp2(cum_buf[k].reshape(8 * pairs, BLOCK))
@@ -262,33 +261,28 @@
                     total = total + other * z[to, width:]
                     half = 0.5 * gate_buf[k, at, cols].astype(F32)
                     gated = total * (half + half * jnp.tanh(half))
-                    out_ref[pl.ds(pl.multiple_of(k * BLOCK + i * TILE, TILE), TILE), cols] = gated
+                    out_ref[pl.ds(k * BLOCK + i * TILE, TILE), cols] = gated
                     squares[i] = squares[i] + gated * gated
         for i in range(TILES):
             sq_ref[k, :, i * TILE : (i + 1) * TILE] = jnp.sum(squares[i].T, axis=0, keepdims=True)
 
 
 def norm_kernel(gated_ref, sq_ref, gain_hbm, out_hbm, out_buf, gain_buf, sems, gain_sem):
-    blocks = out_buf.shape[0]
-    gain = fetch(gain_hbm, gain_buf, gain_sem)
-    copy = lambda k: pltpu.make_async_copy(
-        out_buf.at[k], out_hbm.at[pl.ds(pl.multiple_of(k * BLOCK, BLOCK), BLOCK)], sems.at[k]
-    )
-    gain.wait()
-
-    @pl.loop(0, blocks)
-    def _(k):
-        factor = lax.rsqrt(sq_ref[k] * (1.0 / INNER) + 1e-05)
-        factor = jnp.broadcast_to(factor, (128, factor.shape[1])).T
-        rows = pl.ds(pl.multiple_of(k * BLOCK, BLOCK), BLOCK)
+    fetch(gain_hbm, gain_buf, gain_sem).wait()
+    chunk = out_buf.shape[1]
+    copies = []
+    for k in range(out_buf.shape[0]):
+        start = k * chunk % BLOCK
+        squares = sq_ref[k * chunk // BLOCK, :, start : start + chunk]
+        factor = lax.rsqrt(squares * (1.0 / INNER) + 1e-05)
+        factor = jnp.broadcast_to(factor, (128, chunk)).T
+        rows = pl.ds(k * chunk, chunk)
         for n in range(gated_ref.shape[1] // 128):
             cols = slice(n * 128, (n + 1) * 128)
             out_buf[k, :, cols] = (gated_ref[rows, cols] * factor * gain_buf[:, cols]).astype(BF16)
-        copy(k).start()
-
-    @pl.loop(0, blocks)
-    def _(k):
-        copy(k).wait()
+        copies.append(fetch(out_buf.at[k], out_hbm.at[rows], sems.at[k]))
+    for copy in copies:
+        copy.wait()
 
 
 def incoming(finals, beside):
@@ -510,9 +504,9 @@
         out_specs=ANY,
         out_shape=shape(length, channels, dtype=BF16),
         scratch_shapes=[
-            pltpu.VMEM((blocks, BLOCK, channels), BF16),
+            pltpu.VMEM((2 * blocks, BLOCK // 2, channels), BF16),
             pltpu.VMEM((1, channels), F32),
-            pltpu.SemaphoreType.DMA((blocks,)),
+            pltpu.SemaphoreType.DMA((2 * blocks,)),
             pltpu.SemaphoreType.DMA(()),
         ],
         compiler_params=pltpu.CompilerParams(vmem_limit_bytes=24 * 1024 * 1024),

time: 71.4 us -> 71.1 us (level)
  no operation moved by 1% of the time
where the time goes in v6:
time: 71.1 us; the launch traced here: 70.7 us
  Pallas kernels  47.2 us (66%)
  starting transfers between devices  14 us (20%)
  waiting for transfers between devices  6.76 us (10%)
  other arithmetic  1.62 us (2%)
  local copies, waits for them, and re-layouts  0.81 us (1%)
    pallas_call x5, Pallas kernels, piece(): pl.pallas_call(functools.partial(within_kernel, headdim, chunks, start, b...  27.1 us
    ppermute x7, starting transfers between devices, incoming(): send = lambda value, route: lax.ppermute(value, 'seq', route)  12.3 us
    pallas_call x1, Pallas kernels, shards(): pl.pallas_call(functools.partial(states_kernel, headdim, bool(done)), gri...  8.92 us
    pallas_call x1, Pallas kernels, shards(): pl.pallas_call(functools.partial(carried_kernel, headdim), in_specs=[ANY]...  8.24 us
    ppermute x7, waiting for transfers between devices, incoming(): send = lambda value, route: lax.ppermute(value, 'seq', route)  3.46 us
    ppermute x2, waiting for transfers between devices, shards(): lax.ppermute(squares, 'ch', [(i, i ^ step) for i in range(size)])  3.3 us
    pallas_call x1, Pallas kernels, shards(): pl.pallas_call(norm_kernel, in_specs=[WHOLE, WHOLE, ANY], out_specs=ANY,...  2.96 us
    ppermute x2, starting transfers between devices, shards(): lax.ppermute(squares, 'ch', [(i, i ^ step) for i in range(size)])  1.65 us
  transfers between devices with their start and end apart: 9, of which 4 were waited for; matrix products, arithmetic and copies ran while one was open for 2% of the time, Pallas kernels for 38%

profile of v6, /device:TPU:0, one launch (start us, length us, event | category | flops | bytes accessed | tf_op | source)
XLA Modules:
  0.0 70.7 jit_solution(13834451148257170707)
XLA Ops:
  0.0 8.9 %states.1 = (f32[8,8,2048]{2,1,0:T(8,128)}, f32[4,2,128,1024]{3,2,1,0:T(8,128)}, f32[4,8,1024]{2,1,0:T(8,128)}, f32[2,136,1024]{2,1,0:T(8,128)S(1)}) custom-call(bf16[2048,1024]{1,0:T(8,128)(2,1)} %x_ref.11, bf16[2048,128]{1,0:T(8,128)(2,1)} %b_ref.11, f32[16,2048]{1,0:T(8,128)} %lf_ref.1, f32[16,2048]{1,0:T(8,128)} %lr_ref.1), custom_call_target="tpu_custom_call" | custom-call | tf_op jit(solution)/shard_map/states/pallas_call | solution.py:392
  8.9 0.1 slice_select_fusion
  9.1 3.0 %collective-permute-start = (f32[136,512]{1,0:T(8,128)S(1)}, f32[136,512]{1,0:T(8,128)S(1)}, u32[]{:S(2)}, u32[]{:S(2)}) collective-permute-start(f32[136,512]{1,0:T(8,128)S(1)} %select_bitcast_fusion.dep_ref), channel_id=1, source_target_pairs={{0,4},{4,0},{8,12},{12,8},{16,20},{20,16},{24,28},{28,24},{1,5},{5... | collective-permute-start | bytes 835592 | tf_op jit(solution)/shard_map/ppermute | solution.py:293
  12.1 0.7 %broadcast_in_dim.11 = f32[16,64]{1,0:T(8,128)S(1)} broadcast(f32[16]{0:T(128)} %param.14), dimensions={0} | broadcast | bytes 4160 | tf_op jit(solution)/shard_map/broadcast_in_dim | solution.py:427
  12.8 0.1 broadcast_in_dim_reshape.3.skip_ref
  12.9 6.3 %within.5 = (f32[2048,1024]{1,0:T(8,128)}, f32[8,512]{1,0:T(8,128)S(1)}) custom-call(bf16[2048,1024]{1,0:T(8,128)(2,1)} %x_ref.11, bf16[2048,128]{1,0:T(8,128)(2,1)} %b_ref.11, bf16[2048,128]{1,0:T(8,128)(2,1)} %c_hbm.1, f32[8,8,2048]{2,1,0:T(8,128)} %get-tuple-element.20.cum_ref.cum_hbm, f32[1,1024]{1,0:T(1,128)S(1)} %broadcast_in_dim_reshape.3.skip_ref, ...), custom_call_target="tpu_custom_call" | custom-call | flops 4294967296 | bytes 3145728 | tf_op jit(solution)/shard_map/within/pallas_call | solution.py:442
  19.2 0.0 collective-permute-done
  19.2 0.2 fusion.11
  19.4 0.1 select_add_fusion.2.dep_ref
  19.6 3.5 %collective-permute-start.2 = (f32[128,512]{1,0:T(8,128)S(1)}, f32[128,512]{1,0:T(8,128)S(1)}, u32[]{:S(2)}, u32[]{:S(2)}) collective-permute-start(f32[128,512]{1,0:T(8,128)S(1)} %select_add_fusion.2.dep_ref), channel_id=1, source_target_pairs={{0,8},{4,12},{24,16},{28,20},{1,9},{5,13},{25,17},{29,21},{2,10},{... | collective-permute-start | bytes 786440 | tf_op jit(solution)/shard_map/ppermute | solution.py:293
  23.1 4.0 %within.6 = (f32[2048,1024]{1,0:T(8,128)}, f32[8,512]{1,0:T(8,128)S(1)}) custom-call(bf16[2048,1024]{1,0:T(8,128)(2,1)} %x_ref.11, bf16[2048,128]{1,0:T(8,128)(2,1)} %b_ref.11, bf16[2048,128]{1,0:T(8,128)(2,1)} %c_hbm.1, f32[8,8,2048]{2,1,0:T(8,128)} %get-tuple-element.20.cum_ref.cum_hbm, ...), custom_call_target="tpu_custom_call", output_to_operand_aliasing={{0}: (6, {})} | custom-call | flops 4294967296 | bytes 3145728 | tf_op jit(solution)/shard_map/within/pallas_call | solution.py:442
  27.1 1.3 %collective-permute-start.1 = (f32[136,512]{1,0:T(8,128)S(1)}, f32[136,512]{1,0:T(8,128)S(1)}, u32[]{:S(2)}, u32[]{:S(2)}) collective-permute-start(f32[136,512]{1,0:T(8,128)S(1)} %get-tuple-element.73), channel_id=1, source_target_pairs={{0,4},{4,0},{8,12},{12,8},{16,20},{20,16},{24,28},{28,24},{1,5},{5... | collective-permute-start | bytes 835592 | tf_op jit(solution)/shard_map/ppermute | solution.py:293
  28.4 0.0 collective-permute-done.2
  28.4 0.2 broadcast_select_fusion.3
  28.5 0.8 %collective-permute-start.5 = (f32[128,512]{1,0:T(8,128)S(1)}, f32[128,512]{1,0:T(8,128)S(1)}, u32[]{:S(2)}, u32[]{:S(2)}) collective-permute-start(f32[128,512]{1,0:T(8,128)S(1)} %get-tuple-element.35), channel_id=1, source_target_pairs={{0,4},{4,0},{8,12},{12,8},{16,20},{20,16},{24,28},{28,24},{1,5},{5... | collective-permute-start | bytes 786440 | tf_op jit(solution)/shard_map/ppermute | solution.py:293
  29.4 0.7 collective-permute-start.3
  30.0 4.1 %within.7 = (f32[2048,1024]{1,0:T(8,128)}, f32[8,512]{1,0:T(8,128)S(1)}) custom-call(bf16[2048,1024]{1,0:T(8,128)(2,1)} %x_ref.11, bf16[2048,128]{1,0:T(8,128)(2,1)} %b_ref.11, bf16[2048,128]{1,0:T(8,128)(2,1)} %c_hbm.1, f32[8,8,2048]{2,1,0:T(8,128)} %get-tuple-element.20.cum_ref.cum_hbm, ...), custom_call_target="tpu_custom_call", output_to_operand_aliasing={{0}: (6, {})} | custom-call | flops 4294967296 | bytes 3145728 | tf_op jit(solution)/shard_map/within/pallas_call | solution.py:442
  34.1 2.6 %collective-permute-done.1 = f32[136,512]{1,0:T(8,128)S(1)} collective-permute-done((f32[136,512]{1,0:T(8,128)S(1)}, f32[136,512]{1,0:T(8,128)S(1)}, u32[]{:S(2)}, u32[]{:S(2)}) %collective-permute-start.1) | collective-permute-done | bytes 278560 | tf_op jit(solution)/shard_map/ppermute | solution.py:293
  36.7 0.1 fusion.9
  36.8 0.0 collective-permute-done.3
  36.9 0.3 fusion.5
  37.2 1.5 %collective-permute-start.4 = (f32[128,512]{1,0:T(8,128)S(1)}, f32[128,512]{1,0:T(8,128)S(1)}, u32[]{:S(2)}, u32[]{:S(2)}) collective-permute-start(f32[128,512]{1,0:T(8,128)S(1)} %get-tuple-element.41.dep_ref), channel_id=1, source_target_pairs={{16,24},{20,28},{8,0},{12,4},{17,25},{21,29},{9,1},{13,5},{18,26},... | collective-permute-start | bytes 786440 | tf_op jit(solution)/shard_map/ppermute | solution.py:293
  38.7 6.3 %within.8 = (f32[2048,1024]{1,0:T(8,128)}, f32[8,512]{1,0:T(8,128)S(1)}) custom-call(bf16[2048,1024]{1,0:T(8,128)(2,1)} %x_ref.11, bf16[2048,128]{1,0:T(8,128)(2,1)} %b_ref.11, bf16[2048,128]{1,0:T(8,128)(2,1)} %c_hbm.1, f32[8,8,2048]{2,1,0:T(8,128)} %get-tuple-element.20.cum_ref.cum_hbm, ...), custom_call_target="tpu_custom_call", output_to_operand_aliasing={{0}: (6, {})} | custom-call | flops 4294967296 | bytes 3145728 | tf_op jit(solution)/shard_map/within/pallas_call | solution.py:442
  45.0 0.0 collective-permute-done.5
  45.0 0.1 select_bitcast_fusion.4
  45.1 0.9 %collective-permute-done.4 = f32[128,512]{1,0:T(8,128)S(1)} collective-permute-done((f32[128,512]{1,0:T(8,128)S(1)}, f32[128,512]{1,0:T(8,128)S(1)}, u32[]{:S(2)}, u32[]{:S(2)}) %collective-permute-start.4) | collective-permute-done | bytes 262176 | tf_op jit(solution)/shard_map/ppermute | solution.py:293
  45.9 0.2 select_add_fusion
  46.1 1.6 %collective-permute-start.6 = (f32[128,512]{1,0:T(8,128)S(1)}, f32[128,512]{1,0:T(8,128)S(1)}, u32[]{:S(2)}, u32[]{:S(2)}) collective-permute-start(f32[128,512]{1,0:T(8,128)S(1)} %get-tuple-element.38.dep_ref), channel_id=1, source_target_pairs={{0,4},{4,0},{8,12},{12,8},{16,20},{20,16},{24,28},{28,24},{1,5},{5... | collective-permute-start | bytes 786440 | tf_op jit(solution)/shard_map/ppermute | solution.py:293
  47.7 6.4 %within.9 = (f32[2048,1024]{1,0:T(8,128)}, f32[8,512]{1,0:T(8,128)}) custom-call(bf16[2048,1024]{1,0:T(8,128)(2,1)} %x_ref.11, bf16[2048,128]{1,0:T(8,128)(2,1)} %b_ref.11, bf16[2048,128]{1,0:T(8,128)(2,1)} %c_hbm.1, f32[8,8,2048]{2,1,0:T(8,128)} %get-tuple-element.20.cum_ref.cum_hbm, ...), custom_call_target="tpu_custom_call", output_to_operand_aliasing={{0}: (6, {})} | custom-call | flops 4294967296 | bytes 3145728 | tf_op jit(solution)/shard_map/within/pallas_call | solution.py:442
  54.1 0.0 collective-permute-done.6
  54.1 0.1 select_bitcast_fusion.2
  54.2 0.1 fusion.1
  54.3 0.1 pad_maximum_fusion.in_ref
  54.4 8.2 %carried.1 = (f32[2048,1024]{1,0:T(8,128)S(1)}, f32[4,1,512]{2,1,0:T(1,128)S(1)}) custom-call(f32[2048,1024]{1,0:T(8,128)} %get-tuple-element.30.a_hbm, bf16[2048,1024]{1,0:T(8,128)(2,1)} %gate_hbm.1, bf16[2048,128]{1,0:T(8,128)(2,1)} %c_hbm.1, f32[8,8,2048]{2,1,0:T(8,128)} %get-tuple-element.20.cum_ref.cum_hbm, ...), custom_call_target="tpu_custom_call" | custom-call | tf_op jit(solution)/shard_map/carried/pallas_call | solution.py:479
  62.6 0.1 collective-permute-start.7
  62.7 1.2 %collective-permute-done.7 = f32[4,1,512]{2,1,0:T(1,128)S(1)} collective-permute-done((f32[4,1,512]{2,1,0:T(1,128)S(1)}, f32[4,1,512]{2,1,0:T(1,128)S(1)}, u32[]{:S(2)}, u32[]{:S(2)}) %collective-permute-start.7) | collective-permute-done | bytes 8224 | tf_op jit(solution)/shard_map/ppermute | solution.py:499
  63.9 1.6 %collective-permute-start.8 = (f32[4,1,512]{2,1,0:T(1,128)S(1)}, f32[4,1,512]{2,1,0:T(1,128)S(1)}, u32[]{:S(2)}, u32[]{:S(2)}) collective-permute-start(f32[4,1,512]{2,1,0:T(1,128)S(1)} %add.150), channel_id=1, source_target_pairs={{0,2},{1,3},{2,0},{3,1},{4,6},{5,7},{6,4},{7,5},{8,10},{9,11},{10,... | collective-permute-start | bytes 24584 | tf_op jit(solution)/shard_map/ppermute | solution.py:499
  65.4 2.1 %collective-permute-done.8 = f32[4,1,512]{2,1,0:T(1,128)S(1)} collective-permute-done((f32[4,1,512]{2,1,0:T(1,128)S(1)}, f32[4,1,512]{2,1,0:T(1,128)S(1)}, u32[]{:S(2)}, u32[]{:S(2)}) %collective-permute-start.8) | collective-permute-done | bytes 8224 | tf_op jit(solution)/shard_map/ppermute | solution.py:499
  67.6 3.0 %norm.1 = bf16[2048,1024]{1,0:T(8,128)(2,1)} custom-call(f32[2048,1024]{1,0:T(8,128)S(1)} %get-tuple-element.33.gated_ref, f32[4,1,512]{2,1,0:T(1,128)S(1)} %add.151.sq_ref, f32[1,1024]{1,0:T(1,128)} %bitcast.71), custom_call_target="tpu_custom_call" | custom-call | tf_op jit(solution)/shard_map/norm/pallas_call | solution.py:501
  (12 shorter events, 0.1 us)
Async XLA Ops:
  9.1 10.1 %collective-permute-start = (f32[136,512]{1,0:T(8,128)S(1)}, f32[136,512]{1,0:T(8,128)S(1)}, u32[]{:S(2)}, u32[]{:S(2)}) collective-permute-start(f32[136,512]{1,0:T(8,128)S(1)} %select_bitcast_fusion.dep_ref), channel_id=1, source_target_pairs={{0,4},{4,0},{8,12},{12,8},{16,20},{20,16},{24,28},{28,24},{1,5},{5... | collective-permute-start | bytes 835592 | tf_op jit(solution)/shard_map/ppermute | solution.py:293
  19.6 8.8 %collective-permute-start.2 = (f32[128,512]{1,0:T(8,128)S(1)}, f32[128,512]{1,0:T(8,128)S(1)}, u32[]{:S(2)}, u32[]{:S(2)}) collective-permute-start(f32[128,512]{1,0:T(8,128)S(1)} %select_add_fusion.2.dep_ref), channel_id=1, source_target_pairs={{0,8},{4,12},{24,16},{28,20},{1,9},{5,13},{25,17},{29,21},{2,10},{... | collective-permute-start | bytes 786440 | tf_op jit(solution)/shard_map/ppermute | solution.py:293
  27.1 9.6 %collective-permute-start.1 = (f32[136,512]{1,0:T(8,128)S(1)}, f32[136,512]{1,0:T(8,128)S(1)}, u32[]{:S(2)}, u32[]{:S(2)}) collective-permute-start(f32[136,512]{1,0:T(8,128)S(1)} %get-tuple-element.73), channel_id=1, source_target_pairs={{0,4},{4,0},{8,12},{12,8},{16,20},{20,16},{24,28},{28,24},{1,5},{5... | collective-permute-start | bytes 835592 | tf_op jit(solution)/shard_map/ppermute | solution.py:293
  28.5 16.4 %collective-permute-start.5 = (f32[128,512]{1,0:T(8,128)S(1)}, f32[128,512]{1,0:T(8,128)S(1)}, u32[]{:S(2)}, u32[]{:S(2)}) collective-permute-start(f32[128,512]{1,0:T(8,128)S(1)} %get-tuple-element.35), channel_id=1, source_target_pairs={{0,4},{4,0},{8,12},{12,8},{16,20},{20,16},{24,28},{28,24},{1,5},{5... | collective-permute-start | bytes 786440 | tf_op jit(solution)/shard_map/ppermute | solution.py:293
  29.4 7.5 %collective-permute-start.3 = (f32[128,512]{1,0:T(8,128)S(1)}, f32[128,512]{1,0:T(8,128)S(1)}, u32[]{:S(2)}, u32[]{:S(2)}) collective-permute-start(f32[128,512]{1,0:T(8,128)S(1)} %get-tuple-element.62.dep_ref), channel_id=1, source_target_pairs={{8,16},{12,20},{16,8},{20,12},{9,17},{13,21},{17,9},{21,13},{10,18... | collective-permute-start | bytes 786440 | tf_op jit(solution)/shard_map/ppermute | solution.py:293
  37.2 8.7 %collective-permute-start.4 = (f32[128,512]{1,0:T(8,128)S(1)}, f32[128,512]{1,0:T(8,128)S(1)}, u32[]{:S(2)}, u32[]{:S(2)}) collective-permute-start(f32[128,512]{1,0:T(8,128)S(1)} %get-tuple-element.41.dep_ref), channel_id=1, source_target_pairs={{16,24},{20,28},{8,0},{12,4},{17,25},{21,29},{9,1},{13,5},{18,26},... | collective-permute-start | bytes 786440 | tf_op jit(solution)/shard_map/ppermute | solution.py:293
  46.1 8.0 %collective-permute-start.6 = (f32[128,512]{1,0:T(8,128)S(1)}, f32[128,512]{1,0:T(8,128)S(1)}, u32[]{:S(2)}, u32[]{:S(2)}) collective-permute-start(f32[128,512]{1,0:T(8,128)S(1)} %get-tuple-element.38.dep_ref), channel_id=1, source_target_pairs={{0,4},{4,0},{8,12},{12,8},{16,20},{20,16},{24,28},{28,24},{1,5},{5... | collective-permute-start | bytes 786440 | tf_op jit(solution)/shard_map/ppermute | solution.py:293
  62.6 1.2 %collective-permute-start.7 = (f32[4,1,512]{2,1,0:T(1,128)S(1)}, f32[4,1,512]{2,1,0:T(1,128)S(1)}, u32[]{:S(2)}, u32[]{:S(2)}) collective-permute-start(f32[4,1,512]{2,1,0:T(1,128)S(1)} %get-tuple-element.34), channel_id=1, source_target_pairs={{0,1},{1,0},{2,3},{3,2},{4,5},{5,4},{6,7},{7,6},{8,9},{9,8},{10,11... | collective-permute-start | bytes 24584 | tf_op jit(solution)/shard_map/ppermute | solution.py:499
  63.9 3.7 %collective-permute-start.8 = (f32[4,1,512]{2,1,0:T(1,128)S(1)}, f32[4,1,512]{2,1,0:T(1,128)S(1)}, u32[]{:S(2)}, u32[]{:S(2)}) collective-permute-start(f32[4,1,512]{2,1,0:T(1,128)S(1)} %add.150), channel_id=1, source_target_pairs={{0,2},{1,3},{2,0},{3,1},{4,6},{5,7},{6,4},{7,5},{8,10},{9,11},{10,... | collective-permute-start | bytes 24584 | tf_op jit(solution)/shard_map/ppermute | solution.py:499

commit v7 on v5

--- a/solution.py
+++ b/solution.py
@@ -202,21 +202,31 @@
     blocks, pairs = a_buf.shape[0], cum_buf.shape[1]
     width = 2 * headdim
 
-    def copies(k):
-        at = pl.ds(pl.multiple_of(k * BLOCK, BLOCK), BLOCK)
-        pieces = [
-            (before_hbm.at[k], before_buf.at[k]),
-            (off_hbm.at[k], off_buf.at[k]),
-            (c_hbm.at[at], c_buf.at[k]),
-            (cum_hbm.at[:, :, at], cum_buf.at[k]),
-            (gate_hbm.at[at], gate_buf.at[k]),
-            (a_hbm.at[at], a_buf.at[k]),
-        ]
-        return [pltpu.make_async_copy(f, t, sems.at[n, k]) for n, (f, t) in enumerate(pieces)]
+    half_lanes = pairs * width // 2
+
+    def copies(k, side):
+        at = pl.ds(k * BLOCK, BLOCK)
+        if side is None:
+            pieces = [
+                (off_hbm.at[k], off_buf.at[k]),
+                (c_hbm.at[at], c_buf.at[k]),
+                (cum_hbm.at[:, :, at], cum_buf.at[k]),
+            ]
+            sem = 0
+        else:
+            cols = pl.ds(side * half_lanes, half_lanes)
+            pieces = [
+                (before_hbm.at[k, :, :, cols], before_buf.at[k, :, :, cols]),
+                (gate_hbm.at[at, cols], gate_buf.at[k, :, cols]),
+                (a_hbm.at[at, cols], a_buf.at[k, :, cols]),
+            ]
+            sem = 3 + 3 * side
+        return [pltpu.make_async_copy(f, t, sems.at[sem + n, k]) for n, (f, t) in enumerate(pieces)]
 
     for k in range(blocks):
-        for copy in copies(k):
-            copy.start()
+        for side in (None, 0, 1):
+            for copy in copies(k, side):
+                copy.start()
     row = lax.broadcasted_iota(jnp.int32, (16 * pairs, 1), 0)
     row = jnp.where(row < 8 * pairs, row, row - 8 * pairs)
     lane = lax.broadcasted_iota(jnp.int32, (1, width), 1)
@@ -224,9 +234,8 @@
         hot = jnp.where(row == 8 * p + 2 + jnp.where(lane < headdim, 0, 1), 1.0, 0.0)
         hot_ref[:, p * width : (p + 1) * width] = hot.astype(BF16)
 
-    @pl.loop(0, blocks)
-    def _(k):
-        for copy in copies(k):
+    for k in range(blocks):
+        for copy in copies(k, None):
             copy.wait()
         every = jnp.exp2(cum_buf[k].reshape(8 * pairs, BLOCK))
         high = every.astype(BF16).astype(F32)
@@ -236,6 +245,9 @@
         squares = [jnp.zeros((TILE, width), F32)] * TILES
         scales = [None, None]
         for p in range(pairs):
+            if 2 * p % pairs == 0:
+                for copy in copies(k, 2 * p // pairs):
+                    copy.wait()
             cols = slice(p * width, (p + 1) * width)
             decay = every[8 * p : 8 * p + 8]
             held = [
@@ -262,7 +274,7 @@
                     total = total + other * z[to, width:]
                     half = 0.5 * gate_buf[k, at, cols].astype(F32)
                     gated = total * (half + half * jnp.tanh(half))
-                    out_ref[pl.ds(pl.multiple_of(k * BLOCK + i * TILE, TILE), TILE), cols] = gated
+                    out_ref[pl.ds(k * BLOCK + i * TILE, TILE), cols] = gated
                     squares[i] = squares[i] + gated * gated
         for i in range(TILES):
             sq_ref[k, :, i * TILE : (i + 1) * TILE] = jnp.sum(squares[i].T, axis=0, keepdims=True)
@@ -495,7 +507,7 @@
             pltpu.VMEM((blocks, 2, state, channels), F32),
             pltpu.VMEM((blocks, 8, channels), F32),
             pltpu.VMEM((16 * pairs, channels), BF16),
-            pltpu.SemaphoreType.DMA((6, blocks)),
+            pltpu.SemaphoreType.DMA((9, blocks)),
         ],
         compiler_params=pltpu.CompilerParams(vmem_limit_bytes=40 * 1024 * 1024),
         name="carried",

time: 71.4 us -> 71.3 us (level)
  no operation moved by 1% of the time
where the time goes in v7:
time: 71.3 us; the launch traced here: 70.9 us
  Pallas kernels  47.3 us (66%)
  starting transfers between devices  14 us (20%)
  waiting for transfers between devices  6.76 us (9%)
  other arithmetic  1.62 us (2%)
  local copies, waits for them, and re-layouts  0.81 us (1%)
    pallas_call x5, Pallas kernels, piece(): pl.pallas_call(functools.partial(within_kernel, headdim, chunks, start, b...  27.1 us
    ppermute x7, starting transfers between devices, incoming(): send = lambda value, route: lax.ppermute(value, 'seq', route)  12.3 us
    pallas_call x1, Pallas kernels, shards(): pl.pallas_call(functools.partial(states_kernel, headdim, bool(done)), gri...  8.92 us
    pallas_call x1, Pallas kernels, shards(): pl.pallas_call(functools.partial(carried_kernel, headdim), in_specs=[ANY]...  8.29 us
    ppermute x7, waiting for transfers between devices, incoming(): send = lambda value, route: lax.ppermute(value, 'seq', route)  3.46 us
    ppermute x2, waiting for transfers between devices, shards(): lax.ppermute(squares, 'ch', [(i, i ^ step) for i in range(size)])  3.3 us
    pallas_call x1, Pallas kernels, shards(): pl.pallas_call(norm_kernel, in_specs=[WHOLE, WHOLE, ANY], out_specs=ANY,...  3.05 us
    ppermute x2, starting transfers between devices, shards(): lax.ppermute(squares, 'ch', [(i, i ^ step) for i in range(size)])  1.65 us
  transfers between devices with their start and end apart: 9, of which 4 were waited for; matrix products, arithmetic and copies ran while one was open for 2% of the time, Pallas kernels for 38%

profile of v7, /device:TPU:0, one launch (start us, length us, event | category | flops | bytes accessed | tf_op | source)
XLA Modules:
  0.0 70.9 jit_solution(1897290142267805855)
XLA Ops:
  0.0 8.9 %states.1 = (f32[8,8,2048]{2,1,0:T(8,128)}, f32[4,2,128,1024]{3,2,1,0:T(8,128)}, f32[4,8,1024]{2,1,0:T(8,128)}, f32[2,136,1024]{2,1,0:T(8,128)S(1)}) custom-call(bf16[2048,1024]{1,0:T(8,128)(2,1)} %x_ref.11, bf16[2048,128]{1,0:T(8,128)(2,1)} %b_ref.11, f32[16,2048]{1,0:T(8,128)} %lf_ref.1, f32[16,2048]{1,0:T(8,128)} %lr_ref.1), custom_call_target="tpu_custom_call" | custom-call | tf_op jit(solution)/shard_map/states/pallas_call | solution.py:410
  8.9 0.1 slice_select_fusion
  9.1 3.0 %collective-permute-start = (f32[136,512]{1,0:T(8,128)S(1)}, f32[136,512]{1,0:T(8,128)S(1)}, u32[]{:S(2)}, u32[]{:S(2)}) collective-permute-start(f32[136,512]{1,0:T(8,128)S(1)} %select_bitcast_fusion.dep_ref), channel_id=1, source_target_pairs={{0,4},{4,0},{8,12},{12,8},{16,20},{20,16},{24,28},{28,24},{1,5},{5... | collective-permute-start | bytes 835592 | tf_op jit(solution)/shard_map/ppermute | solution.py:311
  12.1 0.7 %broadcast_in_dim.11 = f32[16,64]{1,0:T(8,128)S(1)} broadcast(f32[16]{0:T(128)} %param.14), dimensions={0} | broadcast | bytes 4160 | tf_op jit(solution)/shard_map/broadcast_in_dim | solution.py:445
  12.8 0.1 broadcast_in_dim_reshape.3.skip_ref
  12.9 6.3 %within.5 = (f32[2048,1024]{1,0:T(8,128)}, f32[8,512]{1,0:T(8,128)S(1)}) custom-call(bf16[2048,1024]{1,0:T(8,128)(2,1)} %x_ref.11, bf16[2048,128]{1,0:T(8,128)(2,1)} %b_ref.11, bf16[2048,128]{1,0:T(8,128)(2,1)} %c_hbm.1, f32[8,8,2048]{2,1,0:T(8,128)} %get-tuple-element.20.cum_ref.cum_hbm, f32[1,1024]{1,0:T(1,128)S(1)} %broadcast_in_dim_reshape.3.skip_ref, ...), custom_call_target="tpu_custom_call" | custom-call | flops 4294967296 | bytes 3145728 | tf_op jit(solution)/shard_map/within/pallas_call | solution.py:460
  19.2 0.0 collective-permute-done
  19.2 0.2 fusion.11
  19.4 0.1 select_add_fusion.2.dep_ref
  19.6 3.5 %collective-permute-start.2 = (f32[128,512]{1,0:T(8,128)S(1)}, f32[128,512]{1,0:T(8,128)S(1)}, u32[]{:S(2)}, u32[]{:S(2)}) collective-permute-start(f32[128,512]{1,0:T(8,128)S(1)} %select_add_fusion.2.dep_ref), channel_id=1, source_target_pairs={{0,8},{4,12},{24,16},{28,20},{1,9},{5,13},{25,17},{29,21},{2,10},{... | collective-permute-start | bytes 786440 | tf_op jit(solution)/shard_map/ppermute | solution.py:311
  23.1 4.0 %within.6 = (f32[2048,1024]{1,0:T(8,128)}, f32[8,512]{1,0:T(8,128)S(1)}) custom-call(bf16[2048,1024]{1,0:T(8,128)(2,1)} %x_ref.11, bf16[2048,128]{1,0:T(8,128)(2,1)} %b_ref.11, bf16[2048,128]{1,0:T(8,128)(2,1)} %c_hbm.1, f32[8,8,2048]{2,1,0:T(8,128)} %get-tuple-element.20.cum_ref.cum_hbm, ...), custom_call_target="tpu_custom_call", output_to_operand_aliasing={{0}: (6, {})} | custom-call | flops 4294967296 | bytes 3145728 | tf_op jit(solution)/shard_map/within/pallas_call | solution.py:460
  27.1 1.3 %collective-permute-start.1 = (f32[136,512]{1,0:T(8,128)S(1)}, f32[136,512]{1,0:T(8,128)S(1)}, u32[]{:S(2)}, u32[]{:S(2)}) collective-permute-start(f32[136,512]{1,0:T(8,128)S(1)} %get-tuple-element.73), channel_id=1, source_target_pairs={{0,4},{4,0},{8,12},{12,8},{16,20},{20,16},{24,28},{28,24},{1,5},{5... | collective-permute-start | bytes 835592 | tf_op jit(solution)/shard_map/ppermute | solution.py:311
  28.4 0.0 collective-permute-done.2
  28.4 0.2 broadcast_select_fusion.3
  28.5 0.8 %collective-permute-start.5 = (f32[128,512]{1,0:T(8,128)S(1)}, f32[128,512]{1,0:T(8,128)S(1)}, u32[]{:S(2)}, u32[]{:S(2)}) collective-permute-start(f32[128,512]{1,0:T(8,128)S(1)} %get-tuple-element.35), channel_id=1, source_target_pairs={{0,4},{4,0},{8,12},{12,8},{16,20},{20,16},{24,28},{28,24},{1,5},{5... | collective-permute-start | bytes 786440 | tf_op jit(solution)/shard_map/ppermute | solution.py:311
  29.4 0.7 collective-permute-start.3
  30.0 4.1 %within.7 = (f32[2048,1024]{1,0:T(8,128)}, f32[8,512]{1,0:T(8,128)S(1)}) custom-call(bf16[2048,1024]{1,0:T(8,128)(2,1)} %x_ref.11, bf16[2048,128]{1,0:T(8,128)(2,1)} %b_ref.11, bf16[2048,128]{1,0:T(8,128)(2,1)} %c_hbm.1, f32[8,8,2048]{2,1,0:T(8,128)} %get-tuple-element.20.cum_ref.cum_hbm, ...), custom_call_target="tpu_custom_call", output_to_operand_aliasing={{0}: (6, {})} | custom-call | flops 4294967296 | bytes 3145728 | tf_op jit(solution)/shard_map/within/pallas_call | solution.py:460
  34.1 2.6 %collective-permute-done.1 = f32[136,512]{1,0:T(8,128)S(1)} collective-permute-done((f32[136,512]{1,0:T(8,128)S(1)}, f32[136,512]{1,0:T(8,128)S(1)}, u32[]{:S(2)}, u32[]{:S(2)}) %collective-permute-start.1) | collective-permute-done | bytes 278560 | tf_op jit(solution)/shard_map/ppermute | solution.py:311
  36.7 0.1 fusion.9
  36.8 0.0 collective-permute-done.3
  36.9 0.3 fusion.5
  37.2 1.5 %collective-permute-start.4 = (f32[128,512]{1,0:T(8,128)S(1)}, f32[128,512]{1,0:T(8,128)S(1)}, u32[]{:S(2)}, u32[]{:S(2)}) collective-permute-start(f32[128,512]{1,0:T(8,128)S(1)} %get-tuple-element.41.dep_ref), channel_id=1, source_target_pairs={{16,24},{20,28},{8,0},{12,4},{17,25},{21,29},{9,1},{13,5},{18,26},... | collective-permute-start | bytes 786440 | tf_op jit(solution)/shard_map/ppermute | solution.py:311
  38.7 6.3 %within.8 = (f32[2048,1024]{1,0:T(8,128)}, f32[8,512]{1,0:T(8,128)S(1)}) custom-call(bf16[2048,1024]{1,0:T(8,128)(2,1)} %x_ref.11, bf16[2048,128]{1,0:T(8,128)(2,1)} %b_ref.11, bf16[2048,128]{1,0:T(8,128)(2,1)} %c_hbm.1, f32[8,8,2048]{2,1,0:T(8,128)} %get-tuple-element.20.cum_ref.cum_hbm, ...), custom_call_target="tpu_custom_call", output_to_operand_aliasing={{0}: (6, {})} | custom-call | flops 4294967296 | bytes 3145728 | tf_op jit(solution)/shard_map/within/pallas_call | solution.py:460
  45.0 0.0 collective-permute-done.5
  45.0 0.1 select_bitcast_fusion.4
  45.1 0.9 %collective-permute-done.4 = f32[128,512]{1,0:T(8,128)S(1)} collective-permute-done((f32[128,512]{1,0:T(8,128)S(1)}, f32[128,512]{1,0:T(8,128)S(1)}, u32[]{:S(2)}, u32[]{:S(2)}) %collective-permute-start.4) | collective-permute-done | bytes 262176 | tf_op jit(solution)/shard_map/ppermute | solution.py:311
  45.9 0.2 select_add_fusion
  46.1 1.6 %collective-permute-start.6 = (f32[128,512]{1,0:T(8,128)S(1)}, f32[128,512]{1,0:T(8,128)S(1)}, u32[]{:S(2)}, u32[]{:S(2)}) collective-permute-start(f32[128,512]{1,0:T(8,128)S(1)} %get-tuple-element.38.dep_ref), channel_id=1, source_target_pairs={{0,4},{4,0},{8,12},{12,8},{16,20},{20,16},{24,28},{28,24},{1,5},{5... | collective-permute-start | bytes 786440 | tf_op jit(solution)/shard_map/ppermute | solution.py:311
  47.7 6.4 %within.9 = (f32[2048,1024]{1,0:T(8,128)}, f32[8,512]{1,0:T(8,128)}) custom-call(bf16[2048,1024]{1,0:T(8,128)(2,1)} %x_ref.11, bf16[2048,128]{1,0:T(8,128)(2,1)} %b_ref.11, bf16[2048,128]{1,0:T(8,128)(2,1)} %c_hbm.1, f32[8,8,2048]{2,1,0:T(8,128)} %get-tuple-element.20.cum_ref.cum_hbm, ...), custom_call_target="tpu_custom_call", output_to_operand_aliasing={{0}: (6, {})} | custom-call | flops 4294967296 | bytes 3145728 | tf_op jit(solution)/shard_map/within/pallas_call | solution.py:460
  54.1 0.0 collective-permute-done.6
  54.1 0.1 select_bitcast_fusion.2
  54.2 0.1 fusion.1
  54.3 0.1 pad_maximum_fusion.in_ref
  54.4 8.3 %carried.1 = (f32[2048,1024]{1,0:T(8,128)S(1)}, f32[4,1,512]{2,1,0:T(1,128)S(1)}) custom-call(f32[2048,1024]{1,0:T(8,128)} %get-tuple-element.30.a_hbm, bf16[2048,1024]{1,0:T(8,128)(2,1)} %gate_hbm.1, bf16[2048,128]{1,0:T(8,128)(2,1)} %c_hbm.1, f32[8,8,2048]{2,1,0:T(8,128)} %get-tuple-element.20.cum_ref.cum_hbm, ...), custom_call_target="tpu_custom_call" | custom-call | tf_op jit(solution)/shard_map/carried/pallas_call | solution.py:497
  62.7 0.1 collective-permute-start.7
  62.7 1.2 %collective-permute-done.7 = f32[4,1,512]{2,1,0:T(1,128)S(1)} collective-permute-done((f32[4,1,512]{2,1,0:T(1,128)S(1)}, f32[4,1,512]{2,1,0:T(1,128)S(1)}, u32[]{:S(2)}, u32[]{:S(2)}) %collective-permute-start.7) | collective-permute-done | bytes 8224 | tf_op jit(solution)/shard_map/ppermute | solution.py:517
  63.9 1.6 %collective-permute-start.8 = (f32[4,1,512]{2,1,0:T(1,128)S(1)}, f32[4,1,512]{2,1,0:T(1,128)S(1)}, u32[]{:S(2)}, u32[]{:S(2)}) collective-permute-start(f32[4,1,512]{2,1,0:T(1,128)S(1)} %add.150), channel_id=1, source_target_pairs={{0,2},{1,3},{2,0},{3,1},{4,6},{5,7},{6,4},{7,5},{8,10},{9,11},{10,... | collective-permute-start | bytes 24584 | tf_op jit(solution)/shard_map/ppermute | solution.py:517
  65.5 2.1 %collective-permute-done.8 = f32[4,1,512]{2,1,0:T(1,128)S(1)} collective-permute-done((f32[4,1,512]{2,1,0:T(1,128)S(1)}, f32[4,1,512]{2,1,0:T(1,128)S(1)}, u32[]{:S(2)}, u32[]{:S(2)}) %collective-permute-start.8) | collective-permute-done | bytes 8224 | tf_op jit(solution)/shard_map/ppermute | solution.py:517
  67.6 3.1 %norm.1 = bf16[2048,1024]{1,0:T(8,128)(2,1)} custom-call(f32[2048,1024]{1,0:T(8,128)S(1)} %get-tuple-element.33.gated_ref, f32[4,1,512]{2,1,0:T(1,128)S(1)} %add.151.sq_ref, f32[1,1024]{1,0:T(1,128)} %bitcast.71), custom_call_target="tpu_custom_call" | custom-call | tf_op jit(solution)/shard_map/norm/pallas_call | solution.py:519
  (12 shorter events, 0.1 us)
Async XLA Ops:
  9.1 10.1 %collective-permute-start = (f32[136,512]{1,0:T(8,128)S(1)}, f32[136,512]{1,0:T(8,128)S(1)}, u32[]{:S(2)}, u32[]{:S(2)}) collective-permute-start(f32[136,512]{1,0:T(8,128)S(1)} %select_bitcast_fusion.dep_ref), channel_id=1, source_target_pairs={{0,4},{4,0},{8,12},{12,8},{16,20},{20,16},{24,28},{28,24},{1,5},{5... | collective-permute-start | bytes 835592 | tf_op jit(solution)/shard_map/ppermute | solution.py:311
  19.6 8.8 %collective-permute-start.2 = (f32[128,512]{1,0:T(8,128)S(1)}, f32[128,512]{1,0:T(8,128)S(1)}, u32[]{:S(2)}, u32[]{:S(2)}) collective-permute-start(f32[128,512]{1,0:T(8,128)S(1)} %select_add_fusion.2.dep_ref), channel_id=1, source_target_pairs={{0,8},{4,12},{24,16},{28,20},{1,9},{5,13},{25,17},{29,21},{2,10},{... | collective-permute-start | bytes 786440 | tf_op jit(solution)/shard_map/ppermute | solution.py:311
  27.1 9.6 %collective-permute-start.1 = (f32[136,512]{1,0:T(8,128)S(1)}, f32[136,512]{1,0:T(8,128)S(1)}, u32[]{:S(2)}, u32[]{:S(2)}) collective-permute-start(f32[136,512]{1,0:T(8,128)S(1)} %get-tuple-element.73), channel_id=1, source_target_pairs={{0,4},{4,0},{8,12},{12,8},{16,20},{20,16},{24,28},{28,24},{1,5},{5... | collective-permute-start | bytes 835592 | tf_op jit(solution)/shard_map/ppermute | solution.py:311
  28.5 16.4 %collective-permute-start.5 = (f32[128,512]{1,0:T(8,128)S(1)}, f32[128,512]{1,0:T(8,128)S(1)}, u32[]{:S(2)}, u32[]{:S(2)}) collective-permute-start(f32[128,512]{1,0:T(8,128)S(1)} %get-tuple-element.35), channel_id=1, source_target_pairs={{0,4},{4,0},{8,12},{12,8},{16,20},{20,16},{24,28},{28,24},{1,5},{5... | collective-permute-start | bytes 786440 | tf_op jit(solution)/shard_map/ppermute | solution.py:311
  29.4 7.5 %collective-permute-start.3 = (f32[128,512]{1,0:T(8,128)S(1)}, f32[128,512]{1,0:T(8,128)S(1)}, u32[]{:S(2)}, u32[]{:S(2)}) collective-permute-start(f32[128,512]{1,0:T(8,128)S(1)} %get-tuple-element.62.dep_ref), channel_id=1, source_target_pairs={{8,16},{12,20},{16,8},{20,12},{9,17},{13,21},{17,9},{21,13},{10,18... | collective-permute-start | bytes 786440 | tf_op jit(solution)/shard_map/ppermute | solution.py:311
  37.2 8.7 %collective-permute-start.4 = (f32[128,512]{1,0:T(8,128)S(1)}, f32[128,512]{1,0:T(8,128)S(1)}, u32[]{:S(2)}, u32[]{:S(2)}) collective-permute-start(f32[128,512]{1,0:T(8,128)S(1)} %get-tuple-element.41.dep_ref), channel_id=1, source_target_pairs={{16,24},{20,28},{8,0},{12,4},{17,25},{21,29},{9,1},{13,5},{18,26},... | collective-permute-start | bytes 786440 | tf_op jit(solution)/shard_map/ppermute | solution.py:311
  46.1 8.0 %collective-permute-start.6 = (f32[128,512]{1,0:T(8,128)S(1)}, f32[128,512]{1,0:T(8,128)S(1)}, u32[]{:S(2)}, u32[]{:S(2)}) collective-permute-start(f32[128,512]{1,0:T(8,128)S(1)} %get-tuple-element.38.dep_ref), channel_id=1, source_target_pairs={{0,4},{4,0},{8,12},{12,8},{16,20},{20,16},{24,28},{28,24},{1,5},{5... | collective-permute-start | bytes 786440 | tf_op jit(solution)/shard_map/ppermute | solution.py:311
  62.7 1.2 %collective-permute-start.7 = (f32[4,1,512]{2,1,0:T(1,128)S(1)}, f32[4,1,512]{2,1,0:T(1,128)S(1)}, u32[]{:S(2)}, u32[]{:S(2)}) collective-permute-start(f32[4,1,512]{2,1,0:T(1,128)S(1)} %get-tuple-element.34), channel_id=1, source_target_pairs={{0,1},{1,0},{2,3},{3,2},{4,5},{5,4},{6,7},{7,6},{8,9},{9,8},{10,11... | collective-permute-start | bytes 24584 | tf_op jit(solution)/shard_map/ppermute | solution.py:517
  63.9 3.7 %collective-permute-start.8 = (f32[4,1,512]{2,1,0:T(1,128)S(1)}, f32[4,1,512]{2,1,0:T(1,128)S(1)}, u32[]{:S(2)}, u32[]{:S(2)}) collective-permute-start(f32[4,1,512]{2,1,0:T(1,128)S(1)} %add.150), channel_id=1, source_target_pairs={{0,2},{1,3},{2,0},{3,1},{4,6},{5,7},{6,4},{7,5},{8,10},{9,11},{10,... | collective-permute-start | bytes 24584 | tf_op jit(solution)/shard_map/ppermute | solution.py:517
